TPU v7x, 128 devices: a whole 4x4x4 slice. The times are simulated.
128 devices in a mesh: dp: 8 (over z, core), mp: 16 (over x, y).
Axes of the slice: x: 4, y: 4, z: 4, core: 2. Of those that a mesh axis runs over, the one named last changes fastest.
Arguments:
- gradient: bfloat16 [8, 8192, 8192], P('dp', 'mp'), may hold values from -6 to 6
- error: bfloat16 [8, 8192, 8192], P('dp', 'mp'), may hold values from -4 to 4
- query: bfloat16 [8192, 256], P('mp'), may hold values from -0.0625 to 0.0625
Outputs:
- factor: float32 [8192, 256], P('mp')
- new_error: bfloat16 [8, 8192, 8192], P('dp', 'mp')
All inputs are finite; a program needn't handle non-finite values.
Results may differ from a plain program's by a relative error of at most 0.013.
Values may be sent and summed in bfloat16 or wider, within the bound.
No kernel may reach another device: no remote copies, remote signals or barrier semaphores. Data moves between devices by JAX's collectives and lax.ppermute only.
A program may use at most 128 MiB of HBM per device.

v0:
```python
import jax
import jax.numpy as jnp
from jax import lax
from jax.sharding import PartitionSpec as P


def orthonormal(rows_proj, gram):
    lower = jnp.linalg.cholesky(gram)
    return lax.linalg.triangular_solve(
        lower, rows_proj, left_side=False, lower=True, transpose_a=True
    ).astype(jnp.bfloat16)


def gram_of(rows_proj):
    return jnp.dot(rows_proj.T, rows_proj, precision=lax.Precision.HIGHEST)


def shards(gradient, error, query):
    adjusted = (gradient[0].astype(jnp.float32) + error[0].astype(jnp.float32)).astype(jnp.bfloat16)
    cols_dev = query.shape[0]
    replicas = lax.axis_size("dp")
    projection = jnp.dot(
        adjusted,
        lax.all_gather(query, "mp", axis=0, tiled=True),
        preferred_element_type=jnp.float32,
    )
    summed = lax.psum(projection, "dp")
    gram = lax.psum(gram_of(summed).astype(jnp.bfloat16), "mp").astype(jnp.float32)
    basis = orthonormal(summed, gram)
    contract = (((0,), (0,)), ((), ()))
    term = lax.dot_general(adjusted, basis, contract, preferred_element_type=jnp.float32)
    factor_full = lax.psum(term, ("dp", "mp")) / replicas
    factor_half = factor_full.astype(jnp.bfloat16)
    own = lax.dynamic_slice_in_dim(factor_full, lax.axis_index("mp") * cols_dev, cols_dev, 0)
    approx = lax.dot_general(
        basis, factor_half, (((1,), (1,)), ((), ())), preferred_element_type=jnp.float32
    )
    new_error = (adjusted.astype(jnp.float32) - approx).astype(jnp.bfloat16)
    return (own, new_error[None])


def solution(mesh):
    in_specs = (P("dp", "mp", None), P("dp", "mp", None), P("mp", None))
    out_specs = (P("mp", None), P("dp", "mp", None))
    return jax.shard_map(shards, mesh=mesh, in_specs=in_specs, out_specs=out_specs, check_vma=False)
```

profile of v0, /device:TPU:1, one launch (start us, length us, event | category | flops | bytes accessed | tf_op | source)
XLA Modules:
  0.0 484.4 jit_solution(14559030289876648018)
XLA Ops:
  7.2 0.0 all-gather.2.cloned.1.call-start
  7.2 0.7 all-gather.2.cloned.1.call-update
  7.9 0.0 all-reduce.5.cloned.1.call-start
  7.9 56.8 %all-gather.2.cloned.1.call-done = bf16[8192,256]{1,0:T(8,128)(2,1)} async-done(((bf16[512,256]{1,0:T(8,128)(2,1)}), bf16[8192,256]{1,0:T(8,128)(2,1)}) %all-gather.2.cloned.1.call-update) | async-done | bytes 4194320 | tf_op jit(solution)/shard_map/all_gather | solution.py:24
  64.8 10.1 %fusion.14 = f32[512,256]{1,0:T(8,128)} fusion(bf16[8192,256]{1,0:T(8,128)(2,1)} %all-gather.2.cloned.1.call-done, bf16[1,512,8192]{2,1,0:T(8,128)(2,1)} %param.4, bf16[1,512,8192]{2,1,0:T(8,128)(2,1)} %param.3), kind=kOutput, calls=%fused_computation.39 | convolution fusion | flops 2164260864 | bytes 21495808 | tf_op jit(solution)/shard_map/dot_general | solution.py:22
  74.9 0.0 all-reduce.5.cloned.1.call-update
  74.9 0.0 all-reduce.7.cloned.1.call-start
  75.0 58.7 %all-reduce.5.cloned.1.call-done = f32[512,256]{1,0:T(8,128)} async-done(((f32[512,256]{1,0:T(8,128)}), f32[512,256]{1,0:T(8,128)}) %all-reduce.5.cloned.1.call-update) | async-done | bytes 524304 | tf_op jit(solution)/shard_map/psum | solution.py:27
  133.7 2.9 convolution_convert_fusion
  136.5 0.0 all-reduce.7.cloned.1.call-update
  136.5 0.2 all-reduce.9.cloned.1.call-start
  136.8 82.5 %all-reduce.7.cloned.1.call-done = bf16[256,256]{0,1:T(8,128)(2,1)} async-done(((bf16[256,256]{0,1:T(8,128)(2,1)}), bf16[256,256]{0,1:T(8,128)(2,1)}) %all-reduce.7.cloned.1.call-update) | async-done | bytes 131088 | tf_op jit(solution)/shard_map/psum | solution.py:28
  219.3 1.0 copy.6
  220.3 0.9 fusion.5
  221.3 11.7 %cholesky.50 = f32[128,128]{1,0:T(8,128)S(1)} custom-call(f32[128,128]{1,0:T(8,128)S(1)} %cholesky.118), custom_call_target="Cholesky" | custom-call | tf_op jit(solution)/shard_map/jit(cholesky)/cholesky | solution.py:8
  233.0 9.8 %custom-call.14 = f32[1,128,128]{1,2,0:T(8,128)S(1)} custom-call(f32[1,128,128]{2,1,0:T(8,128)S(1)} %get-tuple-element.23), custom_call_target="InvertDiagBlocksLowerTriangular" | custom-call | tf_op jit(solution)/shard_map/jit(cholesky)/cholesky | solution.py:8
  242.9 0.2 constant_dynamic-update-slice_fusion
  243.1 0.3 convolution_subtract_fusion.1
  243.3 11.7 %cholesky.105 = f32[128,128]{1,0:T(8,128)S(1)} custom-call(f32[128,128]{1,0:T(8,128)S(1)} %convolution_subtract_fusion.1), custom_call_target="Cholesky" | custom-call | tf_op jit(solution)/shard_map/jit(cholesky)/cholesky | solution.py:8
  255.1 0.7 compare_reduce_fusion
  257.2 0.1 triangular_solve.58
  257.3 4.3 while.1
  257.5 0.6 fusion.26
  258.1 1.4 bitcast_dynamic-update-slice_fusion.2
  259.5 0.6 fusion.26
  260.1 1.4 bitcast_dynamic-update-slice_fusion.2
  261.6 19.7 %custom-call.15 = f32[2,128,128]{1,2,0:T(8,128)S(1)} custom-call(f32[2,128,128]{2,1,0:T(8,128)S(1)} %get-tuple-element.9), custom_call_target="InvertDiagBlocksLowerTriangular" | custom-call | tf_op jit(solution)/shard_map/triangular_solve | solution.py:9
  281.2 1.4 fusion.17
  282.6 1.5 convolution_subtract_fusion
  284.2 0.4 convolution_convert_fusion.1
  284.6 13.2 %fusion.6 = f32[8192,256]{1,0:T(8,128)} fusion(bf16[512,128]{0,1:T(8,128)(2,1)S(1)} %convolution_convert_fusion.1, bf16[512,128]{0,1:T(8,128)(2,1)S(1)} %get-tuple-element.26, bf16[1,512,8192]{2,1,0:T(8,128)(2,1)} %param.4, bf16[1,512,8192]{2,1,0:T(8,128)(2,1)} %param.3), kind=kOutput, calls=%fused_computation.19 | convolution fusion | flops 2164785152 | bytes 25427968 | tf_op jit(solution)/shard_map/dot_general | solution.py:31
  297.8 0.0 all-reduce.9.cloned.1.call-update
  297.8 162.8 %all-reduce.9.cloned.1.call-done = f32[8192,256]{1,0:T(8,128)} async-done(((f32[8192,256]{1,0:T(8,128)}), f32[8192,256]{1,0:T(8,128)}) %all-reduce.9.cloned.1.call-update) | async-done | bytes 8388624 | tf_op jit(solution)/shard_map/psum | solution.py:32
  460.6 3.9 broadcast_multiply_fusion
  464.6 0.8 constant_dynamic-slice_fusion.1
  465.4 12.5 %fusion = bf16[1,512,8192]{2,1,0:T(8,128)(2,1)} fusion(bf16[512,128]{0,1:T(8,128)(2,1)S(1)} %convolution_convert_fusion.1, bf16[512,128]{0,1:T(8,128)(2,1)S(1)} %get-tuple-element.26, f32[8192,256]{1,0:T(8,128)} %all-reduce.9.cloned.1.call-done, bf16[1,512,8192]{2,1,0:T(8,128)(2,1)} %param.4, bf16[1,512,8192]{2,1,0:T(8,128)(2,1)} %param.3), kind=kOutput, calls=%fused_computation.4 | convolution fusion | flops 2181562368 | bytes 33816576 | tf_op jit(solution)/shard_map/dot_general | solution.py:35
  (9 shorter events, 0.1 us)
Async XLA Ops:
  7.2 57.6 %all-gather.2.cloned.1.call-start = ((), (), s32[]{:S(2)}) async-start(), calls=%async_computation | async-start | bytes 4456448 | tf_op jit(solution)/shard_map/all_gather | solution.py:24
  7.9 125.8 %all-reduce.5.cloned.1.call-start = ((), (), s32[]{:S(2)}) async-start(), calls=%async_computation.1 | async-start | bytes 1048576 | tf_op jit(solution)/shard_map/psum | solution.py:27
  74.9 144.4 %all-reduce.7.cloned.1.call-start = ((), (), s32[]{:S(2)}) async-start(), calls=%async_computation.2 | async-start | bytes 262144 | tf_op jit(solution)/shard_map/psum | solution.py:28
  136.5 324.1 %all-reduce.9.cloned.1.call-start = ((), (), s32[]{:S(2)}) async-start(), calls=%async_computation.3 | async-start | bytes 16777216 | tf_op jit(solution)/shard_map/psum | solution.py:32
Sparse Core Ops, SparseCore 0:
  10.1 54.5 all-gather.1
  75.0 58.5 all-reduce.4
  137.8 81.5 all-reduce.6
  297.9 162.6 all-reduce.8
where the time goes:
time: 485 us; the launch traced here: 484 us
  waiting for transfers between devices  362 us (75%)
  other arithmetic  58.6 us (12%)
  matrix products  42.5 us (9%)
  between operations  15.2 us (3%)
  local copies, waits for them, and re-layouts  5.99 us (1%)
    psum x1, waiting for transfers between devices, shards(): factor_full = lax.psum(term, ('dp', 'mp')) / replicas  163 us
    psum x1, waiting for transfers between devices, shards(): lax.psum(gram_of(summed).astype(jnp.bfloat16), 'mp').astype(jnp.float32)  82.5 us
    psum x1, waiting for transfers between devices, shards(): summed = lax.psum(projection, 'dp')  58.7 us
    all_gather x1, waiting for transfers between devices, shards(): lax.all_gather(query, 'mp', axis=0, tiled=True)  56.8 us
    another operation x6, other arithmetic, orthonormal(): lower = jnp.linalg.cholesky(gram)  34 us
    another operation x3, other arithmetic, orthonormal(): lax.linalg.triangular_solve(lower, rows_proj, left_side=False, lower=True...  19.7 us
    dot_general x1, matrix products, shards(): lax.dot_general(adjusted, basis, contract, preferred_element_type=jnp.flo...  13.2 us
    dot_general x1, matrix products, shards(): lax.dot_general(basis, factor_half, (((1,), (1,)), ((), ())), preferred_e...  12.5 us
  transfers between devices with their start and end apart: 4, of which 4 were waited for; matrix products, arithmetic and copies ran while one was open for 0% of the time, Pallas kernels for 0%

commit v1 on v0

v1 whole, which is shorter than its diff:
```python
import jax
import jax.numpy as jnp
from jax import lax
from jax.experimental import pallas as pl
from jax.experimental.pallas import tpu as pltpu
from jax.sharding import Mesh, PartitionSpec as P

BF16 = jnp.bfloat16
F32 = jnp.float32
VMEM_LIMIT = 48 * 1024 * 1024
ROWS, COLS, RANK = 512, 8192, 256
NZ, NM = 4, 16
HALF = COLS // 2
BLK = COLS // NM
SUB = BLK // 2
TN_DOT = (((0,), (0,)), ((), ()))

SMEM = pl.BlockSpec(memory_space=pltpu.SMEM)


def params(**kw):
    return pltpu.CompilerParams(vmem_limit_bytes=VMEM_LIMIT, **kw)


def pick(c, first, second):
    return jnp.where(c == 0, first, second)


def adjust_kernel(c_ref, g_ref, e_ref, own_ref, other_ref):
    c = c_ref[0]
    a = (g_ref[...].astype(F32) + e_ref[...].astype(F32)).astype(BF16)
    shards = a.shape[1] // BLK
    for ref, flip in ((own_ref, 0), (other_ref, 1)):
        for s in range(shards):
            lo = a[:, s * BLK : s * BLK + SUB]
            hi = a[:, s * BLK + SUB : (s + 1) * BLK]
            ref[:, s * SUB : (s + 1) * SUB] = pick(c, (lo, hi)[flip], (hi, lo)[flip])


def adjust(c, gradient, error):
    steps = 8
    wide = pl.BlockSpec((ROWS, COLS // steps), lambda j: (0, j))
    half = pl.BlockSpec((ROWS, HALF // steps), lambda j: (0, j))
    out = jax.ShapeDtypeStruct((ROWS, HALF), BF16)
    return pl.pallas_call(
        adjust_kernel,
        grid=(steps,),
        in_specs=[SMEM, wide, wide],
        out_specs=[half, half],
        out_shape=[out, out],
        compiler_params=params(),
        cost_estimate=pl.CostEstimate(flops=ROWS * COLS, bytes_accessed=6 * ROWS * COLS, transcendentals=0),
    )(c, gradient, error)


def project_kernel(c_ref, a_ref, b_ref, q_ref, keep_ref, give_ref, acc):
    step = pl.program_id(0)

    @pl.when(step == 0)
    def _():
        acc[...] = jnp.zeros_like(acc)

    q = q_ref[...]
    acc[...] += jnp.dot(a_ref[...], q, preferred_element_type=F32)
    acc[...] += jnp.dot(b_ref[...], q, preferred_element_type=F32)

    @pl.when(step == pl.num_programs(0) - 1)
    def _():
        c = c_ref[0]
        h = ROWS // 2
        keep_ref[...] = acc[pl.ds(c * h, h), :]
        give_ref[...] = acc[pl.ds((1 - c) * h, h), :]


def project(c, own, recv, query):
    steps = 4
    a = pl.BlockSpec((ROWS, HALF // steps), lambda j: (0, j))
    q = pl.BlockSpec((HALF // steps, RANK), lambda j: (j, 0))
    o = pl.BlockSpec((ROWS // 2, RANK), lambda j: (0, 0))
    out = jax.ShapeDtypeStruct((ROWS // 2, RANK), F32)
    return pl.pallas_call(
        project_kernel,
        grid=(steps,),
        in_specs=[SMEM, a, a, q],
        out_specs=[o, o],
        out_shape=[out, out],
        scratch_shapes=[pltpu.VMEM((ROWS, RANK), F32)],
        compiler_params=params(),
        cost_estimate=pl.CostEstimate(flops=4 * ROWS * HALF * RANK, bytes_accessed=4 * ROWS * HALF + 2 * HALF * RANK, transcendentals=0),
    )(c, own, recv, query)


def term_kernel(c_ref, s_ref, a_ref, b_ref, t_ref, g_ref):
    s = s_ref[...]
    t = lax.dot_general(s, a_ref[...], TN_DOT, preferred_element_type=F32)
    t += lax.dot_general(s, b_ref[...], TN_DOT, preferred_element_type=F32)
    t_ref[0] = t.astype(BF16).reshape(NM, RANK // NM, HALF // NZ)

    @pl.when(pl.program_id(0) == 0)
    def _():
        g = lax.dot_general(s, s, TN_DOT, preferred_element_type=F32)
        h = RANK // 2
        g_ref[...] = pick(c_ref[0], g[:h], g[h:])


def term(c, summed, own, recv):
    a = pl.BlockSpec((ROWS, HALF // NZ), lambda j: (0, j))
    return pl.pallas_call(
        term_kernel,
        grid=(NZ,),
        in_specs=[SMEM, pl.BlockSpec((ROWS, RANK), lambda j: (0, 0)), a, a],
        out_specs=[
            pl.BlockSpec((1, NM, RANK // NM, HALF // NZ), lambda j: (j, 0, 0, 0)),
            pl.BlockSpec((RANK // 2, RANK), lambda j: (0, 0)),
        ],
        out_shape=[
            jax.ShapeDtypeStruct((NZ, NM, RANK // NM, HALF // NZ), BF16),
            jax.ShapeDtypeStruct((RANK // 2, RANK), F32),
        ],
        compiler_params=params(),
        cost_estimate=pl.CostEstimate(flops=4 * ROWS * HALF * RANK, bytes_accessed=4 * ROWS * HALF + 2 * HALF * RANK, transcendentals=0),
    )(c, summed, own, recv)


def total_kernel(x_ref, o_ref):
    n = x_ref.shape[0]
    total = jnp.sum(x_ref[...].astype(F32), axis=0).astype(BF16)
    o_ref[...] = jnp.broadcast_to(total[None], (n,) + total.shape)


def total(pieces):
    return pl.pallas_call(
        total_kernel,
        in_specs=[pl.BlockSpec(memory_space=pltpu.VMEM)],
        out_specs=pl.BlockSpec(memory_space=pltpu.VMEM),
        out_shape=jax.ShapeDtypeStruct(pieces.shape, BF16),
        compiler_params=params(),
        cost_estimate=pl.CostEstimate(flops=pieces.size, bytes_accessed=4 * pieces.size, transcendentals=0),
    )(pieces)


def finish_kernel(c_ref, m_ref, w_ref, inv_ref, own_ref, other_ref, t_ref, u_ref, err_ref, f_ref):
    c, m = c_ref[0], m_ref[0]
    w = w_ref[...]
    t = t_ref[0].reshape(RANK, HALF // NZ)
    u = u_ref[0].reshape(RANK, HALF // NZ)
    mine = own_ref[...].astype(F32) - jnp.dot(w, t, preferred_element_type=F32)
    theirs = other_ref[...].astype(F32) - jnp.dot(w, u, preferred_element_type=F32)
    mine, theirs = mine.astype(BF16), theirs.astype(BF16)
    shards = HALF // NZ // SUB
    for s in range(shards):
        x = mine[:, s * SUB : (s + 1) * SUB]
        y = theirs[:, s * SUB : (s + 1) * SUB]
        err_ref[:, s * BLK : s * BLK + SUB] = pick(c, x, y)
        err_ref[:, s * BLK + SUB : (s + 1) * BLK] = pick(c, y, x)

        @pl.when(pl.program_id(0) * shards + s == m)
        def _():
            cut = slice(s * SUB, (s + 1) * SUB)
            tm = pick(c, t[:, cut], u[:, cut]), pick(c, u[:, cut], t[:, cut])
            for k in range(2):
                f = jnp.dot(inv_ref[...], tm[k].astype(F32), precision=lax.Precision.HIGHEST, preferred_element_type=F32)
                f_ref[k * SUB : (k + 1) * SUB, :] = f.T * 0.125


def finish(c, m, w, inv, own, other, t, u):
    a = pl.BlockSpec((ROWS, HALF // NZ), lambda j: (0, j))
    tt = pl.BlockSpec((1, NM, RANK // NM, HALF // NZ), lambda j: (j, 0, 0, 0))
    return pl.pallas_call(
        finish_kernel,
        grid=(NZ,),
        in_specs=[
            SMEM,
            SMEM,
            pl.BlockSpec((ROWS, RANK), lambda j: (0, 0)),
            pl.BlockSpec((RANK, RANK), lambda j: (0, 0)),
            a,
            a,
            tt,
            tt,
        ],
        out_specs=[
            pl.BlockSpec((ROWS, COLS // NZ), lambda j: (0, j)),
            pl.BlockSpec((BLK, RANK), lambda j: (0, 0)),
        ],
        out_shape=[
            jax.ShapeDtypeStruct((ROWS, COLS), BF16),
            jax.ShapeDtypeStruct((BLK, RANK), F32),
        ],
        compiler_params=params(),
        cost_estimate=pl.CostEstimate(flops=2 * ROWS * COLS * RANK, bytes_accessed=4 * ROWS * COLS + 2 * COLS * RANK, transcendentals=0),
    )(c, m, w, inv, own, other, t, u)


def swap(x):
    return lax.ppermute(x, "c", [(0, 1), (1, 0)])


def ring_sum(x, axis):
    x1, x2, x3 = (lax.ppermute(x, axis, [(i, (i + k) % 4) for i in range(4)]) for k in (1, 2, 3))
    return (x.astype(F32) + x2.astype(F32)) + (x1.astype(F32) + x3.astype(F32))


def join(c, mine, theirs):
    return jnp.concatenate([pick(c, mine, theirs), pick(c, theirs, mine)], axis=0)


def shards(gradient, error, query):
    gradient, error = gradient[0], error[0]
    c = lax.axis_index("c")
    m = lax.axis_index("x") * 4 + lax.axis_index("y")
    cv, mv = c.reshape(1).astype(jnp.int32), m.reshape(1).astype(jnp.int32)

    with jax.named_scope("query_gather"):
        part = lax.dynamic_slice_in_dim(query, c * SUB, SUB, 0)
        copies = jnp.broadcast_to(part[None], (NM, SUB, RANK))
        half_query = lax.all_to_all(copies, ("x", "y"), 0, 0, tiled=True).reshape(HALF, RANK)

    with jax.named_scope("adjust"):
        own, other = adjust(cv, gradient, error)
        recv = swap(other)

    with jax.named_scope("project"):
        keep, give = project(cv, own, recv, half_query)
        chip = (keep + swap(give)).astype(BF16)
        rows = ring_sum(chip, "z").astype(BF16)
        summed = join(c, rows, swap(rows))

    with jax.named_scope("term"):
        pieces, gram_half = term(cv, summed, own, recv)
        pieces = pieces.reshape(NZ * NM, RANK // NM, HALF // NZ)
        pieces = lax.all_to_all(pieces, ("z", "x", "y"), 0, 0, tiled=True)

    with jax.named_scope("gram"):
        gram_half = ring_sum(ring_sum(gram_half, "x"), "y")
        gram = join(c, gram_half, swap(gram_half))
        lower = lax.linalg.cholesky(gram, symmetrize_input=False)
        inv = lax.linalg.triangular_solve(lower, jnp.eye(RANK, dtype=F32), left_side=True, lower=True)
        basis = lax.dot_general(summed.astype(F32), inv, (((1,), (1,)), ((), ())), precision=lax.Precision.HIGHEST)
        w = (jnp.dot(basis, inv, precision=lax.Precision.HIGHEST) * 0.125).astype(BF16)

    with jax.named_scope("gather"):
        mine = lax.all_to_all(total(pieces), ("z", "x", "y"), 0, 0, tiled=True)
        mine = mine.reshape(NZ, NM, RANK // NM, HALF // NZ)
        theirs = swap(mine)

    with jax.named_scope("finish"):
        new_error, factor = finish(cv, mv, w, inv, own, other, mine, theirs)
    return factor, new_error[None]


def solution(mesh):
    grid = Mesh(mesh.devices.reshape(4, 2, 4, 4), ("z", "c", "x", "y"))
    in_specs = (P(("z", "c"), ("x", "y"), None), P(("z", "c"), ("x", "y"), None), P(("x", "y"), None))
    out_specs = (P(("x", "y"), None), P(("z", "c"), ("x", "y"), None))
    return jax.shard_map(shards, mesh=grid, in_specs=in_specs, out_specs=out_specs, check_vma=False)
```

time: 485 us -> 228 us (0.47)
  waiting for transfers between devices: 362 us -> 61.3 us
  matrix products: 42.5 us -> 2.32 us
  Pallas kernels: 0 us -> 33.6 us
  blocking collectives: 0 us -> 33.6 us
  starting transfers between devices: 0.34 us -> 32.2 us
  between operations: 15.2 us -> 2.2 us
    psum x3 -> x0, waiting for transfers between devices: 304 us -> none  [the longest x1 163 us: shards(): factor_full = lax.psum(term, ('dp', 'mp')) / replicas]
    all_gather x1 -> x0, waiting for transfers between devices: 56.8 us -> none  [shards(): lax.all_gather(query, 'mp', axis=0, tiled=True)]
    dot_general x4 -> x2, matrix products: 38.7 us -> 1 us  [the longest x1 0.59 us: shards(): jnp.dot(basis, inv, precision=lax.Precision.HIGHEST) * 0.125]
    ppermute x0 -> x14, waiting for transfers between devices: none -> 36.6 us  [the longest x9 33.5 us: ring_sum(): lax.ppermute(x, axis, [(i, (i + k) % 4) for i in range(4)])]
    all_to_all x0 -> x1, blocking collectives: none -> 33.6 us  [shards(): lax.all_to_all(copies, ('x', 'y'), 0, 0, tiled=True).reshape(HALF, RANK)]
    pallas_call x0 -> x5, Pallas kernels: none -> 33.6 us  [the longest x1 10.6 us: adjust(): pl.pallas_call(adjust_kernel, grid=(steps,), in_specs=[SMEM, wide, wide],...]
    all_to_all x0 -> x2, waiting for transfers between devices: none -> 24.7 us  [the longest x1 24.7 us: shards(): pieces = lax.all_to_all(pieces, ('z', 'x', 'y'), 0, 0, tiled=True)]
    ppermute x0 -> x14, starting transfers between devices: none -> 21.4 us  [the longest x9 13.2 us: ring_sum(): lax.ppermute(x, axis, [(i, (i + k) % 4) for i in range(4)])]
  transfers between devices with their start and end apart: 4 -> 16, of which waited for: 4 -> 9; matrix products, arithmetic and copies ran while one was open for 0% -> 27% of each run, Pallas kernels for 0% -> 1%
where the time goes in v1:
time: 228 us; the launch traced here: 227 us
  waiting for transfers between devices  61.3 us (27%)
  other arithmetic  54 us (24%)
  Pallas kernels  33.6 us (15%)
  blocking collectives  33.6 us (15%)
  starting transfers between devices  32.2 us (14%)
  local copies, waits for them, and re-layouts  7.65 us (3%)
  matrix products  2.32 us (1%)
    another operation x6, other arithmetic, shards(): lower = lax.linalg.cholesky(gram, symmetrize_input=False)  34 us
    all_to_all x1, blocking collectives, shards(): lax.all_to_all(copies, ('x', 'y'), 0, 0, tiled=True).reshape(HALF, RANK)  33.6 us
    ppermute x9, waiting for transfers between devices, ring_sum(): lax.ppermute(x, axis, [(i, (i + k) % 4) for i in range(4)])  33.5 us
    all_to_all x1, waiting for transfers between devices, shards(): pieces = lax.all_to_all(pieces, ('z', 'x', 'y'), 0, 0, tiled=True)  24.7 us
    another operation x4, other arithmetic, shards(): lax.linalg.triangular_solve(lower, jnp.eye(RANK, dtype=F32), left_side=Tr...  19.7 us
    ppermute x9, starting transfers between devices, ring_sum(): lax.ppermute(x, axis, [(i, (i + k) % 4) for i in range(4)])  13.2 us
    pallas_call x1, Pallas kernels, adjust(): pl.pallas_call(adjust_kernel, grid=(steps,), in_specs=[SMEM, wide, wide],...  10.6 us
    pallas_call x1, Pallas kernels, finish(): pl.pallas_call(finish_kernel, grid=(NZ,), in_specs=[SMEM, SMEM, pl.BlockS...  10 us
  transfers between devices with their start and end apart: 16, of which 9 were waited for; matrix products, arithmetic and copies ran while one was open for 27% of the time, Pallas kernels for 1%

profile of v1, /device:TPU:1, one launch (start us, length us, event | category | flops | bytes accessed | tf_op | source)
XLA Modules:
  0.0 227.0 jit_solution(8903167957505414817)
XLA Ops:
  0.6 0.0 copy-start
  0.7 10.6 %adjust.1 = (bf16[512,4096]{1,0:T(8,128)(2,1)S(1)}, bf16[512,4096]{1,0:T(8,128)(2,1)}) custom-call(s32[1]{0:T(128)} %bitcast.c_ref, bf16[512,8192]{1,0:T(8,128)(2,1)} %bitcast.40, bf16[512,8192]{1,0:T(8,128)(2,1)} %bitcast.41), custom_call_target="tpu_custom_call" | custom-call | flops 4194304 | bytes 25165824 | tf_op jit(solution)/shard_map/adjust/pallas_call | solution.py:45
  11.2 0.0 copy-start.1
  11.2 2.0 copy-done.1
  13.2 1.4 collective-permute-start
  14.6 0.0 copy-done
  14.6 0.2 broadcast_in_dim.4
  14.8 33.6 %all_to_all.15 = bf16[16,256,256]{2,1,0:T(8,128)(2,1)S(1)} all-to-all(bf16[16,256,256]{2,1,0:T(8,128)(2,1)S(1)} %broadcast_in_dim.4), channel_id=1, replica_groups=mesh['z'=4,'c'=2,'x'=4,'y'=4] {'x','y'}, dimensions={0} | all-to-all | bytes 4194304 | tf_op jit(solution)/shard_map/query_gather/all_to_all | solution.py:217
  48.5 0.0 collective-permute-done.b_ref
  48.5 5.5 %project.1 = (f32[256,256]{1,0:T(8,128)S(1)}, f32[256,256]{1,0:T(8,128)S(1)}) custom-call(s32[1]{0:T(128)} %bitcast.c_ref, bf16[512,4096]{1,0:T(8,128)(2,1)} %copy-done.1, bf16[512,4096]{1,0:T(8,128)(2,1)} %collective-permute-done.b_ref, bf16[4096,256]{1,0:T(8,128)(2,1)S(1)} %bitcast.38), custom_call_target="tpu_custom_call" | custom-call | flops 2147483648 | bytes 10485760 | tf_op jit(solution)/shard_map/project/pallas_call | solution.py:81
  54.0 2.4 %collective-permute-start.1 = (f32[256,256]{1,0:T(8,128)S(1)}, f32[256,256]{1,0:T(8,128)S(1)}, u32[]{:S(2)}, u32[]{:S(2)}) collective-permute-start(f32[256,256]{1,0:T(8,128)S(1)} %get-tuple-element.13), channel_id=1, source_target_pairs={{0,16},{16,0},{1,17},{17,1},{2,18},{18,2},{3,19},{19,3},{4,20},{20... | collective-permute-start | bytes 786440 | tf_op jit(solution)/shard_map/project/ppermute | solution.py:196
  56.4 1.2 collective-permute-done.1
  57.6 3.8 %collective-permute-start.4 = (bf16[256,256]{1,0:T(8,128)(2,1)S(1)}, bf16[256,256]{1,0:T(8,128)(2,1)S(1)}, u32[]{:S(2)}, u32[]{:S(2)}) collective-permute-start(bf16[256,256]{1,0:T(8,128)(2,1)S(1)} %add_convert_fusion.1), channel_id=1, source_target_pairs={{0,96},{32,0},{64,32},{96,64},{1,97},{33,1},{65,33},{97,65},{2,98}... | collective-permute-start | bytes 393224 | tf_op jit(solution)/shard_map/project/ppermute | solution.py:200
  61.4 0.0 collective-permute-start.3
  61.4 1.3 collective-permute-start.2
  62.7 1.2 collective-permute-done.4
  63.9 6.3 %collective-permute-done.3 = bf16[256,256]{1,0:T(8,128)(2,1)S(1)} collective-permute-done((bf16[256,256]{1,0:T(8,128)(2,1)S(1)}, bf16[256,256]{1,0:T(8,128)(2,1)S(1)}, u32[]{:S(2)}, u32[]{:S(2)}) %collective-permute-start.3) | collective-permute-done | bytes 131104 | tf_op jit(solution)/shard_map/project/ppermute | solution.py:200
  70.2 0.0 collective-permute-done.2
  70.2 0.1 add_convert_fusion
  70.3 1.2 collective-permute-start.5
  71.5 1.0 collective-permute-done.5
  72.5 5.7 %term.1 = (bf16[4,16,16,1024]{3,2,1,0:T(8,128)(2,1)S(1)}, f32[128,256]{1,0:T(8,128)S(1)}) custom-call(s32[1]{0:T(128)} %bitcast.c_ref, bf16[512,256]{1,0:T(8,128)(2,1)S(1)} %pad_maximum_fusion.s_ref, bf16[512,4096]{1,0:T(8,128)(2,1)} %copy-done.1, bf16[512,4096]{1,0:T(8,128)(2,1)} %collective-permute-done.b_ref), custom_call_target="tpu_custom_call" | custom-call | flops 2147483648 | bytes 10485760 | tf_op jit(solution)/shard_map/term/pallas_call | solution.py:108
  78.2 0.0 copy-start.2
  78.2 1.3 copy-done.2
  79.5 4.7 %all-to-all-start.1 = ((bf16[64,16,1024]{2,1,0:T(8,128)(2,1)}), bf16[64,16,1024]{2,1,0:T(8,128)(2,1)S(1)}, u32[]{:S(2)}, u32[]{:S(2)}) async-start(bf16[64,16,1024]{2,1,0:T(8,128)(2,1)} %bitcast.39), calls=%async_computation.1 | async-start | bytes 4194304 | tf_op jit(solution)/shard_map/term/all_to_all | solution.py:232
  84.2 2.3 collective-permute-start.8
  86.5 0.0 collective-permute-start.7
  86.5 1.7 collective-permute-start.6
  88.2 24.7 %all-to-all-done.1.x_ref = bf16[64,16,1024]{2,1,0:T(8,128)(2,1)S(1)} async-done(((bf16[64,16,1024]{2,1,0:T(8,128)(2,1)}), bf16[64,16,1024]{2,1,0:T(8,128)(2,1)S(1)}, u32[]{:S(2)}, u32[]{:S(2)}) %all-to-all-start.1) | async-done | bytes 2097184 | tf_op jit(solution)/shard_map/term/all_to_all | solution.py:232
  112.9 1.8 gather.3
  114.7 6.2 %all-to-all-start.2 = ((bf16[64,16,1024]{2,1,0:T(8,128)(2,1)}), bf16[64,16,1024]{2,1,0:T(8,128)(2,1)S(1)}, u32[]{:S(2)}, u32[]{:S(2)}) async-start(bf16[64,16,1024]{2,1,0:T(8,128)(2,1)} %gather.3), calls=%async_computation.2 | async-start | bytes 4194304 | tf_op jit(solution)/shard_map/gather/all_to_all | solution.py:243
  120.9 0.0 collective-permute-done.8
  120.9 0.0 collective-permute-done.7
  120.9 0.0 collective-permute-done.6
  120.9 2.3 %collective-permute-start.11 = (f32[128,256]{1,0:T(8,128)S(1)}, f32[128,256]{1,0:T(8,128)S(1)}, u32[]{:S(2)}, u32[]{:S(2)}) collective-permute-start(f32[128,256]{1,0:T(8,128)S(1)} %add_add_fusion.1), channel_id=1, source_target_pairs={{0,3},{1,0},{2,1},{3,2},{4,7},{5,4},{6,5},{7,6},{8,11},{9,8},{10,9... | collective-permute-start | bytes 393224 | tf_op jit(solution)/shard_map/gram/ppermute | solution.py:200
  123.2 0.0 collective-permute-start.10
  123.2 1.8 collective-permute-start.9
  125.0 17.5 %collective-permute-done.11 = f32[128,256]{1,0:T(8,128)S(1)} collective-permute-done((f32[128,256]{1,0:T(8,128)S(1)}, f32[128,256]{1,0:T(8,128)S(1)}, u32[]{:S(2)}, u32[]{:S(2)}) %collective-permute-start.11) | collective-permute-done | bytes 131104 | tf_op jit(solution)/shard_map/gram/ppermute | solution.py:200
  142.5 3.2 %collective-permute-done.10 = f32[128,256]{1,0:T(8,128)S(1)} collective-permute-done((f32[128,256]{1,0:T(8,128)S(1)}, f32[128,256]{1,0:T(8,128)S(1)}, u32[]{:S(2)}, u32[]{:S(2)}) %collective-permute-start.10) | collective-permute-done | bytes 131104 | tf_op jit(solution)/shard_map/gram/ppermute | solution.py:200
  145.7 5.3 %collective-permute-done.9 = f32[128,256]{1,0:T(8,128)S(1)} collective-permute-done((f32[128,256]{1,0:T(8,128)S(1)}, f32[128,256]{1,0:T(8,128)S(1)}, u32[]{:S(2)}, u32[]{:S(2)}) %collective-permute-start.9) | collective-permute-done | bytes 131104 | tf_op jit(solution)/shard_map/gram/ppermute | solution.py:200
  151.1 2.5 %collective-permute-start.12 = (f32[128,256]{1,0:T(8,128)S(1)}, f32[128,256]{1,0:T(8,128)S(1)}, u32[]{:S(2)}, u32[]{:S(2)}) collective-permute-start(f32[128,256]{1,0:T(8,128)S(1)} %add_add_fusion), channel_id=1, source_target_pairs={{0,16},{16,0},{1,17},{17,1},{2,18},{18,2},{3,19},{19,3},{4,20},{20... | collective-permute-start | bytes 393224 | tf_op jit(solution)/shard_map/gram/ppermute | solution.py:196
  153.7 1.0 collective-permute-done.12
  154.6 11.7 %cholesky.50 = f32[128,128]{1,0:T(8,128)S(1)} custom-call(f32[128,128]{1,0:T(8,128)S(1)} %slice_select_fusion), custom_call_target="Cholesky" | custom-call | tf_op jit(solution)/shard_map/gram/cholesky | solution.py:237
  166.4 9.8 %custom-call.11 = f32[1,128,128]{1,2,0:T(8,128)S(1)} custom-call(f32[1,128,128]{2,1,0:T(8,128)S(1)} %get-tuple-element.41), custom_call_target="InvertDiagBlocksLowerTriangular" | custom-call | tf_op jit(solution)/shard_map/gram/cholesky | solution.py:237
  176.2 0.2 constant_dynamic-update-slice_fusion.1
  176.4 0.3 slice_subtract_fusion
  176.7 11.7 %cholesky.105 = f32[128,128]{1,0:T(8,128)S(1)} custom-call(f32[128,128]{1,0:T(8,128)S(1)} %slice_subtract_fusion), custom_call_target="Cholesky" | custom-call | tf_op jit(solution)/shard_map/gram/cholesky | solution.py:237
  188.5 0.7 compare_reduce_fusion
  190.5 0.0 all-to-all-done.2
  190.5 0.7 collective-permute-start.13
  191.2 0.1 triangular_solve.63
  191.3 4.1 %while.1 = (s32[]{:T(128)}, f32[256,256]{1,0:T(8,128)S(1)}, s32[2,2]{1,0:T(2,128)S(1)}, f32[2,128,128]{2,1,0:T(8,128)S(1)}, s32[]{:T(128)}) while((s32[]{:T(128)}, f32[256,256]{1,0:T(8,128)S(1)}, s32[2,2]{1,0:T(2,128)S(1)}, f32[2,128,128]{2,1,0:T(8,128)S(1)}, s32[]{:T(128)}) %tuple.28), condition=%wide.while_cond, body=%wide.while_body.sunk | while | flops 2 | bytes 131189 | solution.py:238
  191.3 0.6 fusion.16
  191.9 1.4 bitcast_dynamic-update-slice_fusion.2
  193.3 0.6 fusion.16
  193.9 1.4 bitcast_dynamic-update-slice_fusion.2
  195.4 19.7 %custom-call.12 = f32[2,128,128]{1,2,0:T(8,128)S(1)} custom-call(f32[2,128,128]{2,1,0:T(8,128)S(1)} %get-tuple-element.25), custom_call_target="InvertDiagBlocksLowerTriangular" | custom-call | tf_op jit(solution)/shard_map/gram/triangular_solve | solution.py:238
  215.0 0.3 fusion.1
  215.3 0.3 convolution_subtract_fusion
  215.6 0.3 fusion.4
  215.9 0.4 fusion.8
  216.4 0.6 fusion.w_ref
  217.0 0.0 collective-permute-done.13.u_ref
  217.0 10.0 %finish.1 = (bf16[512,8192]{1,0:T(8,128)(2,1)}, f32[512,256]{1,0:T(8,128)}) custom-call(s32[1]{0:T(128)} %bitcast.c_ref, s32[1]{0:T(128)} %bitcast.1.m_ref, bf16[512,256]{1,0:T(8,128)(2,1)S(1)} %fusion.w_ref, f32[256,256]{1,0:T(8,128)S(1)} %pad_maximum_fusion.1.inv_ref, bf16[512,4096]{1,0:T(8,128)(2,1)} %copy-done.1, ...), custom_call_target="tpu_custom_call" | custom-call | flops 2147483648 | bytes 20971520 | tf_op jit(solution)/shard_map/finish/pallas_call | solution.py:169
  (18 shorter events, 0.4 us)
Async XLA Ops:
  0.6 14.0 %copy-start = (bf16[512,256]{1,0:T(8,128)(2,1)S(1)}, bf16[512,256]{1,0:T(8,128)(2,1)}, u32[]{:S(2)}) copy-start(bf16[512,256]{1,0:T(8,128)(2,1)} %param.5) | copy-start | bytes 786436
  11.2 2.0 copy-start.1
  13.2 35.3 %collective-permute-start = (bf16[512,4096]{1,0:T(8,128)(2,1)}, bf16[512,4096]{1,0:T(8,128)(2,1)}, u32[]{:S(2)}, u32[]{:S(2)}) collective-permute-start(bf16[512,4096]{1,0:T(8,128)(2,1)} %get-tuple-element.11.other_ref), channel_id=1, source_target_pairs={{0,16},{16,0},{1,17},{17,1},{2,18},{18,2},{3,19},{19,3},{4,20},{20... | collective-permute-start | bytes 12582920 | tf_op jit(solution)/shard_map/adjust/ppermute | solution.py:196
  54.0 3.6 %collective-permute-start.1 = (f32[256,256]{1,0:T(8,128)S(1)}, f32[256,256]{1,0:T(8,128)S(1)}, u32[]{:S(2)}, u32[]{:S(2)}) collective-permute-start(f32[256,256]{1,0:T(8,128)S(1)} %get-tuple-element.13), channel_id=1, source_target_pairs={{0,16},{16,0},{1,17},{17,1},{2,18},{18,2},{3,19},{19,3},{4,20},{20... | collective-permute-start | bytes 786440 | tf_op jit(solution)/shard_map/project/ppermute | solution.py:196
  57.6 6.3 %collective-permute-start.4 = (bf16[256,256]{1,0:T(8,128)(2,1)S(1)}, bf16[256,256]{1,0:T(8,128)(2,1)S(1)}, u32[]{:S(2)}, u32[]{:S(2)}) collective-permute-start(bf16[256,256]{1,0:T(8,128)(2,1)S(1)} %add_convert_fusion.1), channel_id=1, source_target_pairs={{0,96},{32,0},{64,32},{96,64},{1,97},{33,1},{65,33},{97,65},{2,98}... | collective-permute-start | bytes 393224 | tf_op jit(solution)/shard_map/project/ppermute | solution.py:200
  61.4 8.8 %collective-permute-start.3 = (bf16[256,256]{1,0:T(8,128)(2,1)S(1)}, bf16[256,256]{1,0:T(8,128)(2,1)S(1)}, u32[]{:S(2)}, u32[]{:S(2)}) collective-permute-start(bf16[256,256]{1,0:T(8,128)(2,1)S(1)} %add_convert_fusion.1), channel_id=1, source_target_pairs={{0,32},{32,64},{64,96},{96,0},{1,33},{33,65},{65,97},{97,1},{2,34}... | collective-permute-start | bytes 393224 | tf_op jit(solution)/shard_map/project/ppermute | solution.py:200
  61.4 8.8 %collective-permute-start.2 = (bf16[256,256]{1,0:T(8,128)(2,1)S(1)}, bf16[256,256]{1,0:T(8,128)(2,1)S(1)}, u32[]{:S(2)}, u32[]{:S(2)}) collective-permute-start(bf16[256,256]{1,0:T(8,128)(2,1)S(1)} %add_convert_fusion.1), channel_id=1, source_target_pairs={{0,64},{32,96},{64,0},{96,32},{1,65},{33,97},{65,1},{97,33},{2,66}... | collective-permute-start | bytes 393224 | tf_op jit(solution)/shard_map/project/ppermute | solution.py:200
  70.3 2.2 collective-permute-start.5
  78.2 1.3 copy-start.2
  79.5 33.4 %all-to-all-start.1 = ((bf16[64,16,1024]{2,1,0:T(8,128)(2,1)}), bf16[64,16,1024]{2,1,0:T(8,128)(2,1)S(1)}, u32[]{:S(2)}, u32[]{:S(2)}) async-start(bf16[64,16,1024]{2,1,0:T(8,128)(2,1)} %bitcast.39), calls=%async_computation.1 | async-start | bytes 4194304 | tf_op jit(solution)/shard_map/term/all_to_all | solution.py:232
  84.2 36.6 %collective-permute-start.8 = (f32[128,256]{1,0:T(8,128)S(1)}, f32[128,256]{1,0:T(8,128)S(1)}, u32[]{:S(2)}, u32[]{:S(2)}) collective-permute-start(f32[128,256]{1,0:T(8,128)S(1)} %get-tuple-element.14), channel_id=1, source_target_pairs={{0,12},{4,0},{8,4},{12,8},{1,13},{5,1},{9,5},{13,9},{2,14},{6,2},{... | collective-permute-start | bytes 393224 | tf_op jit(solution)/shard_map/gram/ppermute | solution.py:200
  86.5 34.4 %collective-permute-start.7 = (f32[128,256]{1,0:T(8,128)S(1)}, f32[128,256]{1,0:T(8,128)S(1)}, u32[]{:S(2)}, u32[]{:S(2)}) collective-permute-start(f32[128,256]{1,0:T(8,128)S(1)} %get-tuple-element.14), channel_id=1, source_target_pairs={{0,4},{4,8},{8,12},{12,0},{1,5},{5,9},{9,13},{13,1},{2,6},{6,10},{... | collective-permute-start | bytes 393224 | tf_op jit(solution)/shard_map/gram/ppermute | solution.py:200
  86.5 34.4 %collective-permute-start.6 = (f32[128,256]{1,0:T(8,128)S(1)}, f32[128,256]{1,0:T(8,128)S(1)}, u32[]{:S(2)}, u32[]{:S(2)}) collective-permute-start(f32[128,256]{1,0:T(8,128)S(1)} %get-tuple-element.14), channel_id=1, source_target_pairs={{0,8},{4,12},{8,0},{12,4},{1,9},{5,13},{9,1},{13,5},{2,10},{6,14},... | collective-permute-start | bytes 393224 | tf_op jit(solution)/shard_map/gram/ppermute | solution.py:200
  114.7 75.8 %all-to-all-start.2 = ((bf16[64,16,1024]{2,1,0:T(8,128)(2,1)}), bf16[64,16,1024]{2,1,0:T(8,128)(2,1)S(1)}, u32[]{:S(2)}, u32[]{:S(2)}) async-start(bf16[64,16,1024]{2,1,0:T(8,128)(2,1)} %gather.3), calls=%async_computation.2 | async-start | bytes 4194304 | tf_op jit(solution)/shard_map/gather/all_to_all | solution.py:243
  120.9 21.6 %collective-permute-start.11 = (f32[128,256]{1,0:T(8,128)S(1)}, f32[128,256]{1,0:T(8,128)S(1)}, u32[]{:S(2)}, u32[]{:S(2)}) collective-permute-start(f32[128,256]{1,0:T(8,128)S(1)} %add_add_fusion.1), channel_id=1, source_target_pairs={{0,3},{1,0},{2,1},{3,2},{4,7},{5,4},{6,5},{7,6},{8,11},{9,8},{10,9... | collective-permute-start | bytes 393224 | tf_op jit(solution)/shard_map/gram/ppermute | solution.py:200
  123.2 22.5 %collective-permute-start.10 = (f32[128,256]{1,0:T(8,128)S(1)}, f32[128,256]{1,0:T(8,128)S(1)}, u32[]{:S(2)}, u32[]{:S(2)}) collective-permute-start(f32[128,256]{1,0:T(8,128)S(1)} %add_add_fusion.1), channel_id=1, source_target_pairs={{0,1},{1,2},{2,3},{3,0},{4,5},{5,6},{6,7},{7,4},{8,9},{9,10},{10,1... | collective-permute-start | bytes 393224 | tf_op jit(solution)/shard_map/gram/ppermute | solution.py:200
  123.2 27.8 %collective-permute-start.9 = (f32[128,256]{1,0:T(8,128)S(1)}, f32[128,256]{1,0:T(8,128)S(1)}, u32[]{:S(2)}, u32[]{:S(2)}) collective-permute-start(f32[128,256]{1,0:T(8,128)S(1)} %add_add_fusion.1), channel_id=1, source_target_pairs={{0,2},{1,3},{2,0},{3,1},{4,6},{5,7},{6,4},{7,5},{8,10},{9,11},{10,... | collective-permute-start | bytes 393224 | tf_op jit(solution)/shard_map/gram/ppermute | solution.py:200
  151.1 3.5 %collective-permute-start.12 = (f32[128,256]{1,0:T(8,128)S(1)}, f32[128,256]{1,0:T(8,128)S(1)}, u32[]{:S(2)}, u32[]{:S(2)}) collective-permute-start(f32[128,256]{1,0:T(8,128)S(1)} %add_add_fusion), channel_id=1, source_target_pairs={{0,16},{16,0},{1,17},{17,1},{2,18},{18,2},{3,19},{19,3},{4,20},{20... | collective-permute-start | bytes 393224 | tf_op jit(solution)/shard_map/gram/ppermute | solution.py:196
  190.5 26.5 %collective-permute-start.13 = (bf16[4,16,16,1024]{3,2,1,0:T(8,128)(2,1)S(1)}, bf16[4,16,16,1024]{3,2,1,0:T(8,128)(2,1)}, u32[]{:S(2)}, u32[]{:S(2)}) collective-permute-start(bf16[4,16,16,1024]{3,2,1,0:T(8,128)(2,1)S(1)} %bitcast.36), channel_id=1, source_target_pairs={{0,16},{16,0},{1,17},{17,1},{2,18},{18,2},{3,19},{19,3},{4,20},{20... | collective-permute-start | bytes 6291464 | tf_op jit(solution)/shard_map/gather/ppermute | solution.py:196

commit v2 on v0

v2 whole, which is shorter than its diff:
```python
import jax
import jax.numpy as jnp
from jax import lax
from jax.experimental import pallas as pl
from jax.experimental.pallas import tpu as pltpu
from jax.sharding import Mesh, PartitionSpec as P

BF16 = jnp.bfloat16
F32 = jnp.float32
VMEM_LIMIT = 40 * 1024 * 1024
ROWS, COLS, RANK = 512, 8192, 256
NZ, NM = 4, 16
HALF = COLS // 2
BLK = COLS // NM
SUB = BLK // 2
TN_DOT = (((0,), (0,)), ((), ()))

SMEM = pl.BlockSpec(memory_space=pltpu.SMEM)
VMEM = pl.BlockSpec(memory_space=pltpu.VMEM)
CHUNKS = 4
CHUNK = HALF // CHUNKS
STEP = 512
PER = CHUNK // STEP


def params(limit=VMEM_LIMIT):
    return pltpu.CompilerParams(vmem_limit_bytes=limit)


HBM = pl.BlockSpec(memory_space=pltpu.HBM)


def in_hbm(*arrays):
    return [pltpu.with_memory_space_constraint(x, pltpu.HBM) for x in arrays]


def load(pairs, sem, first=0):
    copies = [pltpu.make_async_copy(src, dst, sem.at[first + i]) for i, (src, dst) in enumerate(pairs)]
    for copy in copies:
        copy.start()
    return copies


class Stream:
    DEPTH = 3

    def __init__(self, groups, sem):
        self.groups, self.sem, self.started = groups, sem, []
        for _ in range(self.DEPTH):
            self.more()

    def more(self):
        k = len(self.started)
        if k < len(self.groups):
            self.started.append(load(self.groups[k], self.sem, sum(len(g) for g in self.groups[:k])))

    def get(self, k):
        for copy in self.started[k]:
            copy.wait()
        self.more()


def strip(width):
    return pl.BlockSpec((ROWS, width), lambda j: (0, j))


def chunk_strips():
    return [pl.BlockSpec((ROWS, STEP), lambda j, k=k: (0, jnp.clip(j - k * PER, 0, PER - 1))) for k in range(CHUNKS)]


def pick(c, first, second):
    return jnp.where(c == 0, first, second)


def adjust_kernel(c_ref, g_ref, e_ref, own_ref, *other_refs):
    c, step = c_ref[0], pl.program_id(0)
    a = (g_ref[...].astype(F32) + e_ref[...].astype(F32)).astype(BF16)
    for s in range(STEP // SUB):
        lo = a[:, s * BLK : s * BLK + SUB]
        hi = a[:, s * BLK + SUB : (s + 1) * BLK]
        own_ref[:, s * SUB : (s + 1) * SUB] = pick(c, lo, hi)
        other = pick(c, hi, lo)
        for k, ref in enumerate(other_refs):

            @pl.when(step // PER == k)
            def _():
                ref[:, s * SUB : (s + 1) * SUB] = other


def adjust(c, gradient, error):
    return pl.pallas_call(
        adjust_kernel,
        grid=(HALF // STEP,),
        in_specs=[SMEM, strip(2 * STEP), strip(2 * STEP)],
        out_specs=[strip(STEP)] + chunk_strips(),
        out_shape=[pltpu.HBM((ROWS, HALF), BF16)] + [pltpu.HBM((ROWS, CHUNK), BF16)] * CHUNKS,
        compiler_params=params(60 * 1024 * 1024),
        cost_estimate=pl.CostEstimate(flops=ROWS * COLS, bytes_accessed=6 * ROWS * COLS, transcendentals=0),
    )(c, gradient, error)


def pair_kernel(own_ref, *refs):
    chunks, o_ref = refs[:CHUNKS], refs[CHUNKS]
    for k, ref in enumerate(chunks):

        @pl.when(pl.program_id(0) // PER == k)
        def _():
            o_ref[...] = (own_ref[...].astype(F32) + ref[...].astype(F32)).astype(BF16)


def pair(own, chunks):
    return pl.pallas_call(
        pair_kernel,
        grid=(HALF // STEP,),
        in_specs=[strip(STEP)] + chunk_strips(),
        out_specs=strip(STEP),
        out_shape=pltpu.HBM((ROWS, HALF), BF16),
        compiler_params=params(60 * 1024 * 1024),
        cost_estimate=pl.CostEstimate(flops=ROWS * HALF, bytes_accessed=6 * ROWS * HALF, transcendentals=0),
    )(*in_hbm(own, *chunks))


def project_kernel(c_ref, q_ref, a_ref, keep_ref, give_ref, acc, a, sem):
    cuts = [slice(k * STEP, (k + 1) * STEP) for k in range(HALF // STEP)]
    stream = Stream([[(a_ref.at[:, cut], a.at[:, cut])] for cut in cuts], sem)
    for k, cut in enumerate(cuts):
        stream.get(k)
        x = jnp.dot(a[:, cut], q_ref[cut, :], preferred_element_type=F32)
        acc[...] = x if k == 0 else acc[...] + x
    c, h = c_ref[0], ROWS // 2
    keep_ref[...] = acc[pl.ds(pl.multiple_of(c * h, h), h), :]
    give_ref[...] = acc[pl.ds(pl.multiple_of((1 - c) * h, h), h), :]


def project(c, query, a):
    out = jax.ShapeDtypeStruct((ROWS // 2, RANK), F32)
    return pl.pallas_call(
        project_kernel,
        in_specs=[SMEM, VMEM, HBM],
        out_specs=[VMEM, VMEM],
        out_shape=[out, out],
        scratch_shapes=[
            pltpu.VMEM((ROWS, RANK), F32),
            pltpu.VMEM((ROWS, HALF), BF16),
            pltpu.SemaphoreType.DMA((HALF // STEP,)),
        ],
        compiler_params=params(),
        cost_estimate=pl.CostEstimate(flops=2 * ROWS * HALF * RANK, bytes_accessed=2 * ROWS * HALF + 2 * HALF * RANK, transcendentals=0),
    )(c, query, *in_hbm(a))


def gram_kernel(c_ref, mine_ref, theirs_ref, s_ref, st_ref, g_ref):
    c = c_ref[0]
    h = ROWS // 2
    x, y = mine_ref[...], theirs_ref[...]
    s_ref[:h, :] = pick(c, x, y)
    s_ref[h:, :] = pick(c, y, x)
    s = s_ref[...]
    st = s.T
    st_ref[...] = st
    r = RANK // 2
    g_ref[...] = jnp.dot(pick(c, st[:r], st[r:]), s, preferred_element_type=F32)


def gram_rows(c, mine, theirs):
    return pl.pallas_call(
        gram_kernel,
        grid=(1,),
        in_specs=[SMEM, VMEM, VMEM],
        out_specs=[pl.BlockSpec((ROWS, RANK), lambda j: (0, 0)), VMEM, VMEM],
        out_shape=[
            pltpu.HBM((ROWS, RANK), BF16),
            jax.ShapeDtypeStruct((RANK, ROWS), BF16),
            jax.ShapeDtypeStruct((RANK // 2, RANK), F32),
        ],
        compiler_params=params(),
        cost_estimate=pl.CostEstimate(flops=2 * ROWS * RANK * RANK, bytes_accessed=4 * ROWS * RANK, transcendentals=0),
    )(c, mine, theirs)


def term_kernel(st_ref, a_ref, t_ref, a, t, sem):
    cuts = [slice(k * STEP, (k + 1) * STEP) for k in range(HALF // STEP)]
    stream = Stream([[(a_ref.at[:, cut], a.at[:, cut])] for cut in cuts], sem)
    st = st_ref[...]
    wide = HALF // NZ
    per = wide // STEP
    sends = []
    for k, cut in enumerate(cuts):
        stream.get(k)
        x = jnp.dot(st, a[:, cut], preferred_element_type=F32)
        part = slice(k % per * STEP, (k % per + 1) * STEP)
        t[k // per, :, :, part] = x.astype(BF16).reshape(NM, RANK // NM, STEP)
        if k % per == per - 1:
            sends += load([(t.at[k // per], t_ref.at[k // per])], sem, len(cuts) + k // per)
    for send in sends:
        send.wait()


def term(st, a):
    return pl.pallas_call(
        term_kernel,
        in_specs=[VMEM, HBM],
        out_specs=HBM,
        out_shape=pltpu.HBM((NZ, NM, RANK // NM, HALF // NZ), BF16),
        scratch_shapes=[
            pltpu.VMEM((ROWS, HALF), BF16),
            pltpu.VMEM((NZ, NM, RANK // NM, HALF // NZ), BF16),
            pltpu.SemaphoreType.DMA((HALF // STEP + NZ,)),
        ],
        compiler_params=params(),
        cost_estimate=pl.CostEstimate(flops=2 * ROWS * HALF * RANK, bytes_accessed=2 * ROWS * HALF + 2 * HALF * RANK, transcendentals=0),
    )(st, *in_hbm(a))


def total_kernel(x_ref, o_ref, copy, sem):
    n, k = x_ref.shape[0], copy.shape[0]
    total = jnp.sum(x_ref[...].astype(F32), axis=0).astype(BF16)
    copy[...] = jnp.broadcast_to(total[None], copy.shape)
    for send in load([(copy, o_ref.at[pl.ds(i, k)]) for i in range(0, n, k)], sem):
        send.wait()


def total(pieces):
    k = 16
    return pl.pallas_call(
        total_kernel,
        in_specs=[VMEM],
        out_specs=HBM,
        out_shape=pltpu.HBM(pieces.shape, BF16),
        scratch_shapes=[
            pltpu.VMEM((k,) + pieces.shape[1:], BF16),
            pltpu.SemaphoreType.DMA((pieces.shape[0] // k,)),
        ],
        compiler_params=params(),
        cost_estimate=pl.CostEstimate(flops=pieces.size, bytes_accessed=4 * pieces.size, transcendentals=0),
    )(pieces)


def dot_hi(a, b, dims=(((1,), (0,)), ((), ()))):
    return lax.dot_general(a, b, dims, precision=lax.Precision.HIGHEST, preferred_element_type=F32)


NT_DOT = (((1,), (1,)), ((), ()))
BASE = 64


def inverse_factor(a):
    n = a.shape[0]
    if n > BASE:
        h = n // 2
        i11 = inverse_factor(a[:h, :h])
        l21 = dot_hi(a[h:, :h], i11, NT_DOT)
        i22 = inverse_factor(a[h:, h:] - dot_hi(l21, l21, NT_DOT))
        i21 = -dot_hi(i22, dot_hi(l21, i11))
        return jnp.concatenate(
            [jnp.concatenate([i11, jnp.zeros((h, h), F32)], axis=1), jnp.concatenate([i21, i22], axis=1)], axis=0
        )
    row = lax.broadcasted_iota(jnp.int32, (n, 2 * n), 0)
    lane = lax.broadcasted_iota(jnp.int32, (n, 2 * n), 1)
    x = jnp.concatenate([a, jnp.where(row == lane, 1.0, 0.0)[:, :n].astype(F32)], axis=1)
    for j in range(n - 1):
        column = jnp.broadcast_to(x[:, j : j + 1], x.shape)
        pivot = column[j : j + 1, :]
        ratio = jnp.where(row > j, column, 0.0) * (1.0 / pivot)
        x = x - ratio * x[j : j + 1, :]
    d = jnp.sum(jnp.where(row == lane, x, 0.0), axis=1, keepdims=True)
    return x[:, n:] * (1.0 / jnp.sqrt(d))


def solve_kernel(g_ref, s_ref, inv_ref, w_ref):
    inv = inverse_factor(g_ref[...])
    inv_ref[...] = inv
    basis = dot_hi(s_ref[...].astype(F32), inv, NT_DOT)
    w_ref[...] = (dot_hi(basis, inv) * 0.125).astype(BF16)


def solve(gram, summed):
    square = pl.BlockSpec((RANK, RANK), lambda j: (0, 0))
    tall = pl.BlockSpec((ROWS, RANK), lambda j: (0, 0))
    return pl.pallas_call(
        solve_kernel,
        grid=(1,),
        in_specs=[VMEM, tall],
        out_specs=[square, tall],
        out_shape=[pltpu.HBM((RANK, RANK), F32), pltpu.HBM((ROWS, RANK), BF16)],
        compiler_params=params(),
        cost_estimate=pl.CostEstimate(flops=2 * 10**10, bytes_accessed=10**6, transcendentals=0),
    )(gram, *in_hbm(summed))


def finish_kernel(c_ref, m_ref, w_ref, inv_ref, t_ref, u_ref, own_ref, *refs):
    chunks, (err_ref, f_ref, u, a, b, out, w_in, inv_in, sem) = refs[:CHUNKS], refs[CHUNKS:]
    c, m = c_ref[0], m_ref[0]
    wide = HALF // NZ
    n = HALF // STEP
    w_load, inv_load = load([(w_ref, w_in), (inv_ref, inv_in)], sem, 4 * n)
    groups = []
    for k in range(n):
        at, cut = k * STEP // wide, slice(k * STEP % wide, k * STEP % wide + STEP)
        half, part = slice(k * STEP, (k + 1) * STEP), slice(k % PER * STEP, (k % PER + 1) * STEP)
        groups.append(
            [
                (u_ref.at[at, :, :, cut], u.at[at, :, :, cut]),
                (own_ref.at[:, half], a.at[:, half]),
                (chunks[k // PER].at[:, part], b.at[:, half]),
            ]
        )
    stream = Stream(groups, sem)
    w_load.wait()
    inv_load.wait()
    w = w_in[...]
    sends = []
    for k in range(n):
        stream.get(k)
        at, cut = k * STEP // wide, slice(k * STEP % wide, k * STEP % wide + STEP)
        half = slice(k * STEP, (k + 1) * STEP)
        x = jnp.dot(w, t_ref[at, :, :, cut].reshape(RANK, STEP), preferred_element_type=F32)
        y = jnp.dot(w, u[at, :, :, cut].reshape(RANK, STEP), preferred_element_type=F32)
        x = (a[:, half].astype(F32) - x).astype(BF16)
        y = (b[:, half].astype(F32) - y).astype(BF16)
        base = 2 * k * STEP
        for s in range(STEP // SUB):
            part = slice(s * SUB, (s + 1) * SUB)
            out[:, base + s * BLK : base + s * BLK + SUB] = pick(c, x[:, part], y[:, part])
            out[:, base + s * BLK + SUB : base + (s + 1) * BLK] = pick(c, y[:, part], x[:, part])
        whole = slice(base, base + 2 * STEP)
        sends += load([(out.at[:, whole], err_ref.at[:, whole])], sem, 3 * n + k)
    per = wide // SUB
    cut = pl.ds(pl.multiple_of(m % per * SUB, SUB), SUB)
    x = t_ref[m // per, :, :, cut].reshape(RANK, SUB)
    y = u[m // per, :, :, cut].reshape(RANK, SUB)
    for k, part in enumerate((pick(c, x, y), pick(c, y, x))):
        f_ref[k * SUB : (k + 1) * SUB, :] = dot_hi(inv_in[...], part.astype(F32)).T * 0.125
    for send in sends:
        send.wait()


def finish(c, m, w, inv, own, others, t, u):
    return pl.pallas_call(
        finish_kernel,
        in_specs=[SMEM, SMEM, HBM, HBM, VMEM, HBM, HBM] + [HBM] * CHUNKS,
        out_specs=[HBM, VMEM],
        out_shape=[pltpu.HBM((ROWS, COLS), BF16), jax.ShapeDtypeStruct((BLK, RANK), F32)],
        scratch_shapes=[
            pltpu.VMEM((NZ, NM, RANK // NM, HALF // NZ), BF16),
            pltpu.VMEM((ROWS, HALF), BF16),
            pltpu.VMEM((ROWS, HALF), BF16),
            pltpu.VMEM((ROWS, COLS), BF16),
            pltpu.VMEM((ROWS, RANK), BF16),
            pltpu.VMEM((RANK, RANK), F32),
            pltpu.SemaphoreType.DMA((4 * HALF // STEP + 2,)),
        ],
        compiler_params=params(),
        cost_estimate=pl.CostEstimate(flops=2 * ROWS * COLS * RANK, bytes_accessed=4 * ROWS * COLS + 2 * COLS * RANK, transcendentals=0),
    )(c, m, *in_hbm(w, inv), t, *in_hbm(u, own, *others))


def swap(x):
    return lax.ppermute(x, "c", [(0, 1), (1, 0)])


def ring_sum(x, axis):
    x1, x2, x3 = (lax.ppermute(x, axis, [(i, (i + k) % 4) for i in range(4)]) for k in (1, 2, 3))
    return (x.astype(F32) + x2.astype(F32)) + (x1.astype(F32) + x3.astype(F32))


def join(c, mine, theirs):
    return jnp.concatenate([pick(c, mine, theirs), pick(c, theirs, mine)], axis=0)


def shards(gradient, error, query):
    gradient, error = gradient[0], error[0]
    c = lax.axis_index("c").astype(jnp.int32)
    m = (lax.axis_index("x") * 4 + lax.axis_index("y")).astype(jnp.int32)
    cv, mv = c.reshape(1), m.reshape(1)

    with jax.named_scope("query_gather"):
        part = lax.dynamic_slice_in_dim(query, c * SUB, SUB, 0)
        copies = jnp.broadcast_to(part[None], (NM, SUB, RANK))
        half_query = lax.all_to_all(copies, ("x", "y"), 0, 0, tiled=True).reshape(HALF, RANK)

    with jax.named_scope("adjust"):
        own, *others = adjust(cv, gradient, error)
        both = pair(own, [swap(other) for other in others])

    with jax.named_scope("project"):
        keep, give = project(cv, half_query, both)
        chip = (keep + swap(give)).astype(BF16)
        rows = ring_sum(chip, "z").astype(BF16)

    with jax.named_scope("gram"):
        summed, summed_t, gram_x = gram_rows(cv, rows, swap(rows))
        gram_x = ring_sum(gram_x, "x")

    with jax.named_scope("term"):
        pieces = term(summed_t, both).reshape(NZ * NM, RANK // NM, HALF // NZ)
        pieces, gram_x = lax.optimization_barrier((pieces, gram_x))
        pieces = lax.all_to_all(pieces, ("z", "x", "y"), 0, 0, tiled=True)

    with jax.named_scope("gather"):
        gram_y = ring_sum(gram_x, "y")
        pieces, gram_y = lax.optimization_barrier((pieces, gram_y))
        mine = lax.all_to_all(total(pieces), ("z", "x", "y"), 0, 0, tiled=True)

    with jax.named_scope("solve"):
        inv, w = solve(join(c, gram_y, swap(gram_y)), summed)
        mine, inv, w = lax.optimization_barrier((mine, inv, w))

    with jax.named_scope("finish"):
        mine = mine.reshape(NZ, NM, RANK // NM, HALF // NZ)
        new_error, factor = finish(cv, mv, w, inv, own, others, mine, swap(mine))
    return factor, new_error[None]


def solution(mesh):
    grid = Mesh(mesh.devices.reshape(4, 2, 4, 4), ("z", "c", "x", "y"))
    in_specs = (P(("z", "c"), ("x", "y"), None), P(("z", "c"), ("x", "y"), None), P(("x", "y"), None))
    out_specs = (P(("x", "y"), None), P(("z", "c"), ("x", "y"), None))
    return jax.shard_map(shards, mesh=grid, in_specs=in_specs, out_specs=out_specs, check_vma=False)
```

time: 485 us -> 164 us (0.34)
  waiting for transfers between devices: 362 us -> 48.9 us
  Pallas kernels: 0 us -> 68.3 us
  other arithmetic: 58.6 us -> 0.23 us
  matrix products: 42.5 us -> 0 us
  starting transfers between devices: 0.34 us -> 42.7 us
  between operations: 15.2 us -> 0.94 us
    psum x3 -> x0, waiting for transfers between devices: 304 us -> none  [the longest x1 163 us: shards(): factor_full = lax.psum(term, ('dp', 'mp')) / replicas]
    pallas_call x0 -> x8, Pallas kernels: none -> 68.3 us  [the longest x1 27.1 us: solve(): pl.pallas_call(solve_kernel, grid=(1,), in_specs=[VMEM, tall], out_specs=...]
    all_gather x1 -> x0, waiting for transfers between devices: 56.8 us -> none  [shards(): lax.all_gather(query, 'mp', axis=0, tiled=True)]
    another operation x9 -> x0, other arithmetic: 53.7 us -> none  [the longest x6 34 us: orthonormal(): lower = jnp.linalg.cholesky(gram)]
    ppermute x0 -> x17, waiting for transfers between devices: none -> 47.3 us  [the longest x9 34.7 us: ring_sum(): lax.ppermute(x, axis, [(i, (i + k) % 4) for i in range(4)])]
    dot_general x4 -> x0, matrix products: 38.7 us -> none  [the longest x1 13.2 us: shards(): lax.dot_general(adjusted, basis, contract, preferred_element_type=jnp.flo...]
    all_to_all x0 -> x3, starting transfers between devices: none -> 21.9 us  [the longest x1 8.42 us: shards(): mine = lax.all_to_all(total(pieces), ('z', 'x', 'y'), 0, 0, tiled=True)]
    ppermute x0 -> x17, starting transfers between devices: none -> 20.8 us  [the longest x9 11.4 us: ring_sum(): lax.ppermute(x, axis, [(i, (i + k) % 4) for i in range(4)])]
  transfers between devices with their start and end apart: 4 -> 20, of which waited for: 4 -> 14; matrix products, arithmetic and copies ran while one was open for 0% -> 0% of each run, Pallas kernels for 0% -> 33%
where the time goes in v2:
time: 164 us
  Pallas kernels  68.3 us (42%)
  waiting for transfers between devices  48.9 us (30%)
  starting transfers between devices  42.7 us (26%)
  local copies, waits for them, and re-layouts  2.52 us (2%)
    ppermute x9, waiting for transfers between devices, ring_sum(): lax.ppermute(x, axis, [(i, (i + k) % 4) for i in range(4)])  34.7 us
    pallas_call x1, Pallas kernels, solve(): pl.pallas_call(solve_kernel, grid=(1,), in_specs=[VMEM, tall], out_specs=...  27.1 us
    ppermute x8, waiting for transfers between devices, swap(): return lax.ppermute(x, 'c', [(0, 1), (1, 0)])  12.6 us
    pallas_call x1, Pallas kernels, adjust(): pl.pallas_call(adjust_kernel, grid=(HALF // STEP,), in_specs=[SMEM, strip...  12.5 us
    ppermute x9, starting transfers between devices, ring_sum(): lax.ppermute(x, axis, [(i, (i + k) % 4) for i in range(4)])  11.4 us
    ppermute x8, starting transfers between devices, swap(): return lax.ppermute(x, 'c', [(0, 1), (1, 0)])  9.43 us
    pallas_call x1, Pallas kernels, finish(): pl.pallas_call(finish_kernel, in_specs=[SMEM, SMEM, HBM, HBM, VMEM, HBM,...  9.05 us
    all_to_all x1, starting transfers between devices, shards(): mine = lax.all_to_all(total(pieces), ('z', 'x', 'y'), 0, 0, tiled=True)  8.42 us
  transfers between devices with their start and end apart: 20, of which 14 were waited for; matrix products, arithmetic and copies ran while one was open for 0% of the time, Pallas kernels for 33%

profile of v2, /device:TPU:1, one launch (start us, length us, event | category | flops | bytes accessed | tf_op | source)
XLA Modules:
  0.0 163.5 jit_solution(6207620749637528324)
XLA Ops:
  0.6 0.0 copy-start
  0.7 0.9 copy-done
  1.6 1.6 broadcast_in_dim.4
  3.2 7.6 %all-to-all-start = ((bf16[16,256,256]{2,1,0:T(8,128)(2,1)}), bf16[16,256,256]{2,1,0:T(8,128)(2,1)S(1)}, u32[]{:S(2)}, u32[]{:S(2)}) async-start(bf16[16,256,256]{2,1,0:T(8,128)(2,1)} %broadcast_in_dim.4), calls=%async_computation | async-start | bytes 4194304 | tf_op jit(solution)/shard_map/query_gather/all_to_all | solution.py:380
  10.8 12.5 %adjust.2 = (bf16[512,4096]{1,0:T(8,128)(2,1)}, bf16[512,1024]{1,0:T(8,128)(2,1)}, bf16[512,1024]{1,0:T(8,128)(2,1)}, bf16[512,1024]{1,0:T(8,128)(2,1)}, bf16[512,1024]{1,0:T(8,128)(2,1)}) custom-call(s32[1]{0:T(128)} %bitcast.c_ref, bf16[512,8192]{1,0:T(8,128)(2,1)} %bitcast.11, bf16[512,8192]{1,0:T(8,128)(2,1)} %bitcast.12), custom_call_target="tpu_custom_call" | custom-call | flops 4194304 | bytes 25165824 | tf_op jit(solution)/shard_map/adjust/pallas_call | solution.py:91
  23.2 1.0 collective-permute-start
  24.2 0.1 collective-permute-start.1
  24.2 0.4 collective-permute-start.2
  24.7 0.1 collective-permute-start.3
  24.8 2.6 %collective-permute-done.refs_0_ = bf16[512,1024]{1,0:T(8,128)(2,1)S(1)} collective-permute-done((bf16[512,1024]{1,0:T(8,128)(2,1)}, bf16[512,1024]{1,0:T(8,128)(2,1)S(1)}, u32[]{:S(2)}, u32[]{:S(2)}) %collective-permute-start) | collective-permute-done | bytes 1048608 | tf_op jit(solution)/shard_map/adjust/ppermute | solution.py:359
  27.4 0.0 copy-start.1
  27.4 0.9 collective-permute-done.1.refs_1_
  28.3 1.5 collective-permute-done.2.refs_2_
  29.8 1.5 collective-permute-done.3.refs_3_
  31.3 0.0 copy-done.1
  31.3 7.9 %adjust.3.a_ref = bf16[512,4096]{1,0:T(8,128)(2,1)} custom-call(bf16[512,4096]{1,0:T(8,128)(2,1)} %get-tuple-element.23.own_ref, bf16[512,1024]{1,0:T(8,128)(2,1)} %copy-done.1, bf16[512,1024]{1,0:T(8,128)(2,1)} %collective-permute-done.1.refs_1_, bf16[512,1024]{1,0:T(8,128)(2,1)} %collective-permute-done.2.refs_2_, ...), custom_call_target="tpu_custom_call" | custom-call | flops 2097152 | bytes 12582912 | tf_op jit(solution)/shard_map/adjust/pallas_call | solution.py:112
  39.2 0.0 all-to-all-done
  39.2 4.2 %project.1 = (f32[256,256]{1,0:T(8,128)S(1)}, f32[256,256]{1,0:T(8,128)S(1)}) custom-call(s32[1]{0:T(128)} %bitcast.c_ref, bf16[4096,256]{1,0:T(8,128)(2,1)S(1)} %bitcast.8, bf16[512,4096]{1,0:T(8,128)(2,1)} %adjust.3.a_ref), custom_call_target="tpu_custom_call" | custom-call | flops 1073741824 | bytes 6291456 | tf_op jit(solution)/shard_map/project/pallas_call | solution.py:137
  43.5 3.0 %collective-permute-start.4 = (f32[256,256]{1,0:T(8,128)S(1)}, f32[256,256]{1,0:T(8,128)S(1)}, u32[]{:S(2)}, u32[]{:S(2)}) collective-permute-start(f32[256,256]{1,0:T(8,128)S(1)} %get-tuple-element.29), channel_id=1, source_target_pairs={{0,16},{16,0},{1,17},{17,1},{2,18},{18,2},{3,19},{19,3},{4,20},{20... | collective-permute-start | bytes 786440 | tf_op jit(solution)/shard_map/project/ppermute | solution.py:359
  46.4 1.2 collective-permute-done.4
  47.6 3.8 %collective-permute-start.7 = (bf16[256,256]{1,0:T(8,128)(2,1)S(1)}, bf16[256,256]{1,0:T(8,128)(2,1)S(1)}, u32[]{:S(2)}, u32[]{:S(2)}) collective-permute-start(bf16[256,256]{1,0:T(8,128)(2,1)S(1)} %add_convert_fusion.1), channel_id=1, source_target_pairs={{0,96},{32,0},{64,32},{96,64},{1,97},{33,1},{65,33},{97,65},{2,98}... | collective-permute-start | bytes 393224 | tf_op jit(solution)/shard_map/project/ppermute | solution.py:363
  51.4 0.0 collective-permute-start.6
  51.4 1.3 collective-permute-start.5
  52.7 1.2 collective-permute-done.7
  53.9 6.3 %collective-permute-done.6 = bf16[256,256]{1,0:T(8,128)(2,1)S(1)} collective-permute-done((bf16[256,256]{1,0:T(8,128)(2,1)S(1)}, bf16[256,256]{1,0:T(8,128)(2,1)S(1)}, u32[]{:S(2)}, u32[]{:S(2)}) %collective-permute-start.6) | collective-permute-done | bytes 131104 | tf_op jit(solution)/shard_map/project/ppermute | solution.py:363
  60.2 0.0 collective-permute-done.5
  60.2 0.1 add_convert_fusion.mine_ref
  60.3 1.2 collective-permute-start.8
  61.5 1.0 collective-permute-done.8.theirs_ref
  62.5 0.8 gram.1
  63.4 0.3 collective-permute-start.11
  63.7 1.1 collective-permute-start.10
  64.8 0.7 collective-permute-start.9
  65.6 5.0 %term.1 = bf16[4,16,16,1024]{3,2,1,0:T(8,128)(2,1)} custom-call(bf16[256,512]{1,0:T(8,128)(2,1)S(1)} %get-tuple-element.30.st_ref, bf16[512,4096]{1,0:T(8,128)(2,1)} %adjust.3.a_ref), custom_call_target="tpu_custom_call" | custom-call | flops 1073741824 | bytes 6291456 | tf_op jit(solution)/shard_map/term/pallas_call | solution.py:200
  70.6 0.0 collective-permute-done.11
  70.6 0.0 collective-permute-done.10
  70.6 1.0 collective-permute-done.9
  71.6 5.9 %all-to-all-start.1 = ((bf16[64,16,1024]{2,1,0:T(8,128)(2,1)}), bf16[64,16,1024]{2,1,0:T(8,128)(2,1)S(1)}, u32[]{:S(2)}, u32[]{:S(2)}) async-start(bf16[64,16,1024]{2,1,0:T(8,128)(2,1)} %bitcast.13), calls=%async_computation.1 | async-start | bytes 4194304 | tf_op jit(solution)/shard_map/term/all_to_all | solution.py:398
  77.5 2.3 %collective-permute-start.14 = (f32[128,256]{1,0:T(8,128)S(1)}, f32[128,256]{1,0:T(8,128)S(1)}, u32[]{:S(2)}, u32[]{:S(2)}) collective-permute-start(f32[128,256]{1,0:T(8,128)S(1)} %add_add_fusion.1), channel_id=1, source_target_pairs={{0,3},{1,0},{2,1},{3,2},{4,7},{5,4},{6,5},{7,6},{8,11},{9,8},{10,9... | collective-permute-start | bytes 393224 | tf_op jit(solution)/shard_map/gather/ppermute | solution.py:363
  79.8 0.0 collective-permute-start.13
  79.8 1.8 %collective-permute-start.12 = (f32[128,256]{1,0:T(8,128)S(1)}, f32[128,256]{1,0:T(8,128)S(1)}, u32[]{:S(2)}, u32[]{:S(2)}) collective-permute-start(f32[128,256]{1,0:T(8,128)S(1)} %add_add_fusion.1), channel_id=1, source_target_pairs={{0,2},{1,3},{2,0},{3,1},{4,6},{5,7},{6,4},{7,5},{8,10},{9,11},{10,... | collective-permute-start | bytes 393224 | tf_op jit(solution)/shard_map/gather/ppermute | solution.py:363
  81.6 18.5 %collective-permute-done.14 = f32[128,256]{1,0:T(8,128)S(1)} collective-permute-done((f32[128,256]{1,0:T(8,128)S(1)}, f32[128,256]{1,0:T(8,128)S(1)}, u32[]{:S(2)}, u32[]{:S(2)}) %collective-permute-start.14) | collective-permute-done | bytes 131104 | tf_op jit(solution)/shard_map/gather/ppermute | solution.py:363
  100.0 1.4 collective-permute-done.13
  101.5 6.3 %collective-permute-done.12 = f32[128,256]{1,0:T(8,128)S(1)} collective-permute-done((f32[128,256]{1,0:T(8,128)S(1)}, f32[128,256]{1,0:T(8,128)S(1)}, u32[]{:S(2)}, u32[]{:S(2)}) %collective-permute-start.12) | collective-permute-done | bytes 131104 | tf_op jit(solution)/shard_map/gather/ppermute | solution.py:363
  107.7 0.0 all-to-all-done.1.x_ref
  107.8 2.0 %collective-permute-start.15 = (f32[128,256]{1,0:T(8,128)S(1)}, f32[128,256]{1,0:T(8,128)S(1)}, u32[]{:S(2)}, u32[]{:S(2)}) collective-permute-start(f32[128,256]{1,0:T(8,128)S(1)} %add_add_fusion), channel_id=1, source_target_pairs={{0,16},{16,0},{1,17},{17,1},{2,18},{18,2},{3,19},{19,3},{4,20},{20... | collective-permute-start | bytes 393224 | tf_op jit(solution)/shard_map/solve/ppermute | solution.py:359
  109.7 1.7 %gather.1 = bf16[64,16,1024]{2,1,0:T(8,128)(2,1)} custom-call(bf16[64,16,1024]{2,1,0:T(8,128)(2,1)S(1)} %all-to-all-done.1.x_ref), custom_call_target="tpu_custom_call" | custom-call | flops 1048576 | bytes 4194304 | tf_op jit(solution)/shard_map/gather/pallas_call | solution.py:225
  111.4 8.4 %all-to-all-start.2 = ((bf16[64,16,1024]{2,1,0:T(8,128)(2,1)}), bf16[64,16,1024]{2,1,0:T(8,128)(2,1)S(1)}, u32[]{:S(2)}, u32[]{:S(2)}) async-start(bf16[64,16,1024]{2,1,0:T(8,128)(2,1)} %gather.1), calls=%async_computation.2 | async-start | bytes 4194304 | tf_op jit(solution)/shard_map/gather/all_to_all | solution.py:403
  119.8 0.0 collective-permute-done.15
  119.9 27.1 %solve.1 = (f32[256,256]{1,0:T(8,128)}, bf16[512,256]{1,0:T(8,128)(2,1)}) custom-call(f32[256,256]{1,0:T(8,128)S(1)} %pad_maximum_fusion.g_ref, bf16[512,256]{1,0:T(8,128)(2,1)} %get-tuple-element.36.s_ref), custom_call_target="tpu_custom_call" | custom-call | flops 20000000000 | bytes 1000000 | tf_op jit(solution)/shard_map/solve/pallas_call | solution.py:280
  147.0 1.6 all-to-all-done.2
  148.6 1.8 %collective-permute-start.16 = (bf16[4,16,16,1024]{3,2,1,0:T(8,128)(2,1)S(1)}, bf16[4,16,16,1024]{3,2,1,0:T(8,128)(2,1)}, u32[]{:S(2)}, u32[]{:S(2)}) collective-permute-start(bf16[4,16,16,1024]{3,2,1,0:T(8,128)(2,1)S(1)} %bitcast.9), channel_id=1, source_target_pairs={{0,16},{16,0},{1,17},{17,1},{2,18},{18,2},{3,19},{19,3},{4,20},{20... | collective-permute-start | bytes 6291464 | tf_op jit(solution)/shard_map/finish/ppermute | solution.py:359
  150.4 3.9 %collective-permute-done.16.u_ref = bf16[4,16,16,1024]{3,2,1,0:T(8,128)(2,1)} collective-permute-done((bf16[4,16,16,1024]{3,2,1,0:T(8,128)(2,1)S(1)}, bf16[4,16,16,1024]{3,2,1,0:T(8,128)(2,1)}, u32[]{:S(2)}, u32[]{:S(2)}) %collective-permute-start.16) | collective-permute-done | bytes 2097184 | tf_op jit(solution)/shard_map/finish/ppermute | solution.py:359
  154.3 9.1 %finish.1 = (bf16[512,8192]{1,0:T(8,128)(2,1)}, f32[512,256]{1,0:T(8,128)}) custom-call(s32[1]{0:T(128)} %bitcast.c_ref, s32[1]{0:T(128)} %bitcast.1.m_ref, bf16[512,256]{1,0:T(8,128)(2,1)} %get-tuple-element.39.w_ref, f32[256,256]{1,0:T(8,128)} %get-tuple-element.40.inv_ref, bf16[4,16,16,1024]{3,2,1,0:T(8,128)(2,1)S(1)} %bitcast.10, ...), custom_call_target="tpu_custom_call" | custom-call | flops 2147483648 | bytes 20971520 | tf_op jit(solution)/shard_map/finish/pallas_call | solution.py:339
  (6 shorter events, 0.2 us)
Async XLA Ops:
  0.6 1.0 copy-start
  3.2 36.1 %all-to-all-start = ((bf16[16,256,256]{2,1,0:T(8,128)(2,1)}), bf16[16,256,256]{2,1,0:T(8,128)(2,1)S(1)}, u32[]{:S(2)}, u32[]{:S(2)}) async-start(bf16[16,256,256]{2,1,0:T(8,128)(2,1)} %broadcast_in_dim.4), calls=%async_computation | async-start | bytes 4194304 | tf_op jit(solution)/shard_map/query_gather/all_to_all | solution.py:380
  23.2 4.2 %collective-permute-start = (bf16[512,1024]{1,0:T(8,128)(2,1)}, bf16[512,1024]{1,0:T(8,128)(2,1)S(1)}, u32[]{:S(2)}, u32[]{:S(2)}) collective-permute-start(bf16[512,1024]{1,0:T(8,128)(2,1)} %get-tuple-element.24.refs_0_), channel_id=1, source_target_pairs={{0,16},{16,0},{1,17},{17,1},{2,18},{18,2},{3,19},{19,3},{4,20},{20... | collective-permute-start | bytes 3145736 | tf_op jit(solution)/shard_map/adjust/ppermute | solution.py:359
  24.2 4.1 %collective-permute-start.1 = (bf16[512,1024]{1,0:T(8,128)(2,1)}, bf16[512,1024]{1,0:T(8,128)(2,1)}, u32[]{:S(2)}, u32[]{:S(2)}) collective-permute-start(bf16[512,1024]{1,0:T(8,128)(2,1)} %get-tuple-element.25.refs_1_), channel_id=1, source_target_pairs={{0,16},{16,0},{1,17},{17,1},{2,18},{18,2},{3,19},{19,3},{4,20},{20... | collective-permute-start | bytes 3145736 | tf_op jit(solution)/shard_map/adjust/ppermute | solution.py:359
  24.2 5.6 %collective-permute-start.2 = (bf16[512,1024]{1,0:T(8,128)(2,1)}, bf16[512,1024]{1,0:T(8,128)(2,1)}, u32[]{:S(2)}, u32[]{:S(2)}) collective-permute-start(bf16[512,1024]{1,0:T(8,128)(2,1)} %get-tuple-element.26.refs_2_), channel_id=1, source_target_pairs={{0,16},{16,0},{1,17},{17,1},{2,18},{18,2},{3,19},{19,3},{4,20},{20... | collective-permute-start | bytes 3145736 | tf_op jit(solution)/shard_map/adjust/ppermute | solution.py:359
  24.7 6.6 %collective-permute-start.3 = (bf16[512,1024]{1,0:T(8,128)(2,1)}, bf16[512,1024]{1,0:T(8,128)(2,1)}, u32[]{:S(2)}, u32[]{:S(2)}) collective-permute-start(bf16[512,1024]{1,0:T(8,128)(2,1)} %get-tuple-element.27.refs_3_), channel_id=1, source_target_pairs={{0,16},{16,0},{1,17},{17,1},{2,18},{18,2},{3,19},{19,3},{4,20},{20... | collective-permute-start | bytes 3145736 | tf_op jit(solution)/shard_map/adjust/ppermute | solution.py:359
  27.4 3.9 %copy-start.1 = (bf16[512,1024]{1,0:T(8,128)(2,1)}, bf16[512,1024]{1,0:T(8,128)(2,1)S(1)}, u32[]{:S(2)}) copy-start(bf16[512,1024]{1,0:T(8,128)(2,1)S(1)} %collective-permute-done.refs_0_) | copy-start | bytes 3145732
  43.5 4.1 %collective-permute-start.4 = (f32[256,256]{1,0:T(8,128)S(1)}, f32[256,256]{1,0:T(8,128)S(1)}, u32[]{:S(2)}, u32[]{:S(2)}) collective-permute-start(f32[256,256]{1,0:T(8,128)S(1)} %get-tuple-element.29), channel_id=1, source_target_pairs={{0,16},{16,0},{1,17},{17,1},{2,18},{18,2},{3,19},{19,3},{4,20},{20... | collective-permute-start | bytes 786440 | tf_op jit(solution)/shard_map/project/ppermute | solution.py:359
  47.6 6.3 %collective-permute-start.7 = (bf16[256,256]{1,0:T(8,128)(2,1)S(1)}, bf16[256,256]{1,0:T(8,128)(2,1)S(1)}, u32[]{:S(2)}, u32[]{:S(2)}) collective-permute-start(bf16[256,256]{1,0:T(8,128)(2,1)S(1)} %add_convert_fusion.1), channel_id=1, source_target_pairs={{0,96},{32,0},{64,32},{96,64},{1,97},{33,1},{65,33},{97,65},{2,98}... | collective-permute-start | bytes 393224 | tf_op jit(solution)/shard_map/project/ppermute | solution.py:363
  51.4 8.8 %collective-permute-start.6 = (bf16[256,256]{1,0:T(8,128)(2,1)S(1)}, bf16[256,256]{1,0:T(8,128)(2,1)S(1)}, u32[]{:S(2)}, u32[]{:S(2)}) collective-permute-start(bf16[256,256]{1,0:T(8,128)(2,1)S(1)} %add_convert_fusion.1), channel_id=1, source_target_pairs={{0,32},{32,64},{64,96},{96,0},{1,33},{33,65},{65,97},{97,1},{2,34}... | collective-permute-start | bytes 393224 | tf_op jit(solution)/shard_map/project/ppermute | solution.py:363
  51.4 8.8 %collective-permute-start.5 = (bf16[256,256]{1,0:T(8,128)(2,1)S(1)}, bf16[256,256]{1,0:T(8,128)(2,1)S(1)}, u32[]{:S(2)}, u32[]{:S(2)}) collective-permute-start(bf16[256,256]{1,0:T(8,128)(2,1)S(1)} %add_convert_fusion.1), channel_id=1, source_target_pairs={{0,64},{32,96},{64,0},{96,32},{1,65},{33,97},{65,1},{97,33},{2,66}... | collective-permute-start | bytes 393224 | tf_op jit(solution)/shard_map/project/ppermute | solution.py:363
  60.3 2.2 %collective-permute-start.8 = (bf16[256,256]{1,0:T(8,128)(2,1)S(1)}, bf16[256,256]{1,0:T(8,128)(2,1)S(1)}, u32[]{:S(2)}, u32[]{:S(2)}) collective-permute-start(bf16[256,256]{1,0:T(8,128)(2,1)S(1)} %add_convert_fusion.mine_ref), channel_id=1, source_target_pairs={{0,16},{16,0},{1,17},{17,1},{2,18},{18,2},{3,19},{19,3},{4,20},{20... | collective-permute-start | bytes 393224 | tf_op jit(solution)/shard_map/gram/ppermute | solution.py:359
  63.4 7.2 %collective-permute-start.11 = (f32[128,256]{1,0:T(8,128)S(1)}, f32[128,256]{1,0:T(8,128)S(1)}, u32[]{:S(2)}, u32[]{:S(2)}) collective-permute-start(f32[128,256]{1,0:T(8,128)S(1)} %get-tuple-element.31), channel_id=1, source_target_pairs={{0,12},{4,0},{8,4},{12,8},{1,13},{5,1},{9,5},{13,9},{2,14},{6,2},{... | collective-permute-start | bytes 393224 | tf_op jit(solution)/shard_map/gram/ppermute | solution.py:363
  63.7 6.9 %collective-permute-start.10 = (f32[128,256]{1,0:T(8,128)S(1)}, f32[128,256]{1,0:T(8,128)S(1)}, u32[]{:S(2)}, u32[]{:S(2)}) collective-permute-start(f32[128,256]{1,0:T(8,128)S(1)} %get-tuple-element.31), channel_id=1, source_target_pairs={{0,4},{4,8},{8,12},{12,0},{1,5},{5,9},{9,13},{13,1},{2,6},{6,10},{... | collective-permute-start | bytes 393224 | tf_op jit(solution)/shard_map/gram/ppermute | solution.py:363
  64.8 6.8 %collective-permute-start.9 = (f32[128,256]{1,0:T(8,128)S(1)}, f32[128,256]{1,0:T(8,128)S(1)}, u32[]{:S(2)}, u32[]{:S(2)}) collective-permute-start(f32[128,256]{1,0:T(8,128)S(1)} %get-tuple-element.31), channel_id=1, source_target_pairs={{0,8},{4,12},{8,0},{12,4},{1,9},{5,13},{9,1},{13,5},{2,10},{6,14},... | collective-permute-start | bytes 393224 | tf_op jit(solution)/shard_map/gram/ppermute | solution.py:363
  71.6 36.1 %all-to-all-start.1 = ((bf16[64,16,1024]{2,1,0:T(8,128)(2,1)}), bf16[64,16,1024]{2,1,0:T(8,128)(2,1)S(1)}, u32[]{:S(2)}, u32[]{:S(2)}) async-start(bf16[64,16,1024]{2,1,0:T(8,128)(2,1)} %bitcast.13), calls=%async_computation.1 | async-start | bytes 4194304 | tf_op jit(solution)/shard_map/term/all_to_all | solution.py:398
  77.5 22.5 %collective-permute-start.14 = (f32[128,256]{1,0:T(8,128)S(1)}, f32[128,256]{1,0:T(8,128)S(1)}, u32[]{:S(2)}, u32[]{:S(2)}) collective-permute-start(f32[128,256]{1,0:T(8,128)S(1)} %add_add_fusion.1), channel_id=1, source_target_pairs={{0,3},{1,0},{2,1},{3,2},{4,7},{5,4},{6,5},{7,6},{8,11},{9,8},{10,9... | collective-permute-start | bytes 393224 | tf_op jit(solution)/shard_map/gather/ppermute | solution.py:363
  79.8 21.7 %collective-permute-start.13 = (f32[128,256]{1,0:T(8,128)S(1)}, f32[128,256]{1,0:T(8,128)S(1)}, u32[]{:S(2)}, u32[]{:S(2)}) collective-permute-start(f32[128,256]{1,0:T(8,128)S(1)} %add_add_fusion.1), channel_id=1, source_target_pairs={{0,1},{1,2},{2,3},{3,0},{4,5},{5,6},{6,7},{7,4},{8,9},{9,10},{10,1... | collective-permute-start | bytes 393224 | tf_op jit(solution)/shard_map/gather/ppermute | solution.py:363
  79.8 27.9 %collective-permute-start.12 = (f32[128,256]{1,0:T(8,128)S(1)}, f32[128,256]{1,0:T(8,128)S(1)}, u32[]{:S(2)}, u32[]{:S(2)}) collective-permute-start(f32[128,256]{1,0:T(8,128)S(1)} %add_add_fusion.1), channel_id=1, source_target_pairs={{0,2},{1,3},{2,0},{3,1},{4,6},{5,7},{6,4},{7,5},{8,10},{9,11},{10,... | collective-permute-start | bytes 393224 | tf_op jit(solution)/shard_map/gather/ppermute | solution.py:363
  107.8 12.1 %collective-permute-start.15 = (f32[128,256]{1,0:T(8,128)S(1)}, f32[128,256]{1,0:T(8,128)S(1)}, u32[]{:S(2)}, u32[]{:S(2)}) collective-permute-start(f32[128,256]{1,0:T(8,128)S(1)} %add_add_fusion), channel_id=1, source_target_pairs={{0,16},{16,0},{1,17},{17,1},{2,18},{18,2},{3,19},{19,3},{4,20},{20... | collective-permute-start | bytes 393224 | tf_op jit(solution)/shard_map/solve/ppermute | solution.py:359
  111.4 37.2 %all-to-all-start.2 = ((bf16[64,16,1024]{2,1,0:T(8,128)(2,1)}), bf16[64,16,1024]{2,1,0:T(8,128)(2,1)S(1)}, u32[]{:S(2)}, u32[]{:S(2)}) async-start(bf16[64,16,1024]{2,1,0:T(8,128)(2,1)} %gather.1), calls=%async_computation.2 | async-start | bytes 4194304 | tf_op jit(solution)/shard_map/gather/all_to_all | solution.py:403
  148.6 5.7 %collective-permute-start.16 = (bf16[4,16,16,1024]{3,2,1,0:T(8,128)(2,1)S(1)}, bf16[4,16,16,1024]{3,2,1,0:T(8,128)(2,1)}, u32[]{:S(2)}, u32[]{:S(2)}) collective-permute-start(bf16[4,16,16,1024]{3,2,1,0:T(8,128)(2,1)S(1)} %bitcast.9), channel_id=1, source_target_pairs={{0,16},{16,0},{1,17},{17,1},{2,18},{18,2},{3,19},{19,3},{4,20},{20... | collective-permute-start | bytes 6291464 | tf_op jit(solution)/shard_map/finish/ppermute | solution.py:359

commit v3 on v2

--- a/solution.py
+++ b/solution.py
@@ -1,3 +1,5 @@
+import functools
+
 import jax
 import jax.numpy as jnp
 from jax import lax
@@ -17,17 +19,16 @@
 
 SMEM = pl.BlockSpec(memory_space=pltpu.SMEM)
 VMEM = pl.BlockSpec(memory_space=pltpu.VMEM)
+HBM = pl.BlockSpec(memory_space=pltpu.HBM)
 CHUNKS = 4
 CHUNK = HALF // CHUNKS
-STEP = 512
-PER = CHUNK // STEP
+STEP = CHUNK // 2
+STEPS = HALF // STEP
+GROUP = RANK // NM
 
 
 def params(limit=VMEM_LIMIT):
     return pltpu.CompilerParams(vmem_limit_bytes=limit)
-
-
-HBM = pl.BlockSpec(memory_space=pltpu.HBM)
 
 
 def in_hbm(*arrays):
@@ -42,7 +43,7 @@
 
 
 class Stream:
-    DEPTH = 3
+    DEPTH = 4
 
     def __init__(self, groups, sem):
         self.groups, self.sem, self.started = groups, sem, []
@@ -60,68 +61,74 @@
         self.more()
 
 
-def strip(width):
-    return pl.BlockSpec((ROWS, width), lambda j: (0, j))
-
-
-def chunk_strips():
-    return [pl.BlockSpec((ROWS, STEP), lambda j, k=k: (0, jnp.clip(j - k * PER, 0, PER - 1))) for k in range(CHUNKS)]
-
-
 def pick(c, first, second):
     return jnp.where(c == 0, first, second)
 
 
-def adjust_kernel(c_ref, g_ref, e_ref, own_ref, *other_refs):
-    c, step = c_ref[0], pl.program_id(0)
-    a = (g_ref[...].astype(F32) + e_ref[...].astype(F32)).astype(BF16)
-    for s in range(STEP // SUB):
-        lo = a[:, s * BLK : s * BLK + SUB]
-        hi = a[:, s * BLK + SUB : (s + 1) * BLK]
-        own_ref[:, s * SUB : (s + 1) * SUB] = pick(c, lo, hi)
-        other = pick(c, hi, lo)
-        for k, ref in enumerate(other_refs):
-
-            @pl.when(step // PER == k)
-            def _():
-                ref[:, s * SUB : (s + 1) * SUB] = other
+def adjust_kernel(c_ref, g_ref, d_ref, own_ref, *refs):
+    chunks, (g, d, own, other, sem) = refs[:CHUNKS], refs[CHUNKS:]
+    wide = [slice(2 * k * STEP, 2 * (k + 1) * STEP) for k in range(STEPS)]
+    stream = Stream([[(g_ref.at[:, cut], g.at[k]), (d_ref.at[:, cut], d.at[k])] for k, cut in enumerate(wide)], sem)
+    c = c_ref[0]
+    sends = []
+    for k in range(STEPS):
+        stream.get(k)
+        for s in range(STEP // SUB):
+            part = slice(s * SUB, (s + 1) * SUB)
+            for out, core in ((own, c), (other, 1 - c)):
+                cut = pl.ds(pl.multiple_of(s * BLK + core * SUB, SUB), SUB)
+                out[k, :, part] = (g[k, :, cut].astype(F32) + d[k, :, cut].astype(F32)).astype(BF16)
+        cut = slice(k * STEP, (k + 1) * STEP)
+        part = slice(k % 2 * STEP, (k % 2 + 1) * STEP)
+        pairs = [(own.at[k], own_ref.at[:, cut]), (other.at[k], chunks[k // 2].at[:, part])]
+        sends += load(pairs, sem, 2 * STEPS + 2 * k)
+    for send in sends:
+        send.wait()
 
 
 def adjust(c, gradient, error):
     return pl.pallas_call(
         adjust_kernel,
-        grid=(HALF // STEP,),
-        in_specs=[SMEM, strip(2 * STEP), strip(2 * STEP)],
-        out_specs=[strip(STEP)] + chunk_strips(),
+        in_specs=[SMEM, HBM, HBM],
+        out_specs=[HBM] * (1 + CHUNKS),
         out_shape=[pltpu.HBM((ROWS, HALF), BF16)] + [pltpu.HBM((ROWS, CHUNK), BF16)] * CHUNKS,
-        compiler_params=params(60 * 1024 * 1024),
+        scratch_shapes=[pltpu.VMEM((STEPS, ROWS, 2 * STEP), BF16)] * 2
+        + [pltpu.VMEM((STEPS, ROWS, STEP), BF16)] * 2
+        + [pltpu.SemaphoreType.DMA((4 * STEPS,))],
+        compiler_params=params(),
         cost_estimate=pl.CostEstimate(flops=ROWS * COLS, bytes_accessed=6 * ROWS * COLS, transcendentals=0),
-    )(c, gradient, error)
+    )(c, *in_hbm(gradient, error))
 
 
 def pair_kernel(own_ref, *refs):
-    chunks, o_ref = refs[:CHUNKS], refs[CHUNKS]
-    for k, ref in enumerate(chunks):
-
-        @pl.when(pl.program_id(0) // PER == k)
-        def _():
-            o_ref[...] = (own_ref[...].astype(F32) + ref[...].astype(F32)).astype(BF16)
+    chunks, (o_ref, a, b, sem) = refs[:CHUNKS], refs[CHUNKS:]
+    cuts = [slice(k * STEP, (k + 1) * STEP) for k in range(STEPS)]
+    parts = [slice(k % 2 * STEP, (k % 2 + 1) * STEP) for k in range(STEPS)]
+    groups = [[(own_ref.at[:, cuts[k]], a.at[k]), (chunks[k // 2].at[:, parts[k]], b.at[k])] for k in range(STEPS)]
+    stream = Stream(groups, sem)
+    sends = []
+    for k, cut in enumerate(cuts):
+        stream.get(k)
+        a[k] = (a[k].astype(F32) + b[k].astype(F32)).astype(BF16)
+        sends += load([(a.at[k], o_ref.at[:, cut])], sem, 2 * STEPS + k)
+    for send in sends:
+        send.wait()
 
 
 def pair(own, chunks):
     return pl.pallas_call(
         pair_kernel,
-        grid=(HALF // STEP,),
-        in_specs=[strip(STEP)] + chunk_strips(),
-        out_specs=strip(STEP),
+        in_specs=[HBM] * (1 + CHUNKS),
+        out_specs=HBM,
         out_shape=pltpu.HBM((ROWS, HALF), BF16),
-        compiler_params=params(60 * 1024 * 1024),
+        scratch_shapes=[pltpu.VMEM((STEPS, ROWS, STEP), BF16)] * 2 + [pltpu.SemaphoreType.DMA((3 * STEPS,))],
+        compiler_params=params(),
         cost_estimate=pl.CostEstimate(flops=ROWS * HALF, bytes_accessed=6 * ROWS * HALF, transcendentals=0),
     )(*in_hbm(own, *chunks))
 
 
 def project_kernel(c_ref, q_ref, a_ref, keep_ref, give_ref, acc, a, sem):
-    cuts = [slice(k * STEP, (k + 1) * STEP) for k in range(HALF // STEP)]
+    cuts = [slice(k * CHUNK, (k + 1) * CHUNK) for k in range(CHUNKS)]
     stream = Stream([[(a_ref.at[:, cut], a.at[:, cut])] for cut in cuts], sem)
     for k, cut in enumerate(cuts):
         stream.get(k)
@@ -142,7 +149,7 @@
         scratch_shapes=[
             pltpu.VMEM((ROWS, RANK), F32),
             pltpu.VMEM((ROWS, HALF), BF16),
-            pltpu.SemaphoreType.DMA((HALF // STEP,)),
+            pltpu.SemaphoreType.DMA((CHUNKS,)),
         ],
         compiler_params=params(),
         cost_estimate=pl.CostEstimate(flops=2 * ROWS * HALF * RANK, bytes_accessed=2 * ROWS * HALF + 2 * HALF * RANK, transcendentals=0),
@@ -159,7 +166,7 @@
     st = s.T
     st_ref[...] = st
     r = RANK // 2
-    g_ref[...] = jnp.dot(pick(c, st[:r], st[r:]), s, preferred_element_type=F32)
+    g_ref[...] = jnp.dot(pick(c, st[:r], st[r:]), s, preferred_element_type=F32).astype(BF16)
 
 
 def gram_rows(c, mine, theirs):
@@ -171,7 +178,7 @@
         out_shape=[
             pltpu.HBM((ROWS, RANK), BF16),
             jax.ShapeDtypeStruct((RANK, ROWS), BF16),
-            jax.ShapeDtypeStruct((RANK // 2, RANK), F32),
+            jax.ShapeDtypeStruct((RANK // 2, RANK), BF16),
         ],
         compiler_params=params(),
         cost_estimate=pl.CostEstimate(flops=2 * ROWS * RANK * RANK, bytes_accessed=4 * ROWS * RANK, transcendentals=0),
@@ -179,19 +186,15 @@
 
 
 def term_kernel(st_ref, a_ref, t_ref, a, t, sem):
-    cuts = [slice(k * STEP, (k + 1) * STEP) for k in range(HALF // STEP)]
-    stream = Stream([[(a_ref.at[:, cut], a.at[:, cut])] for cut in cuts], sem)
+    cuts = [slice(k * CHUNK, (k + 1) * CHUNK) for k in range(CHUNKS)]
+    stream = Stream([[(a_ref.at[:, cut], a.at[k])] for k, cut in enumerate(cuts)], sem)
     st = st_ref[...]
-    wide = HALF // NZ
-    per = wide // STEP
     sends = []
-    for k, cut in enumerate(cuts):
+    for k in range(CHUNKS):
         stream.get(k)
-        x = jnp.dot(st, a[:, cut], preferred_element_type=F32)
-        part = slice(k % per * STEP, (k % per + 1) * STEP)
-        t[k // per, :, :, part] = x.astype(BF16).reshape(NM, RANK // NM, STEP)
-        if k % per == per - 1:
-            sends += load([(t.at[k // per], t_ref.at[k // per])], sem, len(cuts) + k // per)
+        x = jnp.dot(st, a[k], preferred_element_type=F32)
+        t[k] = x.astype(BF16).reshape(NM, GROUP, CHUNK)
+        sends += load([(t.at[k], t_ref.at[k])], sem, CHUNKS + k)
     for send in sends:
         send.wait()
 
@@ -201,11 +204,11 @@
         term_kernel,
         in_specs=[VMEM, HBM],
         out_specs=HBM,
-        out_shape=pltpu.HBM((NZ, NM, RANK // NM, HALF // NZ), BF16),
+        out_shape=pltpu.HBM((NZ, NM, GROUP, CHUNK), BF16),
         scratch_shapes=[
-            pltpu.VMEM((ROWS, HALF), BF16),
-            pltpu.VMEM((NZ, NM, RANK // NM, HALF // NZ), BF16),
-            pltpu.SemaphoreType.DMA((HALF // STEP + NZ,)),
+            pltpu.VMEM((CHUNKS, ROWS, CHUNK), BF16),
+            pltpu.VMEM((NZ, NM, GROUP, CHUNK), BF16),
+            pltpu.SemaphoreType.DMA((2 * CHUNKS,)),
         ],
         compiler_params=params(),
         cost_estimate=pl.CostEstimate(flops=2 * ROWS * HALF * RANK, bytes_accessed=2 * ROWS * HALF + 2 * HALF * RANK, transcendentals=0),
@@ -288,71 +291,59 @@
     )(gram, *in_hbm(summed))
 
 
-def finish_kernel(c_ref, m_ref, w_ref, inv_ref, t_ref, u_ref, own_ref, *refs):
-    chunks, (err_ref, f_ref, u, a, b, out, w_in, inv_in, sem) = refs[:CHUNKS], refs[CHUNKS:]
-    c, m = c_ref[0], m_ref[0]
-    wide = HALF // NZ
-    n = HALF // STEP
-    w_load, inv_load = load([(w_ref, w_in), (inv_ref, inv_in)], sem, 4 * n)
-    groups = []
-    for k in range(n):
-        at, cut = k * STEP // wide, slice(k * STEP % wide, k * STEP % wide + STEP)
-        half, part = slice(k * STEP, (k + 1) * STEP), slice(k % PER * STEP, (k % PER + 1) * STEP)
-        groups.append(
-            [
-                (u_ref.at[at, :, :, cut], u.at[at, :, :, cut]),
-                (own_ref.at[:, half], a.at[:, half]),
-                (chunks[k // PER].at[:, part], b.at[:, half]),
-            ]
-        )
-    stream = Stream(groups, sem)
-    w_load.wait()
-    inv_load.wait()
+def finish_kernel(held, s_ref, w_ref, inv_ref, t_ref, *refs):
+    ins, (err_ref, f_ref, t, a, out, f, w_in, inv_in, sem) = refs[:-9], refs[-9:]
+    core, m = s_ref[0], s_ref[1]
+    t = t_ref if held else t
+    if ins[0].shape[1] == HALF:
+        parts = [ins[0].at[:, k * CHUNK : (k + 1) * CHUNK] for k in range(CHUNKS)]
+    else:
+        parts = ins[:CHUNKS]
+    first = load([(w_ref, w_in)], sem)
+    groups = [[(parts[k], a.at[k])] for k in range(CHUNKS)]
+    if t is not t_ref:
+        groups = [[(t_ref.at[k], t.at[k])] + group for k, group in enumerate(groups)]
+    stream = Stream(groups, sem.at[pl.ds(2, 2 * CHUNKS)])
+    first += load([(inv_ref, inv_in)], sem, 1)
+    first[0].wait()
     w = w_in[...]
-    sends = []
-    for k in range(n):
+    sends, at = [], 2 + 2 * CHUNKS
+    for k in range(CHUNKS):
         stream.get(k)
-        at, cut = k * STEP // wide, slice(k * STEP % wide, k * STEP % wide + STEP)
-        half = slice(k * STEP, (k + 1) * STEP)
-        x = jnp.dot(w, t_ref[at, :, :, cut].reshape(RANK, STEP), preferred_element_type=F32)
-        y = jnp.dot(w, u[at, :, :, cut].reshape(RANK, STEP), preferred_element_type=F32)
-        x = (a[:, half].astype(F32) - x).astype(BF16)
-        y = (b[:, half].astype(F32) - y).astype(BF16)
-        base = 2 * k * STEP
-        for s in range(STEP // SUB):
-            part = slice(s * SUB, (s + 1) * SUB)
-            out[:, base + s * BLK : base + s * BLK + SUB] = pick(c, x[:, part], y[:, part])
-            out[:, base + s * BLK + SUB : base + (s + 1) * BLK] = pick(c, y[:, part], x[:, part])
-        whole = slice(base, base + 2 * STEP)
-        sends += load([(out.at[:, whole], err_ref.at[:, whole])], sem, 3 * n + k)
-    per = wide // SUB
-    cut = pl.ds(pl.multiple_of(m % per * SUB, SUB), SUB)
-    x = t_ref[m // per, :, :, cut].reshape(RANK, SUB)
-    y = u[m // per, :, :, cut].reshape(RANK, SUB)
-    for k, part in enumerate((pick(c, x, y), pick(c, y, x))):
-        f_ref[k * SUB : (k + 1) * SUB, :] = dot_hi(inv_in[...], part.astype(F32)).T * 0.125
+        x = jnp.dot(w, t[k].reshape(RANK, CHUNK), preferred_element_type=F32)
+        out[k] = (a[k].astype(F32) - x).astype(BF16)
+        for s in range(CHUNK // SUB):
+            to = pl.ds(pl.multiple_of((k * (CHUNK // SUB) + s) * BLK + core * SUB, SUB), SUB)
+            sends += load([(out.at[k, :, s * SUB : (s + 1) * SUB], err_ref.at[:, to])], sem, at + len(sends))
+    first[1].wait()
+    per = CHUNK // SUB
+    x = t[m // per, :, :, pl.ds(pl.multiple_of(m % per * SUB, SUB), SUB)].reshape(RANK, SUB)
+    f[...] = dot_hi(inv_in[...], x.astype(F32)).T * 0.125
+    sends += load([(f, f_ref.at[pl.ds(pl.multiple_of(core * SUB, SUB), SUB)])], sem, at + len(sends))
     for send in sends:
         send.wait()
 
 
-def finish(c, m, w, inv, own, others, t, u):
-    return pl.pallas_call(
-        finish_kernel,
-        in_specs=[SMEM, SMEM, HBM, HBM, VMEM, HBM, HBM] + [HBM] * CHUNKS,
-        out_specs=[HBM, VMEM],
-        out_shape=[pltpu.HBM((ROWS, COLS), BF16), jax.ShapeDtypeStruct((BLK, RANK), F32)],
+def finish(held, where, w, inv, t, parts, before=()):
+    n = 4 + len(parts)
+    return pl.pallas_call(
+        functools.partial(finish_kernel, held),
+        in_specs=[SMEM, HBM, HBM, VMEM if held else HBM] + [HBM] * (len(parts) + len(before)),
+        out_specs=[HBM, HBM],
+        out_shape=[pltpu.HBM((ROWS, COLS), BF16), pltpu.HBM((BLK, RANK), F32)],
+        input_output_aliases={n + i: i for i in range(len(before))},
         scratch_shapes=[
-            pltpu.VMEM((NZ, NM, RANK // NM, HALF // NZ), BF16),
-            pltpu.VMEM((ROWS, HALF), BF16),
-            pltpu.VMEM((ROWS, HALF), BF16),
-            pltpu.VMEM((ROWS, COLS), BF16),
+            pltpu.VMEM((1 if held else NZ, NM, GROUP, CHUNK), BF16),
+            pltpu.VMEM((CHUNKS, ROWS, CHUNK), BF16),
+            pltpu.VMEM((CHUNKS, ROWS, CHUNK), BF16),
+            pltpu.VMEM((SUB, RANK), F32),
             pltpu.VMEM((ROWS, RANK), BF16),
             pltpu.VMEM((RANK, RANK), F32),
-            pltpu.SemaphoreType.DMA((4 * HALF // STEP + 2,)),
+            pltpu.SemaphoreType.DMA((3 + 2 * CHUNKS + NM,)),
         ],
         compiler_params=params(),
-        cost_estimate=pl.CostEstimate(flops=2 * ROWS * COLS * RANK, bytes_accessed=4 * ROWS * COLS + 2 * COLS * RANK, transcendentals=0),
-    )(c, m, *in_hbm(w, inv), t, *in_hbm(u, own, *others))
+        cost_estimate=pl.CostEstimate(flops=2 * ROWS * HALF * RANK, bytes_accessed=4 * ROWS * HALF + 2 * HALF * RANK, transcendentals=0),
+    )(where, *in_hbm(w, inv), t if held else in_hbm(t)[0], *in_hbm(*parts, *before))
 
 
 def swap(x):
@@ -372,7 +363,7 @@
     gradient, error = gradient[0], error[0]
     c = lax.axis_index("c").astype(jnp.int32)
     m = (lax.axis_index("x") * 4 + lax.axis_index("y")).astype(jnp.int32)
-    cv, mv = c.reshape(1), m.reshape(1)
+    cv = c.reshape(1)
 
     with jax.named_scope("query_gather"):
         part = lax.dynamic_slice_in_dim(query, c * SUB, SUB, 0)
@@ -399,16 +390,18 @@
 
     with jax.named_scope("gather"):
         gram_y = ring_sum(gram_x, "y")
-        pieces, gram_y = lax.optimization_barrier((pieces, gram_y))
-        mine = lax.all_to_all(total(pieces), ("z", "x", "y"), 0, 0, tiled=True)
+        sums, gram_y = lax.optimization_barrier((total(pieces), gram_y))
+        mine = lax.all_to_all(sums, ("z", "x", "y"), 0, 0, tiled=True)
 
     with jax.named_scope("solve"):
         inv, w = solve(join(c, gram_y, swap(gram_y)), summed)
         mine, inv, w = lax.optimization_barrier((mine, inv, w))
 
     with jax.named_scope("finish"):
-        mine = mine.reshape(NZ, NM, RANK // NM, HALF // NZ)
-        new_error, factor = finish(cv, mv, w, inv, own, others, mine, swap(mine))
+        mine = mine.reshape(NZ, NM, GROUP, CHUNK)
+        theirs = swap(mine)
+        out = finish(True, jnp.stack([c, m]), w, inv, mine, [own])
+        new_error, factor = finish(False, jnp.stack([1 - c, m]), w, inv, theirs, others, out)
     return factor, new_error[None]
 
 

time: 164 us -> 159 us (0.970)
  Pallas kernels: 68.3 us -> 63.6 us
  waiting for transfers between devices: 48.9 us -> 47.2 us
    ppermute x8, waiting for transfers between devices: 12.6 us -> 8.54 us  [swap(): return lax.ppermute(x, 'c', [(0, 1), (1, 0)])]
    all_to_all x1, waiting for transfers between devices: 0.01 us -> 3.55 us  [shards(): lax.all_to_all(copies, ('x', 'y'), 0, 0, tiled=True).reshape(HALF, RANK)]
    pallas_call x3 -> x4, Pallas kernels: 29.4 us -> 26.3 us  [the longest x2 11 us: finish(): pl.pallas_call(functools.partial(finish_kernel, held), in_specs=[SMEM, HB...]
where the time goes in v3:
time: 159 us; the launch traced here: 158 us
  Pallas kernels  63.6 us (40%)
  waiting for transfers between devices  47.2 us (30%)
  starting transfers between devices  42.4 us (27%)
  local copies, waits for them, and re-layouts  3.51 us (2%)
    ppermute x9, waiting for transfers between devices, ring_sum(): lax.ppermute(x, axis, [(i, (i + k) % 4) for i in range(4)])  33.5 us
    pallas_call x1, Pallas kernels, solve(): pl.pallas_call(solve_kernel, grid=(1,), in_specs=[VMEM, tall], out_specs=...  27.1 us
    ppermute x9, starting transfers between devices, ring_sum(): lax.ppermute(x, axis, [(i, (i + k) % 4) for i in range(4)])  11.5 us
    pallas_call x2, Pallas kernels, finish(): pl.pallas_call(functools.partial(finish_kernel, held), in_specs=[SMEM, HB...  11 us
    ppermute x8, starting transfers between devices, swap(): return lax.ppermute(x, 'c', [(0, 1), (1, 0)])  10.4 us
    pallas_call x1, Pallas kernels, adjust(): pl.pallas_call(adjust_kernel, in_specs=[SMEM, HBM, HBM], out_specs=[HBM]...  9.73 us
    ppermute x8, waiting for transfers between devices, swap(): return lax.ppermute(x, 'c', [(0, 1), (1, 0)])  8.54 us
    all_to_all x1, starting transfers between devices, shards(): mine = lax.all_to_all(sums, ('z', 'x', 'y'), 0, 0, tiled=True)  8.24 us
  transfers between devices with their start and end apart: 20, of which 14 were waited for; matrix products, arithmetic and copies ran while one was open for 0% of the time, Pallas kernels for 33%

profile of v3, /device:TPU:1, one launch (start us, length us, event | category | flops | bytes accessed | tf_op | source)
XLA Modules:
  0.0 158.1 jit_solution(18117787684721663886)
XLA Ops:
  0.6 0.0 copy-start
  0.7 0.9 copy-done
  1.6 1.6 broadcast_in_dim.4
  3.2 7.6 %all-to-all-start = ((bf16[16,256,256]{2,1,0:T(8,128)(2,1)}), bf16[16,256,256]{2,1,0:T(8,128)(2,1)S(1)}, u32[]{:S(2)}, u32[]{:S(2)}) async-start(bf16[16,256,256]{2,1,0:T(8,128)(2,1)} %broadcast_in_dim.4), calls=%async_computation | async-start | bytes 4194304 | tf_op jit(solution)/shard_map/query_gather/all_to_all | solution.py:371
  10.8 9.7 %adjust.2 = (bf16[512,4096]{1,0:T(8,128)(2,1)}, bf16[512,1024]{1,0:T(8,128)(2,1)}, bf16[512,1024]{1,0:T(8,128)(2,1)}, bf16[512,1024]{1,0:T(8,128)(2,1)}, bf16[512,1024]{1,0:T(8,128)(2,1)}) custom-call(s32[1]{0:T(128)} %bitcast.2.c_ref, bf16[512,8192]{1,0:T(8,128)(2,1)} %bitcast.12, bf16[512,8192]{1,0:T(8,128)(2,1)} %bitcast.13), custom_call_target="tpu_custom_call" | custom-call | flops 4194304 | bytes 25165824 | tf_op jit(solution)/shard_map/adjust/pallas_call | solution.py:90
  20.5 1.0 collective-permute-start
  21.5 0.1 collective-permute-start.1
  21.6 0.4 collective-permute-start.2
  22.1 0.1 collective-permute-start.3
  22.1 1.9 %collective-permute-done.refs_0_ = bf16[512,1024]{1,0:T(8,128)(2,1)S(1)} collective-permute-done((bf16[512,1024]{1,0:T(8,128)(2,1)}, bf16[512,1024]{1,0:T(8,128)(2,1)S(1)}, u32[]{:S(2)}, u32[]{:S(2)}) %collective-permute-start) | collective-permute-done | bytes 1048608 | tf_op jit(solution)/shard_map/adjust/ppermute | solution.py:350
  24.0 0.0 copy-start.1
  24.0 1.5 collective-permute-done.1.refs_1_
  25.5 0.0 copy-start.2
  25.5 1.5 collective-permute-done.2.refs_2_
  27.0 0.0 copy-start.3
  27.0 1.5 collective-permute-done.3.refs_3_
  28.5 0.0 copy-start.4
  28.5 0.0 copy-done.1
  28.5 0.0 copy-done.2
  28.5 0.0 copy-done.3
  28.6 1.0 copy-done.4
  29.5 5.6 %adjust.3.a_ref = bf16[512,4096]{1,0:T(8,128)(2,1)} custom-call(bf16[512,4096]{1,0:T(8,128)(2,1)} %get-tuple-element.25.own_ref.refs_0_, bf16[512,1024]{1,0:T(8,128)(2,1)} %copy-done.1, bf16[512,1024]{1,0:T(8,128)(2,1)} %copy-done.2, bf16[512,1024]{1,0:T(8,128)(2,1)} %copy-done.3, bf16[512,1024]{1,0:T(8,128)(2,1)} %copy-done.4), custom_call_target="tpu_custom_call" | custom-call | flops 2097152 | bytes 12582912 | tf_op jit(solution)/shard_map/adjust/pallas_call | solution.py:119
  35.1 3.5 %all-to-all-done = bf16[16,256,256]{2,1,0:T(8,128)(2,1)S(1)} async-done(((bf16[16,256,256]{2,1,0:T(8,128)(2,1)}), bf16[16,256,256]{2,1,0:T(8,128)(2,1)S(1)}, u32[]{:S(2)}, u32[]{:S(2)}) %all-to-all-start) | async-done | bytes 2097184 | tf_op jit(solution)/shard_map/query_gather/all_to_all | solution.py:371
  38.7 3.8 %project.1 = (f32[256,256]{1,0:T(8,128)S(1)}, f32[256,256]{1,0:T(8,128)S(1)}) custom-call(s32[1]{0:T(128)} %bitcast.2.c_ref, bf16[4096,256]{1,0:T(8,128)(2,1)S(1)} %bitcast.9, bf16[512,4096]{1,0:T(8,128)(2,1)} %adjust.3.a_ref), custom_call_target="tpu_custom_call" | custom-call | flops 1073741824 | bytes 6291456 | tf_op jit(solution)/shard_map/project/pallas_call | solution.py:144
  42.5 3.5 %collective-permute-start.4 = (f32[256,256]{1,0:T(8,128)S(1)}, f32[256,256]{1,0:T(8,128)S(1)}, u32[]{:S(2)}, u32[]{:S(2)}) collective-permute-start(f32[256,256]{1,0:T(8,128)S(1)} %get-tuple-element.31), channel_id=1, source_target_pairs={{0,16},{16,0},{1,17},{17,1},{2,18},{18,2},{3,19},{19,3},{4,20},{20... | collective-permute-start | bytes 786440 | tf_op jit(solution)/shard_map/project/ppermute | solution.py:350
  46.0 1.2 collective-permute-done.4
  47.2 3.8 %collective-permute-start.7 = (bf16[256,256]{1,0:T(8,128)(2,1)S(1)}, bf16[256,256]{1,0:T(8,128)(2,1)S(1)}, u32[]{:S(2)}, u32[]{:S(2)}) collective-permute-start(bf16[256,256]{1,0:T(8,128)(2,1)S(1)} %add_convert_fusion.1), channel_id=1, source_target_pairs={{0,96},{32,0},{64,32},{96,64},{1,97},{33,1},{65,33},{97,65},{2,98}... | collective-permute-start | bytes 393224 | tf_op jit(solution)/shard_map/project/ppermute | solution.py:354
  51.1 0.0 collective-permute-start.6
  51.1 1.3 collective-permute-start.5
  52.4 1.2 collective-permute-done.7
  53.6 6.3 %collective-permute-done.6 = bf16[256,256]{1,0:T(8,128)(2,1)S(1)} collective-permute-done((bf16[256,256]{1,0:T(8,128)(2,1)S(1)}, bf16[256,256]{1,0:T(8,128)(2,1)S(1)}, u32[]{:S(2)}, u32[]{:S(2)}) %collective-permute-start.6) | collective-permute-done | bytes 131104 | tf_op jit(solution)/shard_map/project/ppermute | solution.py:354
  59.9 0.0 collective-permute-done.5
  59.9 0.1 add_convert_fusion.mine_ref
  59.9 1.2 collective-permute-start.8
  61.1 1.0 collective-permute-done.8.theirs_ref
  62.1 0.8 gram.1
  63.0 0.1 collective-permute-start.11
  63.1 1.3 collective-permute-start.10
  64.4 0.7 collective-permute-start.9
  65.2 3.9 %term.1 = bf16[4,16,16,1024]{3,2,1,0:T(8,128)(2,1)} custom-call(bf16[256,512]{1,0:T(8,128)(2,1)S(1)} %get-tuple-element.32.st_ref, bf16[512,4096]{1,0:T(8,128)(2,1)} %adjust.3.a_ref), custom_call_target="tpu_custom_call" | custom-call | flops 1073741824 | bytes 6291456 | tf_op jit(solution)/shard_map/term/pallas_call | solution.py:203
  69.0 0.0 collective-permute-done.11
  69.0 0.0 collective-permute-done.10
  69.1 0.1 collective-permute-done.9
  69.2 4.7 %all-to-all-start.1 = ((bf16[64,16,1024]{2,1,0:T(8,128)(2,1)}), bf16[64,16,1024]{2,1,0:T(8,128)(2,1)S(1)}, u32[]{:S(2)}, u32[]{:S(2)}) async-start(bf16[64,16,1024]{2,1,0:T(8,128)(2,1)} %bitcast.15), calls=%async_computation.1 | async-start | bytes 4194304 | tf_op jit(solution)/shard_map/term/all_to_all | solution.py:389
  73.9 2.4 %collective-permute-start.14 = (f32[128,256]{1,0:T(8,128)S(1)}, f32[128,256]{1,0:T(8,128)S(1)}, u32[]{:S(2)}, u32[]{:S(2)}) collective-permute-start(f32[128,256]{1,0:T(8,128)S(1)} %add_add_fusion.1), channel_id=1, source_target_pairs={{0,3},{1,0},{2,1},{3,2},{4,7},{5,4},{6,5},{7,6},{8,11},{9,8},{10,9... | collective-permute-start | bytes 393224 | tf_op jit(solution)/shard_map/gather/ppermute | solution.py:354
  76.3 0.0 collective-permute-start.13
  76.3 1.8 %collective-permute-start.12 = (f32[128,256]{1,0:T(8,128)S(1)}, f32[128,256]{1,0:T(8,128)S(1)}, u32[]{:S(2)}, u32[]{:S(2)}) collective-permute-start(f32[128,256]{1,0:T(8,128)S(1)} %add_add_fusion.1), channel_id=1, source_target_pairs={{0,2},{1,3},{2,0},{3,1},{4,6},{5,7},{6,4},{7,5},{8,10},{9,11},{10,... | collective-permute-start | bytes 393224 | tf_op jit(solution)/shard_map/gather/ppermute | solution.py:354
  78.0 17.6 %collective-permute-done.14 = f32[128,256]{1,0:T(8,128)S(1)} collective-permute-done((f32[128,256]{1,0:T(8,128)S(1)}, f32[128,256]{1,0:T(8,128)S(1)}, u32[]{:S(2)}, u32[]{:S(2)}) %collective-permute-start.14) | collective-permute-done | bytes 131104 | tf_op jit(solution)/shard_map/gather/ppermute | solution.py:354
  95.6 3.2 %collective-permute-done.13 = f32[128,256]{1,0:T(8,128)S(1)} collective-permute-done((f32[128,256]{1,0:T(8,128)S(1)}, f32[128,256]{1,0:T(8,128)S(1)}, u32[]{:S(2)}, u32[]{:S(2)}) %collective-permute-start.13) | collective-permute-done | bytes 131104 | tf_op jit(solution)/shard_map/gather/ppermute | solution.py:354
  98.8 5.2 %collective-permute-done.12 = f32[128,256]{1,0:T(8,128)S(1)} collective-permute-done((f32[128,256]{1,0:T(8,128)S(1)}, f32[128,256]{1,0:T(8,128)S(1)}, u32[]{:S(2)}, u32[]{:S(2)}) %collective-permute-start.12) | collective-permute-done | bytes 131104 | tf_op jit(solution)/shard_map/gather/ppermute | solution.py:354
  104.0 0.0 all-to-all-done.1.x_ref
  104.0 1.7 %gather.1 = bf16[64,16,1024]{2,1,0:T(8,128)(2,1)} custom-call(bf16[64,16,1024]{2,1,0:T(8,128)(2,1)S(1)} %all-to-all-done.1.x_ref), custom_call_target="tpu_custom_call" | custom-call | flops 1048576 | bytes 4194304 | tf_op jit(solution)/shard_map/gather/pallas_call | solution.py:228
  105.7 2.3 %collective-permute-start.15 = (f32[128,256]{1,0:T(8,128)S(1)}, f32[128,256]{1,0:T(8,128)S(1)}, u32[]{:S(2)}, u32[]{:S(2)}) collective-permute-start(f32[128,256]{1,0:T(8,128)S(1)} %add_add_fusion), channel_id=1, source_target_pairs={{0,16},{16,0},{1,17},{17,1},{2,18},{18,2},{3,19},{19,3},{4,20},{20... | collective-permute-start | bytes 393224 | tf_op jit(solution)/shard_map/solve/ppermute | solution.py:350
  107.9 8.2 %all-to-all-start.2 = ((bf16[64,16,1024]{2,1,0:T(8,128)(2,1)}), bf16[64,16,1024]{2,1,0:T(8,128)(2,1)S(1)}, u32[]{:S(2)}, u32[]{:S(2)}) async-start(bf16[64,16,1024]{2,1,0:T(8,128)(2,1)} %gather.1), calls=%async_computation.2 | async-start | bytes 4194304 | tf_op jit(solution)/shard_map/gather/all_to_all | solution.py:394
  116.2 0.0 collective-permute-done.15
  116.2 27.1 %solve.1 = (f32[256,256]{1,0:T(8,128)}, bf16[512,256]{1,0:T(8,128)(2,1)}) custom-call(f32[256,256]{1,0:T(8,128)S(1)} %pad_maximum_fusion.g_ref, bf16[512,256]{1,0:T(8,128)(2,1)} %get-tuple-element.38.s_ref), custom_call_target="tpu_custom_call" | custom-call | flops 20000000000 | bytes 1000000 | tf_op jit(solution)/shard_map/solve/pallas_call | solution.py:283
  143.3 1.6 %all-to-all-done.2 = bf16[64,16,1024]{2,1,0:T(8,128)(2,1)S(1)} async-done(((bf16[64,16,1024]{2,1,0:T(8,128)(2,1)}), bf16[64,16,1024]{2,1,0:T(8,128)(2,1)S(1)}, u32[]{:S(2)}, u32[]{:S(2)}) %all-to-all-start.2) | async-done | bytes 2097184 | tf_op jit(solution)/shard_map/gather/all_to_all | solution.py:394
  145.0 1.8 %collective-permute-start.16 = (bf16[4,16,16,1024]{3,2,1,0:T(8,128)(2,1)S(1)}, bf16[4,16,16,1024]{3,2,1,0:T(8,128)(2,1)}, u32[]{:S(2)}, u32[]{:S(2)}) collective-permute-start(bf16[4,16,16,1024]{3,2,1,0:T(8,128)(2,1)S(1)} %bitcast.10), channel_id=1, source_target_pairs={{0,16},{16,0},{1,17},{17,1},{2,18},{18,2},{3,19},{19,3},{4,20},{20... | collective-permute-start | bytes 6291464 | tf_op jit(solution)/shard_map/finish/ppermute | solution.py:350
  146.7 0.1 pad_add_fusion.1.s_ref
  146.8 0.1 pad_add_fusion.s_ref
  146.9 5.4 %finish.2 = (bf16[512,8192]{1,0:T(8,128)(2,1)}, f32[512,256]{1,0:T(8,128)}) custom-call(s32[2]{0:T(128)S(1)} %pad_add_fusion.1.s_ref, bf16[512,256]{1,0:T(8,128)(2,1)} %get-tuple-element.41.w_ref, f32[256,256]{1,0:T(8,128)} %get-tuple-element.42.inv_ref, bf16[4,16,16,1024]{3,2,1,0:T(8,128)(2,1)S(1)} %bitcast.11, ...), custom_call_target="tpu_custom_call" | custom-call | flops 1073741824 | bytes 10485760 | tf_op jit(solution)/shard_map/finish/pallas_call | solution.py:329
  152.3 0.0 collective-permute-done.16.t_ref
  152.3 5.6 %finish.3 = (bf16[512,8192]{1,0:T(8,128)(2,1)}, f32[512,256]{1,0:T(8,128)}) custom-call(s32[2]{0:T(128)S(1)} %pad_add_fusion.s_ref, bf16[512,256]{1,0:T(8,128)(2,1)} %get-tuple-element.41.w_ref, f32[256,256]{1,0:T(8,128)} %get-tuple-element.42.inv_ref, ...), custom_call_target="tpu_custom_call", output_to_operand_aliasing={{0}: (8, {}), {1}: (9, {})} | custom-call | flops 1073741824 | bytes 10485760 | tf_op jit(solution)/shard_map/finish/pallas_call | solution.py:329
  (6 shorter events, 0.2 us)
Async XLA Ops:
  0.6 1.0 copy-start
  3.2 35.5 %all-to-all-start = ((bf16[16,256,256]{2,1,0:T(8,128)(2,1)}), bf16[16,256,256]{2,1,0:T(8,128)(2,1)S(1)}, u32[]{:S(2)}, u32[]{:S(2)}) async-start(bf16[16,256,256]{2,1,0:T(8,128)(2,1)} %broadcast_in_dim.4), calls=%async_computation | async-start | bytes 4194304 | tf_op jit(solution)/shard_map/query_gather/all_to_all | solution.py:371
  20.5 3.5 %collective-permute-start = (bf16[512,1024]{1,0:T(8,128)(2,1)}, bf16[512,1024]{1,0:T(8,128)(2,1)S(1)}, u32[]{:S(2)}, u32[]{:S(2)}) collective-permute-start(bf16[512,1024]{1,0:T(8,128)(2,1)} %get-tuple-element.26.refs_0_), channel_id=1, source_target_pairs={{0,16},{16,0},{1,17},{17,1},{2,18},{18,2},{3,19},{19,3},{4,20},{20... | collective-permute-start | bytes 3145736 | tf_op jit(solution)/shard_map/adjust/ppermute | solution.py:350
  21.5 4.0 %collective-permute-start.1 = (bf16[512,1024]{1,0:T(8,128)(2,1)}, bf16[512,1024]{1,0:T(8,128)(2,1)S(1)}, u32[]{:S(2)}, u32[]{:S(2)}) collective-permute-start(bf16[512,1024]{1,0:T(8,128)(2,1)} %get-tuple-element.27.refs_1_), channel_id=1, source_target_pairs={{0,16},{16,0},{1,17},{17,1},{2,18},{18,2},{3,19},{19,3},{4,20},{20... | collective-permute-start | bytes 3145736 | tf_op jit(solution)/shard_map/adjust/ppermute | solution.py:350
  21.6 5.4 %collective-permute-start.2 = (bf16[512,1024]{1,0:T(8,128)(2,1)}, bf16[512,1024]{1,0:T(8,128)(2,1)S(1)}, u32[]{:S(2)}, u32[]{:S(2)}) collective-permute-start(bf16[512,1024]{1,0:T(8,128)(2,1)} %get-tuple-element.28.refs_2_), channel_id=1, source_target_pairs={{0,16},{16,0},{1,17},{17,1},{2,18},{18,2},{3,19},{19,3},{4,20},{20... | collective-permute-start | bytes 3145736 | tf_op jit(solution)/shard_map/adjust/ppermute | solution.py:350
  22.1 6.5 %collective-permute-start.3 = (bf16[512,1024]{1,0:T(8,128)(2,1)}, bf16[512,1024]{1,0:T(8,128)(2,1)S(1)}, u32[]{:S(2)}, u32[]{:S(2)}) collective-permute-start(bf16[512,1024]{1,0:T(8,128)(2,1)} %get-tuple-element.29.refs_3_), channel_id=1, source_target_pairs={{0,16},{16,0},{1,17},{17,1},{2,18},{18,2},{3,19},{19,3},{4,20},{20... | collective-permute-start | bytes 3145736 | tf_op jit(solution)/shard_map/adjust/ppermute | solution.py:350
  24.0 4.5 %copy-start.1 = (bf16[512,1024]{1,0:T(8,128)(2,1)}, bf16[512,1024]{1,0:T(8,128)(2,1)S(1)}, u32[]{:S(2)}) copy-start(bf16[512,1024]{1,0:T(8,128)(2,1)S(1)} %collective-permute-done.refs_0_) | copy-start | bytes 3145732
  25.5 3.0 %copy-start.2 = (bf16[512,1024]{1,0:T(8,128)(2,1)}, bf16[512,1024]{1,0:T(8,128)(2,1)S(1)}, u32[]{:S(2)}) copy-start(bf16[512,1024]{1,0:T(8,128)(2,1)S(1)} %collective-permute-done.1.refs_1_) | copy-start | bytes 3145732
  27.0 1.5 copy-start.3
  28.5 1.0 copy-start.4
  42.5 4.7 %collective-permute-start.4 = (f32[256,256]{1,0:T(8,128)S(1)}, f32[256,256]{1,0:T(8,128)S(1)}, u32[]{:S(2)}, u32[]{:S(2)}) collective-permute-start(f32[256,256]{1,0:T(8,128)S(1)} %get-tuple-element.31), channel_id=1, source_target_pairs={{0,16},{16,0},{1,17},{17,1},{2,18},{18,2},{3,19},{19,3},{4,20},{20... | collective-permute-start | bytes 786440 | tf_op jit(solution)/shard_map/project/ppermute | solution.py:350
  47.2 6.3 %collective-permute-start.7 = (bf16[256,256]{1,0:T(8,128)(2,1)S(1)}, bf16[256,256]{1,0:T(8,128)(2,1)S(1)}, u32[]{:S(2)}, u32[]{:S(2)}) collective-permute-start(bf16[256,256]{1,0:T(8,128)(2,1)S(1)} %add_convert_fusion.1), channel_id=1, source_target_pairs={{0,96},{32,0},{64,32},{96,64},{1,97},{33,1},{65,33},{97,65},{2,98}... | collective-permute-start | bytes 393224 | tf_op jit(solution)/shard_map/project/ppermute | solution.py:354
  51.1 8.8 %collective-permute-start.6 = (bf16[256,256]{1,0:T(8,128)(2,1)S(1)}, bf16[256,256]{1,0:T(8,128)(2,1)S(1)}, u32[]{:S(2)}, u32[]{:S(2)}) collective-permute-start(bf16[256,256]{1,0:T(8,128)(2,1)S(1)} %add_convert_fusion.1), channel_id=1, source_target_pairs={{0,32},{32,64},{64,96},{96,0},{1,33},{33,65},{65,97},{97,1},{2,34}... | collective-permute-start | bytes 393224 | tf_op jit(solution)/shard_map/project/ppermute | solution.py:354
  51.1 8.8 %collective-permute-start.5 = (bf16[256,256]{1,0:T(8,128)(2,1)S(1)}, bf16[256,256]{1,0:T(8,128)(2,1)S(1)}, u32[]{:S(2)}, u32[]{:S(2)}) collective-permute-start(bf16[256,256]{1,0:T(8,128)(2,1)S(1)} %add_convert_fusion.1), channel_id=1, source_target_pairs={{0,64},{32,96},{64,0},{96,32},{1,65},{33,97},{65,1},{97,33},{2,66}... | collective-permute-start | bytes 393224 | tf_op jit(solution)/shard_map/project/ppermute | solution.py:354
  59.9 2.2 %collective-permute-start.8 = (bf16[256,256]{1,0:T(8,128)(2,1)S(1)}, bf16[256,256]{1,0:T(8,128)(2,1)S(1)}, u32[]{:S(2)}, u32[]{:S(2)}) collective-permute-start(bf16[256,256]{1,0:T(8,128)(2,1)S(1)} %add_convert_fusion.mine_ref), channel_id=1, source_target_pairs={{0,16},{16,0},{1,17},{17,1},{2,18},{18,2},{3,19},{19,3},{4,20},{20... | collective-permute-start | bytes 393224 | tf_op jit(solution)/shard_map/gram/ppermute | solution.py:350
  63.0 6.1 %collective-permute-start.11 = (bf16[128,256]{1,0:T(8,128)(2,1)S(1)}, bf16[128,256]{1,0:T(8,128)(2,1)S(1)}, u32[]{:S(2)}, u32[]{:S(2)}) collective-permute-start(bf16[128,256]{1,0:T(8,128)(2,1)S(1)} %get-tuple-element.33), channel_id=1, source_target_pairs={{0,12},{4,0},{8,4},{12,8},{1,13},{5,1},{9,5},{13,9},{2,14},{6,2},{... | collective-permute-start | bytes 196616 | tf_op jit(solution)/shard_map/gram/ppermute | solution.py:354
  63.1 5.9 %collective-permute-start.10 = (bf16[128,256]{1,0:T(8,128)(2,1)S(1)}, bf16[128,256]{1,0:T(8,128)(2,1)S(1)}, u32[]{:S(2)}, u32[]{:S(2)}) collective-permute-start(bf16[128,256]{1,0:T(8,128)(2,1)S(1)} %get-tuple-element.33), channel_id=1, source_target_pairs={{0,4},{4,8},{8,12},{12,0},{1,5},{5,9},{9,13},{13,1},{2,6},{6,10},{... | collective-permute-start | bytes 196616 | tf_op jit(solution)/shard_map/gram/ppermute | solution.py:354
  64.4 4.7 %collective-permute-start.9 = (bf16[128,256]{1,0:T(8,128)(2,1)S(1)}, bf16[128,256]{1,0:T(8,128)(2,1)S(1)}, u32[]{:S(2)}, u32[]{:S(2)}) collective-permute-start(bf16[128,256]{1,0:T(8,128)(2,1)S(1)} %get-tuple-element.33), channel_id=1, source_target_pairs={{0,8},{4,12},{8,0},{12,4},{1,9},{5,13},{9,1},{13,5},{2,10},{6,14},... | collective-permute-start | bytes 196616 | tf_op jit(solution)/shard_map/gram/ppermute | solution.py:354
  69.2 34.8 %all-to-all-start.1 = ((bf16[64,16,1024]{2,1,0:T(8,128)(2,1)}), bf16[64,16,1024]{2,1,0:T(8,128)(2,1)S(1)}, u32[]{:S(2)}, u32[]{:S(2)}) async-start(bf16[64,16,1024]{2,1,0:T(8,128)(2,1)} %bitcast.15), calls=%async_computation.1 | async-start | bytes 4194304 | tf_op jit(solution)/shard_map/term/all_to_all | solution.py:389
  73.9 21.7 %collective-permute-start.14 = (f32[128,256]{1,0:T(8,128)S(1)}, f32[128,256]{1,0:T(8,128)S(1)}, u32[]{:S(2)}, u32[]{:S(2)}) collective-permute-start(f32[128,256]{1,0:T(8,128)S(1)} %add_add_fusion.1), channel_id=1, source_target_pairs={{0,3},{1,0},{2,1},{3,2},{4,7},{5,4},{6,5},{7,6},{8,11},{9,8},{10,9... | collective-permute-start | bytes 393224 | tf_op jit(solution)/shard_map/gather/ppermute | solution.py:354
  76.3 22.5 %collective-permute-start.13 = (f32[128,256]{1,0:T(8,128)S(1)}, f32[128,256]{1,0:T(8,128)S(1)}, u32[]{:S(2)}, u32[]{:S(2)}) collective-permute-start(f32[128,256]{1,0:T(8,128)S(1)} %add_add_fusion.1), channel_id=1, source_target_pairs={{0,1},{1,2},{2,3},{3,0},{4,5},{5,6},{6,7},{7,4},{8,9},{9,10},{10,1... | collective-permute-start | bytes 393224 | tf_op jit(solution)/shard_map/gather/ppermute | solution.py:354
  76.3 27.7 %collective-permute-start.12 = (f32[128,256]{1,0:T(8,128)S(1)}, f32[128,256]{1,0:T(8,128)S(1)}, u32[]{:S(2)}, u32[]{:S(2)}) collective-permute-start(f32[128,256]{1,0:T(8,128)S(1)} %add_add_fusion.1), channel_id=1, source_target_pairs={{0,2},{1,3},{2,0},{3,1},{4,6},{5,7},{6,4},{7,5},{8,10},{9,11},{10,... | collective-permute-start | bytes 393224 | tf_op jit(solution)/shard_map/gather/ppermute | solution.py:354
  105.7 10.5 %collective-permute-start.15 = (f32[128,256]{1,0:T(8,128)S(1)}, f32[128,256]{1,0:T(8,128)S(1)}, u32[]{:S(2)}, u32[]{:S(2)}) collective-permute-start(f32[128,256]{1,0:T(8,128)S(1)} %add_add_fusion), channel_id=1, source_target_pairs={{0,16},{16,0},{1,17},{17,1},{2,18},{18,2},{3,19},{19,3},{4,20},{20... | collective-permute-start | bytes 393224 | tf_op jit(solution)/shard_map/solve/ppermute | solution.py:350
  107.9 37.0 %all-to-all-start.2 = ((bf16[64,16,1024]{2,1,0:T(8,128)(2,1)}), bf16[64,16,1024]{2,1,0:T(8,128)(2,1)S(1)}, u32[]{:S(2)}, u32[]{:S(2)}) async-start(bf16[64,16,1024]{2,1,0:T(8,128)(2,1)} %gather.1), calls=%async_computation.2 | async-start | bytes 4194304 | tf_op jit(solution)/shard_map/gather/all_to_all | solution.py:394
  145.0 7.3 %collective-permute-start.16 = (bf16[4,16,16,1024]{3,2,1,0:T(8,128)(2,1)S(1)}, bf16[4,16,16,1024]{3,2,1,0:T(8,128)(2,1)}, u32[]{:S(2)}, u32[]{:S(2)}) collective-permute-start(bf16[4,16,16,1024]{3,2,1,0:T(8,128)(2,1)S(1)} %bitcast.10), channel_id=1, source_target_pairs={{0,16},{16,0},{1,17},{17,1},{2,18},{18,2},{3,19},{19,3},{4,20},{20... | collective-permute-start | bytes 6291464 | tf_op jit(solution)/shard_map/finish/ppermute | solution.py:350

commit v4 on v3

--- a/solution.py
+++ b/solution.py
@@ -245,6 +245,7 @@
 
 NT_DOT = (((1,), (1,)), ((), ()))
 BASE = 64
+PANEL = 16
 
 
 def inverse_factor(a):
@@ -261,11 +262,14 @@
     row = lax.broadcasted_iota(jnp.int32, (n, 2 * n), 0)
     lane = lax.broadcasted_iota(jnp.int32, (n, 2 * n), 1)
     x = jnp.concatenate([a, jnp.where(row == lane, 1.0, 0.0)[:, :n].astype(F32)], axis=1)
-    for j in range(n - 1):
-        column = jnp.broadcast_to(x[:, j : j + 1], x.shape)
-        pivot = column[j : j + 1, :]
-        ratio = jnp.where(row > j, column, 0.0) * (1.0 / pivot)
-        x = x - ratio * x[j : j + 1, :]
+    for first in range(0, n, PANEL):
+        columns = [jnp.broadcast_to(x[:, j : j + 1], x.shape) for j in range(first, first + PANEL)]
+        for i in range(min(PANEL, n - 1 - first)):
+            j = first + i
+            ratio = jnp.where(row > j, columns[i], 0.0) * (1.0 / columns[i][j : j + 1, :])
+            for k in range(i + 1, PANEL):
+                columns[k] = columns[k] - ratio * columns[k][j : j + 1, :]
+            x = x - ratio * x[j : j + 1, :]
     d = jnp.sum(jnp.where(row == lane, x, 0.0), axis=1, keepdims=True)
     return x[:, n:] * (1.0 / jnp.sqrt(d))
 
@@ -351,7 +355,7 @@
 
 
 def ring_sum(x, axis):
-    x1, x2, x3 = (lax.ppermute(x, axis, [(i, (i + k) % 4) for i in range(4)]) for k in (1, 2, 3))
+    x1, x3, x2 = (lax.ppermute(x, axis, [(i, (i + k) % 4) for i in range(4)]) for k in (1, 3, 2))
     return (x.astype(F32) + x2.astype(F32)) + (x1.astype(F32) + x3.astype(F32))
 
 
@@ -389,7 +393,7 @@
         pieces = lax.all_to_all(pieces, ("z", "x", "y"), 0, 0, tiled=True)
 
     with jax.named_scope("gather"):
-        gram_y = ring_sum(gram_x, "y")
+        gram_y = ring_sum(gram_x.astype(BF16), "y")
         sums, gram_y = lax.optimization_barrier((total(pieces), gram_y))
         mine = lax.all_to_all(sums, ("z", "x", "y"), 0, 0, tiled=True)
 

time: 159 us -> 156 us (0.981)
  Pallas kernels: 63.6 us -> 48.6 us
  waiting for transfers between devices: 47.2 us -> 58.9 us
    all_to_all x1, waiting for transfers between devices: 1.62 us -> 16.6 us  [shards(): mine = lax.all_to_all(sums, ('z', 'x', 'y'), 0, 0, tiled=True)]
    pallas_call x1, Pallas kernels: 27.1 us -> 12.1 us  [solve(): pl.pallas_call(solve_kernel, grid=(1,), in_specs=[VMEM, tall], out_specs=...]
    ppermute x9, waiting for transfers between devices: 33.5 us -> 26.5 us  [ring_sum(): lax.ppermute(x, axis, [(i, (i + k) % 4) for i in range(4)])]
    all_to_all x1, waiting for transfers between devices: 0.01 us -> 3.66 us  [shards(): pieces = lax.all_to_all(pieces, ('z', 'x', 'y'), 0, 0, tiled=True)]
  transfers between devices with their start and end apart: 20 -> 20, of which waited for: 14 -> 14; matrix products, arithmetic and copies ran while one was open for 0% -> 0% of each run, Pallas kernels for 33% -> 24%
where the time goes in v4:
time: 156 us; the launch traced here: 155 us
  waiting for transfers between devices  58.9 us (38%)
  Pallas kernels  48.6 us (31%)
  starting transfers between devices  42.9 us (28%)
  local copies, waits for them, and re-layouts  3.51 us (2%)
    ppermute x9, waiting for transfers between devices, ring_sum(): lax.ppermute(x, axis, [(i, (i + k) % 4) for i in range(4)])  26.5 us
    all_to_all x1, waiting for transfers between devices, shards(): mine = lax.all_to_all(sums, ('z', 'x', 'y'), 0, 0, tiled=True)  16.6 us
    pallas_call x1, Pallas kernels, solve(): pl.pallas_call(solve_kernel, grid=(1,), in_specs=[VMEM, tall], out_specs=...  12.1 us
    ppermute x9, starting transfers between devices, ring_sum(): lax.ppermute(x, axis, [(i, (i + k) % 4) for i in range(4)])  12.1 us
    ppermute x8, starting transfers between devices, swap(): return lax.ppermute(x, 'c', [(0, 1), (1, 0)])  11.6 us
    pallas_call x2, Pallas kernels, finish(): pl.pallas_call(functools.partial(finish_kernel, held), in_specs=[SMEM, HB...  11 us
    pallas_call x1, Pallas kernels, adjust(): pl.pallas_call(adjust_kernel, in_specs=[SMEM, HBM, HBM], out_specs=[HBM]...  9.73 us
    ppermute x8, waiting for transfers between devices, swap(): return lax.ppermute(x, 'c', [(0, 1), (1, 0)])  8.54 us
  transfers between devices with their start and end apart: 20, of which 14 were waited for; matrix products, arithmetic and copies ran while one was open for 0% of the time, Pallas kernels for 24%

profile of v4, /device:TPU:1, one launch (start us, length us, event | category | flops | bytes accessed | tf_op | source)
XLA Modules:
  0.0 155.2 jit_solution(1411510182792310118)
XLA Ops:
  0.6 0.0 copy-start
  0.7 0.9 copy-done
  1.6 1.6 %broadcast_in_dim.4 = bf16[16,256,256]{2,1,0:T(8,128)(2,1)} broadcast(bf16[256,256]{1,0:T(8,128)(2,1)S(1)} %constant_dynamic-slice_fusion), dimensions={1,2} | broadcast | bytes 2228224 | tf_op jit(solution)/shard_map/query_gather/broadcast_in_dim | solution.py:374
  3.2 7.6 %all-to-all-start = ((bf16[16,256,256]{2,1,0:T(8,128)(2,1)}), bf16[16,256,256]{2,1,0:T(8,128)(2,1)S(1)}, u32[]{:S(2)}, u32[]{:S(2)}) async-start(bf16[16,256,256]{2,1,0:T(8,128)(2,1)} %broadcast_in_dim.4), calls=%async_computation | async-start | bytes 4194304 | tf_op jit(solution)/shard_map/query_gather/all_to_all | solution.py:375
  10.8 9.7 %adjust.2 = (bf16[512,4096]{1,0:T(8,128)(2,1)}, bf16[512,1024]{1,0:T(8,128)(2,1)}, bf16[512,1024]{1,0:T(8,128)(2,1)}, bf16[512,1024]{1,0:T(8,128)(2,1)}, bf16[512,1024]{1,0:T(8,128)(2,1)}) custom-call(s32[1]{0:T(128)} %bitcast.2.c_ref, bf16[512,8192]{1,0:T(8,128)(2,1)} %bitcast.12, bf16[512,8192]{1,0:T(8,128)(2,1)} %bitcast.13), custom_call_target="tpu_custom_call" | custom-call | flops 4194304 | bytes 25165824 | tf_op jit(solution)/shard_map/adjust/pallas_call | solution.py:90
  20.5 1.0 collective-permute-start
  21.5 0.1 collective-permute-start.1
  21.6 0.4 collective-permute-start.2
  22.1 0.1 collective-permute-start.3
  22.1 1.9 %collective-permute-done.refs_0_ = bf16[512,1024]{1,0:T(8,128)(2,1)S(1)} collective-permute-done((bf16[512,1024]{1,0:T(8,128)(2,1)}, bf16[512,1024]{1,0:T(8,128)(2,1)S(1)}, u32[]{:S(2)}, u32[]{:S(2)}) %collective-permute-start) | collective-permute-done | bytes 1048608 | tf_op jit(solution)/shard_map/adjust/ppermute | solution.py:354
  24.0 0.0 copy-start.1
  24.0 1.5 collective-permute-done.1.refs_1_
  25.5 0.0 copy-start.2
  25.5 1.5 collective-permute-done.2.refs_2_
  27.0 0.0 copy-start.3
  27.0 1.5 collective-permute-done.3.refs_3_
  28.5 0.0 copy-start.4
  28.5 0.0 copy-done.1
  28.5 0.0 copy-done.2
  28.5 0.0 copy-done.3
  28.6 1.0 copy-done.4
  29.5 5.6 %adjust.3.a_ref = bf16[512,4096]{1,0:T(8,128)(2,1)} custom-call(bf16[512,4096]{1,0:T(8,128)(2,1)} %get-tuple-element.25.own_ref.refs_0_, bf16[512,1024]{1,0:T(8,128)(2,1)} %copy-done.1, bf16[512,1024]{1,0:T(8,128)(2,1)} %copy-done.2, bf16[512,1024]{1,0:T(8,128)(2,1)} %copy-done.3, bf16[512,1024]{1,0:T(8,128)(2,1)} %copy-done.4), custom_call_target="tpu_custom_call" | custom-call | flops 2097152 | bytes 12582912 | tf_op jit(solution)/shard_map/adjust/pallas_call | solution.py:119
  35.1 3.5 %all-to-all-done = bf16[16,256,256]{2,1,0:T(8,128)(2,1)S(1)} async-done(((bf16[16,256,256]{2,1,0:T(8,128)(2,1)}), bf16[16,256,256]{2,1,0:T(8,128)(2,1)S(1)}, u32[]{:S(2)}, u32[]{:S(2)}) %all-to-all-start) | async-done | bytes 2097184 | tf_op jit(solution)/shard_map/query_gather/all_to_all | solution.py:375
  38.7 3.8 %project.1 = (f32[256,256]{1,0:T(8,128)S(1)}, f32[256,256]{1,0:T(8,128)S(1)}) custom-call(s32[1]{0:T(128)} %bitcast.2.c_ref, bf16[4096,256]{1,0:T(8,128)(2,1)S(1)} %bitcast.9, bf16[512,4096]{1,0:T(8,128)(2,1)} %adjust.3.a_ref), custom_call_target="tpu_custom_call" | custom-call | flops 1073741824 | bytes 6291456 | tf_op jit(solution)/shard_map/project/pallas_call | solution.py:144
  42.5 3.5 %collective-permute-start.4 = (f32[256,256]{1,0:T(8,128)S(1)}, f32[256,256]{1,0:T(8,128)S(1)}, u32[]{:S(2)}, u32[]{:S(2)}) collective-permute-start(f32[256,256]{1,0:T(8,128)S(1)} %get-tuple-element.31), channel_id=1, source_target_pairs={{0,16},{16,0},{1,17},{17,1},{2,18},{18,2},{3,19},{19,3},{4,20},{20... | collective-permute-start | bytes 786440 | tf_op jit(solution)/shard_map/project/ppermute | solution.py:354
  46.0 1.2 collective-permute-done.4
  47.2 3.8 %collective-permute-start.7 = (bf16[256,256]{1,0:T(8,128)(2,1)S(1)}, bf16[256,256]{1,0:T(8,128)(2,1)S(1)}, u32[]{:S(2)}, u32[]{:S(2)}) collective-permute-start(bf16[256,256]{1,0:T(8,128)(2,1)S(1)} %add_convert_fusion.1), channel_id=1, source_target_pairs={{0,96},{32,0},{64,32},{96,64},{1,97},{33,1},{65,33},{97,65},{2,98}... | collective-permute-start | bytes 393224 | tf_op jit(solution)/shard_map/project/ppermute | solution.py:358
  51.1 0.0 collective-permute-start.6
  51.1 1.3 collective-permute-start.5
  52.4 1.2 collective-permute-done.7
  53.6 6.3 %collective-permute-done.6 = bf16[256,256]{1,0:T(8,128)(2,1)S(1)} collective-permute-done((bf16[256,256]{1,0:T(8,128)(2,1)S(1)}, bf16[256,256]{1,0:T(8,128)(2,1)S(1)}, u32[]{:S(2)}, u32[]{:S(2)}) %collective-permute-start.6) | collective-permute-done | bytes 131104 | tf_op jit(solution)/shard_map/project/ppermute | solution.py:358
  59.9 0.0 collective-permute-done.5
  59.9 0.1 add_convert_fusion.mine_ref
  59.9 1.2 collective-permute-start.8
  61.1 1.0 collective-permute-done.8.theirs_ref
  62.1 0.8 gram.1
  63.0 0.1 collective-permute-start.11
  63.1 1.3 collective-permute-start.10
  64.4 0.7 collective-permute-start.9
  65.2 3.9 %term.1 = bf16[4,16,16,1024]{3,2,1,0:T(8,128)(2,1)} custom-call(bf16[256,512]{1,0:T(8,128)(2,1)S(1)} %get-tuple-element.32.st_ref, bf16[512,4096]{1,0:T(8,128)(2,1)} %adjust.3.a_ref), custom_call_target="tpu_custom_call" | custom-call | flops 1073741824 | bytes 6291456 | tf_op jit(solution)/shard_map/term/pallas_call | solution.py:203
  69.0 0.0 collective-permute-done.11
  69.0 0.0 collective-permute-done.10
  69.1 0.1 collective-permute-done.9
  69.2 4.7 %all-to-all-start.1 = ((bf16[64,16,1024]{2,1,0:T(8,128)(2,1)}), bf16[64,16,1024]{2,1,0:T(8,128)(2,1)S(1)}, u32[]{:S(2)}, u32[]{:S(2)}) async-start(bf16[64,16,1024]{2,1,0:T(8,128)(2,1)} %bitcast.15), calls=%async_computation.1 | async-start | bytes 4194304 | tf_op jit(solution)/shard_map/term/all_to_all | solution.py:393
  73.9 1.1 collective-permute-start.13
  75.1 2.4 %collective-permute-start.12 = (bf16[128,256]{1,0:T(8,128)(2,1)S(1)}, bf16[128,256]{1,0:T(8,128)(2,1)S(1)}, u32[]{:S(2)}, u32[]{:S(2)}) collective-permute-start(bf16[128,256]{1,0:T(8,128)(2,1)S(1)} %add_add_fusion.1), channel_id=1, source_target_pairs={{0,2},{1,3},{2,0},{3,1},{4,6},{5,7},{6,4},{7,5},{8,10},{9,11},{10,... | collective-permute-start | bytes 196616 | tf_op jit(solution)/shard_map/gather/ppermute | solution.py:358
  77.5 1.2 collective-permute-start.14
  78.6 10.8 %collective-permute-done.13 = bf16[128,256]{1,0:T(8,128)(2,1)S(1)} collective-permute-done((bf16[128,256]{1,0:T(8,128)(2,1)S(1)}, bf16[128,256]{1,0:T(8,128)(2,1)S(1)}, u32[]{:S(2)}, u32[]{:S(2)}) %collective-permute-start.13) | collective-permute-done | bytes 65568 | tf_op jit(solution)/shard_map/gather/ppermute | solution.py:358
  89.5 8.0 %collective-permute-done.12 = bf16[128,256]{1,0:T(8,128)(2,1)S(1)} collective-permute-done((bf16[128,256]{1,0:T(8,128)(2,1)S(1)}, bf16[128,256]{1,0:T(8,128)(2,1)S(1)}, u32[]{:S(2)}, u32[]{:S(2)}) %collective-permute-start.12) | collective-permute-done | bytes 65568 | tf_op jit(solution)/shard_map/gather/ppermute | solution.py:358
  97.5 0.0 collective-permute-done.14
  97.5 3.7 %all-to-all-done.1.x_ref = bf16[64,16,1024]{2,1,0:T(8,128)(2,1)S(1)} async-done(((bf16[64,16,1024]{2,1,0:T(8,128)(2,1)}), bf16[64,16,1024]{2,1,0:T(8,128)(2,1)S(1)}, u32[]{:S(2)}, u32[]{:S(2)}) %all-to-all-start.1) | async-done | bytes 2097184 | tf_op jit(solution)/shard_map/term/all_to_all | solution.py:393
  101.2 1.7 %gather.1 = bf16[64,16,1024]{2,1,0:T(8,128)(2,1)} custom-call(bf16[64,16,1024]{2,1,0:T(8,128)(2,1)S(1)} %all-to-all-done.1.x_ref), custom_call_target="tpu_custom_call" | custom-call | flops 1048576 | bytes 4194304 | tf_op jit(solution)/shard_map/gather/pallas_call | solution.py:228
  102.9 3.5 %collective-permute-start.15 = (f32[128,256]{1,0:T(8,128)S(1)}, f32[128,256]{1,0:T(8,128)S(1)}, u32[]{:S(2)}, u32[]{:S(2)}) collective-permute-start(f32[128,256]{1,0:T(8,128)S(1)} %add_add_fusion), channel_id=1, source_target_pairs={{0,16},{16,0},{1,17},{17,1},{2,18},{18,2},{3,19},{19,3},{4,20},{20... | collective-permute-start | bytes 393224 | tf_op jit(solution)/shard_map/solve/ppermute | solution.py:354
  106.4 6.9 %all-to-all-start.2 = ((bf16[64,16,1024]{2,1,0:T(8,128)(2,1)}), bf16[64,16,1024]{2,1,0:T(8,128)(2,1)S(1)}, u32[]{:S(2)}, u32[]{:S(2)}) async-start(bf16[64,16,1024]{2,1,0:T(8,128)(2,1)} %gather.1), calls=%async_computation.2 | async-start | bytes 4194304 | tf_op jit(solution)/shard_map/gather/all_to_all | solution.py:398
  113.3 0.0 collective-permute-done.15
  113.4 12.1 %solve.1 = (f32[256,256]{1,0:T(8,128)}, bf16[512,256]{1,0:T(8,128)(2,1)}) custom-call(f32[256,256]{1,0:T(8,128)S(1)} %pad_maximum_fusion.g_ref, bf16[512,256]{1,0:T(8,128)(2,1)} %get-tuple-element.38.s_ref), custom_call_target="tpu_custom_call" | custom-call | flops 20000000000 | bytes 1000000 | tf_op jit(solution)/shard_map/solve/pallas_call | solution.py:287
  125.4 16.6 %all-to-all-done.2 = bf16[64,16,1024]{2,1,0:T(8,128)(2,1)S(1)} async-done(((bf16[64,16,1024]{2,1,0:T(8,128)(2,1)}), bf16[64,16,1024]{2,1,0:T(8,128)(2,1)S(1)}, u32[]{:S(2)}, u32[]{:S(2)}) %all-to-all-start.2) | async-done | bytes 2097184 | tf_op jit(solution)/shard_map/gather/all_to_all | solution.py:398
  142.1 1.8 %collective-permute-start.16 = (bf16[4,16,16,1024]{3,2,1,0:T(8,128)(2,1)S(1)}, bf16[4,16,16,1024]{3,2,1,0:T(8,128)(2,1)}, u32[]{:S(2)}, u32[]{:S(2)}) collective-permute-start(bf16[4,16,16,1024]{3,2,1,0:T(8,128)(2,1)S(1)} %bitcast.10), channel_id=1, source_target_pairs={{0,16},{16,0},{1,17},{17,1},{2,18},{18,2},{3,19},{19,3},{4,20},{20... | collective-permute-start | bytes 6291464 | tf_op jit(solution)/shard_map/finish/ppermute | solution.py:354
  143.9 0.1 pad_add_fusion.1.s_ref
  143.9 0.1 pad_add_fusion.s_ref
  144.0 5.4 %finish.2 = (bf16[512,8192]{1,0:T(8,128)(2,1)}, f32[512,256]{1,0:T(8,128)}) custom-call(s32[2]{0:T(128)S(1)} %pad_add_fusion.1.s_ref, bf16[512,256]{1,0:T(8,128)(2,1)} %get-tuple-element.41.w_ref, f32[256,256]{1,0:T(8,128)} %get-tuple-element.42.inv_ref, bf16[4,16,16,1024]{3,2,1,0:T(8,128)(2,1)S(1)} %bitcast.11, ...), custom_call_target="tpu_custom_call" | custom-call | flops 1073741824 | bytes 10485760 | tf_op jit(solution)/shard_map/finish/pallas_call | solution.py:333
  149.4 0.0 collective-permute-done.16.t_ref
  149.4 5.6 %finish.3 = (bf16[512,8192]{1,0:T(8,128)(2,1)}, f32[512,256]{1,0:T(8,128)}) custom-call(s32[2]{0:T(128)S(1)} %pad_add_fusion.s_ref, bf16[512,256]{1,0:T(8,128)(2,1)} %get-tuple-element.41.w_ref, f32[256,256]{1,0:T(8,128)} %get-tuple-element.42.inv_ref, ...), custom_call_target="tpu_custom_call", output_to_operand_aliasing={{0}: (8, {}), {1}: (9, {})} | custom-call | flops 1073741824 | bytes 10485760 | tf_op jit(solution)/shard_map/finish/pallas_call | solution.py:333
  (6 shorter events, 0.2 us)
Async XLA Ops:
  0.6 1.0 copy-start
  3.2 35.5 %all-to-all-start = ((bf16[16,256,256]{2,1,0:T(8,128)(2,1)}), bf16[16,256,256]{2,1,0:T(8,128)(2,1)S(1)}, u32[]{:S(2)}, u32[]{:S(2)}) async-start(bf16[16,256,256]{2,1,0:T(8,128)(2,1)} %broadcast_in_dim.4), calls=%async_computation | async-start | bytes 4194304 | tf_op jit(solution)/shard_map/query_gather/all_to_all | solution.py:375
  20.5 3.5 %collective-permute-start = (bf16[512,1024]{1,0:T(8,128)(2,1)}, bf16[512,1024]{1,0:T(8,128)(2,1)S(1)}, u32[]{:S(2)}, u32[]{:S(2)}) collective-permute-start(bf16[512,1024]{1,0:T(8,128)(2,1)} %get-tuple-element.26.refs_0_), channel_id=1, source_target_pairs={{0,16},{16,0},{1,17},{17,1},{2,18},{18,2},{3,19},{19,3},{4,20},{20... | collective-permute-start | bytes 3145736 | tf_op jit(solution)/shard_map/adjust/ppermute | solution.py:354
  21.5 4.0 %collective-permute-start.1 = (bf16[512,1024]{1,0:T(8,128)(2,1)}, bf16[512,1024]{1,0:T(8,128)(2,1)S(1)}, u32[]{:S(2)}, u32[]{:S(2)}) collective-permute-start(bf16[512,1024]{1,0:T(8,128)(2,1)} %get-tuple-element.27.refs_1_), channel_id=1, source_target_pairs={{0,16},{16,0},{1,17},{17,1},{2,18},{18,2},{3,19},{19,3},{4,20},{20... | collective-permute-start | bytes 3145736 | tf_op jit(solution)/shard_map/adjust/ppermute | solution.py:354
  21.6 5.4 %collective-permute-start.2 = (bf16[512,1024]{1,0:T(8,128)(2,1)}, bf16[512,1024]{1,0:T(8,128)(2,1)S(1)}, u32[]{:S(2)}, u32[]{:S(2)}) collective-permute-start(bf16[512,1024]{1,0:T(8,128)(2,1)} %get-tuple-element.28.refs_2_), channel_id=1, source_target_pairs={{0,16},{16,0},{1,17},{17,1},{2,18},{18,2},{3,19},{19,3},{4,20},{20... | collective-permute-start | bytes 3145736 | tf_op jit(solution)/shard_map/adjust/ppermute | solution.py:354
  22.1 6.5 %collective-permute-start.3 = (bf16[512,1024]{1,0:T(8,128)(2,1)}, bf16[512,1024]{1,0:T(8,128)(2,1)S(1)}, u32[]{:S(2)}, u32[]{:S(2)}) collective-permute-start(bf16[512,1024]{1,0:T(8,128)(2,1)} %get-tuple-element.29.refs_3_), channel_id=1, source_target_pairs={{0,16},{16,0},{1,17},{17,1},{2,18},{18,2},{3,19},{19,3},{4,20},{20... | collective-permute-start | bytes 3145736 | tf_op jit(solution)/shard_map/adjust/ppermute | solution.py:354
  24.0 4.5 %copy-start.1 = (bf16[512,1024]{1,0:T(8,128)(2,1)}, bf16[512,1024]{1,0:T(8,128)(2,1)S(1)}, u32[]{:S(2)}) copy-start(bf16[512,1024]{1,0:T(8,128)(2,1)S(1)} %collective-permute-done.refs_0_) | copy-start | bytes 3145732
  25.5 3.0 %copy-start.2 = (bf16[512,1024]{1,0:T(8,128)(2,1)}, bf16[512,1024]{1,0:T(8,128)(2,1)S(1)}, u32[]{:S(2)}) copy-start(bf16[512,1024]{1,0:T(8,128)(2,1)S(1)} %collective-permute-done.1.refs_1_) | copy-start | bytes 3145732
  27.0 1.5 copy-start.3
  28.5 1.0 copy-start.4
  42.5 4.7 %collective-permute-start.4 = (f32[256,256]{1,0:T(8,128)S(1)}, f32[256,256]{1,0:T(8,128)S(1)}, u32[]{:S(2)}, u32[]{:S(2)}) collective-permute-start(f32[256,256]{1,0:T(8,128)S(1)} %get-tuple-element.31), channel_id=1, source_target_pairs={{0,16},{16,0},{1,17},{17,1},{2,18},{18,2},{3,19},{19,3},{4,20},{20... | collective-permute-start | bytes 786440 | tf_op jit(solution)/shard_map/project/ppermute | solution.py:354
  47.2 6.3 %collective-permute-start.7 = (bf16[256,256]{1,0:T(8,128)(2,1)S(1)}, bf16[256,256]{1,0:T(8,128)(2,1)S(1)}, u32[]{:S(2)}, u32[]{:S(2)}) collective-permute-start(bf16[256,256]{1,0:T(8,128)(2,1)S(1)} %add_convert_fusion.1), channel_id=1, source_target_pairs={{0,96},{32,0},{64,32},{96,64},{1,97},{33,1},{65,33},{97,65},{2,98}... | collective-permute-start | bytes 393224 | tf_op jit(solution)/shard_map/project/ppermute | solution.py:358
  51.1 8.8 %collective-permute-start.6 = (bf16[256,256]{1,0:T(8,128)(2,1)S(1)}, bf16[256,256]{1,0:T(8,128)(2,1)S(1)}, u32[]{:S(2)}, u32[]{:S(2)}) collective-permute-start(bf16[256,256]{1,0:T(8,128)(2,1)S(1)} %add_convert_fusion.1), channel_id=1, source_target_pairs={{0,32},{32,64},{64,96},{96,0},{1,33},{33,65},{65,97},{97,1},{2,34}... | collective-permute-start | bytes 393224 | tf_op jit(solution)/shard_map/project/ppermute | solution.py:358
  51.1 8.8 %collective-permute-start.5 = (bf16[256,256]{1,0:T(8,128)(2,1)S(1)}, bf16[256,256]{1,0:T(8,128)(2,1)S(1)}, u32[]{:S(2)}, u32[]{:S(2)}) collective-permute-start(bf16[256,256]{1,0:T(8,128)(2,1)S(1)} %add_convert_fusion.1), channel_id=1, source_target_pairs={{0,64},{32,96},{64,0},{96,32},{1,65},{33,97},{65,1},{97,33},{2,66}... | collective-permute-start | bytes 393224 | tf_op jit(solution)/shard_map/project/ppermute | solution.py:358
  59.9 2.2 %collective-permute-start.8 = (bf16[256,256]{1,0:T(8,128)(2,1)S(1)}, bf16[256,256]{1,0:T(8,128)(2,1)S(1)}, u32[]{:S(2)}, u32[]{:S(2)}) collective-permute-start(bf16[256,256]{1,0:T(8,128)(2,1)S(1)} %add_convert_fusion.mine_ref), channel_id=1, source_target_pairs={{0,16},{16,0},{1,17},{17,1},{2,18},{18,2},{3,19},{19,3},{4,20},{20... | collective-permute-start | bytes 393224 | tf_op jit(solution)/shard_map/gram/ppermute | solution.py:354
  63.0 6.1 %collective-permute-start.11 = (bf16[128,256]{1,0:T(8,128)(2,1)S(1)}, bf16[128,256]{1,0:T(8,128)(2,1)S(1)}, u32[]{:S(2)}, u32[]{:S(2)}) collective-permute-start(bf16[128,256]{1,0:T(8,128)(2,1)S(1)} %get-tuple-element.33), channel_id=1, source_target_pairs={{0,12},{4,0},{8,4},{12,8},{1,13},{5,1},{9,5},{13,9},{2,14},{6,2},{... | collective-permute-start | bytes 196616 | tf_op jit(solution)/shard_map/gram/ppermute | solution.py:358
  63.1 5.9 %collective-permute-start.10 = (bf16[128,256]{1,0:T(8,128)(2,1)S(1)}, bf16[128,256]{1,0:T(8,128)(2,1)S(1)}, u32[]{:S(2)}, u32[]{:S(2)}) collective-permute-start(bf16[128,256]{1,0:T(8,128)(2,1)S(1)} %get-tuple-element.33), channel_id=1, source_target_pairs={{0,4},{4,8},{8,12},{12,0},{1,5},{5,9},{9,13},{13,1},{2,6},{6,10},{... | collective-permute-start | bytes 196616 | tf_op jit(solution)/shard_map/gram/ppermute | solution.py:358
  64.4 4.7 %collective-permute-start.9 = (bf16[128,256]{1,0:T(8,128)(2,1)S(1)}, bf16[128,256]{1,0:T(8,128)(2,1)S(1)}, u32[]{:S(2)}, u32[]{:S(2)}) collective-permute-start(bf16[128,256]{1,0:T(8,128)(2,1)S(1)} %get-tuple-element.33), channel_id=1, source_target_pairs={{0,8},{4,12},{8,0},{12,4},{1,9},{5,13},{9,1},{13,5},{2,10},{6,14},... | collective-permute-start | bytes 196616 | tf_op jit(solution)/shard_map/gram/ppermute | solution.py:358
  69.2 32.0 %all-to-all-start.1 = ((bf16[64,16,1024]{2,1,0:T(8,128)(2,1)}), bf16[64,16,1024]{2,1,0:T(8,128)(2,1)S(1)}, u32[]{:S(2)}, u32[]{:S(2)}) async-start(bf16[64,16,1024]{2,1,0:T(8,128)(2,1)} %bitcast.15), calls=%async_computation.1 | async-start | bytes 4194304 | tf_op jit(solution)/shard_map/term/all_to_all | solution.py:393
  73.9 15.6 %collective-permute-start.13 = (bf16[128,256]{1,0:T(8,128)(2,1)S(1)}, bf16[128,256]{1,0:T(8,128)(2,1)S(1)}, u32[]{:S(2)}, u32[]{:S(2)}) collective-permute-start(bf16[128,256]{1,0:T(8,128)(2,1)S(1)} %add_add_fusion.1), channel_id=1, source_target_pairs={{0,1},{1,2},{2,3},{3,0},{4,5},{5,6},{6,7},{7,4},{8,9},{9,10},{10,1... | collective-permute-start | bytes 196616 | tf_op jit(solution)/shard_map/gather/ppermute | solution.py:358
  75.1 22.4 %collective-permute-start.12 = (bf16[128,256]{1,0:T(8,128)(2,1)S(1)}, bf16[128,256]{1,0:T(8,128)(2,1)S(1)}, u32[]{:S(2)}, u32[]{:S(2)}) collective-permute-start(bf16[128,256]{1,0:T(8,128)(2,1)S(1)} %add_add_fusion.1), channel_id=1, source_target_pairs={{0,2},{1,3},{2,0},{3,1},{4,6},{5,7},{6,4},{7,5},{8,10},{9,11},{10,... | collective-permute-start | bytes 196616 | tf_op jit(solution)/shard_map/gather/ppermute | solution.py:358
  77.5 20.0 %collective-permute-start.14 = (bf16[128,256]{1,0:T(8,128)(2,1)S(1)}, bf16[128,256]{1,0:T(8,128)(2,1)S(1)}, u32[]{:S(2)}, u32[]{:S(2)}) collective-permute-start(bf16[128,256]{1,0:T(8,128)(2,1)S(1)} %add_add_fusion.1), channel_id=1, source_target_pairs={{0,3},{1,0},{2,1},{3,2},{4,7},{5,4},{6,5},{7,6},{8,11},{9,8},{10,9... | collective-permute-start | bytes 196616 | tf_op jit(solution)/shard_map/gather/ppermute | solution.py:358
  102.9 10.4 %collective-permute-start.15 = (f32[128,256]{1,0:T(8,128)S(1)}, f32[128,256]{1,0:T(8,128)S(1)}, u32[]{:S(2)}, u32[]{:S(2)}) collective-permute-start(f32[128,256]{1,0:T(8,128)S(1)} %add_add_fusion), channel_id=1, source_target_pairs={{0,16},{16,0},{1,17},{17,1},{2,18},{18,2},{3,19},{19,3},{4,20},{20... | collective-permute-start | bytes 393224 | tf_op jit(solution)/shard_map/solve/ppermute | solution.py:354
  106.4 35.7 %all-to-all-start.2 = ((bf16[64,16,1024]{2,1,0:T(8,128)(2,1)}), bf16[64,16,1024]{2,1,0:T(8,128)(2,1)S(1)}, u32[]{:S(2)}, u32[]{:S(2)}) async-start(bf16[64,16,1024]{2,1,0:T(8,128)(2,1)} %gather.1), calls=%async_computation.2 | async-start | bytes 4194304 | tf_op jit(solution)/shard_map/gather/all_to_all | solution.py:398
  142.1 7.3 %collective-permute-start.16 = (bf16[4,16,16,1024]{3,2,1,0:T(8,128)(2,1)S(1)}, bf16[4,16,16,1024]{3,2,1,0:T(8,128)(2,1)}, u32[]{:S(2)}, u32[]{:S(2)}) collective-permute-start(bf16[4,16,16,1024]{3,2,1,0:T(8,128)(2,1)S(1)} %bitcast.10), channel_id=1, source_target_pairs={{0,16},{16,0},{1,17},{17,1},{2,18},{18,2},{3,19},{19,3},{4,20},{20... | collective-permute-start | bytes 6291464 | tf_op jit(solution)/shard_map/finish/ppermute | solution.py:354

commit v5 on v4

--- a/solution.py
+++ b/solution.py
@@ -42,23 +42,20 @@
     return copies
 
 
-class Stream:
-    DEPTH = 4
-
-    def __init__(self, groups, sem):
-        self.groups, self.sem, self.started = groups, sem, []
-        for _ in range(self.DEPTH):
-            self.more()
-
-    def more(self):
-        k = len(self.started)
-        if k < len(self.groups):
-            self.started.append(load(self.groups[k], self.sem, sum(len(g) for g in self.groups[:k])))
-
-    def get(self, k):
-        for copy in self.started[k]:
-            copy.wait()
-        self.more()
+def arrived(dst, sem):
+    pltpu.make_async_copy(dst, dst, sem).wait()
+
+
+def rolled(count, step):
+    def body(k, carry):
+        step(k)
+        return carry
+
+    lax.fori_loop(0, count, body, 0)
+
+
+def aligned(start, size):
+    return pl.ds(pl.multiple_of(start, size), size)
 
 
 def pick(c, first, second):
@@ -67,23 +64,33 @@
 
 def adjust_kernel(c_ref, g_ref, d_ref, own_ref, *refs):
     chunks, (g, d, own, other, sem) = refs[:CHUNKS], refs[CHUNKS:]
-    wide = [slice(2 * k * STEP, 2 * (k + 1) * STEP) for k in range(STEPS)]
-    stream = Stream([[(g_ref.at[:, cut], g.at[k]), (d_ref.at[:, cut], d.at[k])] for k, cut in enumerate(wide)], sem)
+    for k in range(STEPS):
+        cut = slice(2 * k * STEP, 2 * (k + 1) * STEP)
+        load([(g_ref.at[:, cut], g.at[k]), (d_ref.at[:, cut], d.at[k])], sem, 2 * k)
     c = c_ref[0]
-    sends = []
-    for k in range(STEPS):
-        stream.get(k)
+
+    def step(k):
+        arrived(g.at[k], sem.at[2 * k])
+        arrived(d.at[k], sem.at[2 * k + 1])
         for s in range(STEP // SUB):
             part = slice(s * SUB, (s + 1) * SUB)
             for out, core in ((own, c), (other, 1 - c)):
-                cut = pl.ds(pl.multiple_of(s * BLK + core * SUB, SUB), SUB)
+                cut = aligned(s * BLK + core * SUB, SUB)
                 out[k, :, part] = (g[k, :, cut].astype(F32) + d[k, :, cut].astype(F32)).astype(BF16)
-        cut = slice(k * STEP, (k + 1) * STEP)
-        part = slice(k % 2 * STEP, (k % 2 + 1) * STEP)
-        pairs = [(own.at[k], own_ref.at[:, cut]), (other.at[k], chunks[k // 2].at[:, part])]
-        sends += load(pairs, sem, 2 * STEPS + 2 * k)
-    for send in sends:
-        send.wait()
+        load([(own.at[k], own_ref.at[:, aligned(k * STEP, STEP)])], sem, 2 * STEPS + k)
+        for i, ref in enumerate(chunks):
+
+            @pl.when(k // 2 == i)
+            def _():
+                load([(other.at[k], ref.at[:, aligned(k % 2 * STEP, STEP)])], sem, 3 * STEPS + k)
+
+    rolled(STEPS, step)
+
+    def sent(k):
+        arrived(own.at[k], sem.at[2 * STEPS + k])
+        arrived(other.at[k], sem.at[3 * STEPS + k])
+
+    rolled(STEPS, sent)
 
 
 def adjust(c, gradient, error):
@@ -102,17 +109,18 @@
 
 def pair_kernel(own_ref, *refs):
     chunks, (o_ref, a, b, sem) = refs[:CHUNKS], refs[CHUNKS:]
-    cuts = [slice(k * STEP, (k + 1) * STEP) for k in range(STEPS)]
-    parts = [slice(k % 2 * STEP, (k % 2 + 1) * STEP) for k in range(STEPS)]
-    groups = [[(own_ref.at[:, cuts[k]], a.at[k]), (chunks[k // 2].at[:, parts[k]], b.at[k])] for k in range(STEPS)]
-    stream = Stream(groups, sem)
-    sends = []
-    for k, cut in enumerate(cuts):
-        stream.get(k)
+    for k in range(STEPS):
+        part = slice(k % 2 * STEP, (k % 2 + 1) * STEP)
+        load([(own_ref.at[:, k * STEP : (k + 1) * STEP], a.at[k]), (chunks[k // 2].at[:, part], b.at[k])], sem, 2 * k)
+
+    def step(k):
+        arrived(a.at[k], sem.at[2 * k])
+        arrived(b.at[k], sem.at[2 * k + 1])
         a[k] = (a[k].astype(F32) + b[k].astype(F32)).astype(BF16)
-        sends += load([(a.at[k], o_ref.at[:, cut])], sem, 2 * STEPS + k)
-    for send in sends:
-        send.wait()
+        load([(a.at[k], o_ref.at[:, aligned(k * STEP, STEP)])], sem, 2 * STEPS + k)
+
+    rolled(STEPS, step)
+    rolled(STEPS, lambda k: arrived(a.at[k], sem.at[2 * STEPS + k]))
 
 
 def pair(own, chunks):
@@ -128,15 +136,18 @@
 
 
 def project_kernel(c_ref, q_ref, a_ref, keep_ref, give_ref, acc, a, sem):
-    cuts = [slice(k * CHUNK, (k + 1) * CHUNK) for k in range(CHUNKS)]
-    stream = Stream([[(a_ref.at[:, cut], a.at[:, cut])] for cut in cuts], sem)
-    for k, cut in enumerate(cuts):
-        stream.get(k)
-        x = jnp.dot(a[:, cut], q_ref[cut, :], preferred_element_type=F32)
-        acc[...] = x if k == 0 else acc[...] + x
+    for k in range(CHUNKS):
+        load([(a_ref.at[:, k * CHUNK : (k + 1) * CHUNK], a.at[k])], sem, k)
+    acc[...] = jnp.zeros_like(acc)
+
+    def step(k):
+        arrived(a.at[k], sem.at[k])
+        acc[...] += jnp.dot(a[k], q_ref[aligned(k * CHUNK, CHUNK), :], preferred_element_type=F32)
+
+    rolled(CHUNKS, step)
     c, h = c_ref[0], ROWS // 2
-    keep_ref[...] = acc[pl.ds(pl.multiple_of(c * h, h), h), :]
-    give_ref[...] = acc[pl.ds(pl.multiple_of((1 - c) * h, h), h), :]
+    keep_ref[...] = acc[aligned(c * h, h), :]
+    give_ref[...] = acc[aligned((1 - c) * h, h), :]
 
 
 def project(c, query, a):
@@ -148,7 +159,7 @@
         out_shape=[out, out],
         scratch_shapes=[
             pltpu.VMEM((ROWS, RANK), F32),
-            pltpu.VMEM((ROWS, HALF), BF16),
+            pltpu.VMEM((CHUNKS, ROWS, CHUNK), BF16),
             pltpu.SemaphoreType.DMA((CHUNKS,)),
         ],
         compiler_params=params(),
@@ -186,17 +197,17 @@
 
 
 def term_kernel(st_ref, a_ref, t_ref, a, t, sem):
-    cuts = [slice(k * CHUNK, (k + 1) * CHUNK) for k in range(CHUNKS)]
-    stream = Stream([[(a_ref.at[:, cut], a.at[k])] for k, cut in enumerate(cuts)], sem)
-    st = st_ref[...]
-    sends = []
     for k in range(CHUNKS):
-        stream.get(k)
-        x = jnp.dot(st, a[k], preferred_element_type=F32)
+        load([(a_ref.at[:, k * CHUNK : (k + 1) * CHUNK], a.at[k])], sem, k)
+
+    def step(k):
+        arrived(a.at[k], sem.at[k])
+        x = jnp.dot(st_ref[...], a[k], preferred_element_type=F32)
         t[k] = x.astype(BF16).reshape(NM, GROUP, CHUNK)
-        sends += load([(t.at[k], t_ref.at[k])], sem, CHUNKS + k)
-    for send in sends:
-        send.wait()
+        load([(t.at[k], t_ref.at[k])], sem, CHUNKS + k)
+
+    rolled(CHUNKS, step)
+    rolled(CHUNKS, lambda k: arrived(t.at[k], sem.at[CHUNKS + k]))
 
 
 def term(st, a):
@@ -296,36 +307,43 @@
 
 
 def finish_kernel(held, s_ref, w_ref, inv_ref, t_ref, *refs):
-    ins, (err_ref, f_ref, t, a, out, f, w_in, inv_in, sem) = refs[:-9], refs[-9:]
+    ins, (err_ref, f_ref, t, a, out, f, w, inv, sem) = refs[:-9], refs[-9:]
     core, m = s_ref[0], s_ref[1]
-    t = t_ref if held else t
     if ins[0].shape[1] == HALF:
         parts = [ins[0].at[:, k * CHUNK : (k + 1) * CHUNK] for k in range(CHUNKS)]
     else:
         parts = ins[:CHUNKS]
-    first = load([(w_ref, w_in)], sem)
-    groups = [[(parts[k], a.at[k])] for k in range(CHUNKS)]
-    if t is not t_ref:
-        groups = [[(t_ref.at[k], t.at[k])] + group for k, group in enumerate(groups)]
-    stream = Stream(groups, sem.at[pl.ds(2, 2 * CHUNKS)])
-    first += load([(inv_ref, inv_in)], sem, 1)
-    first[0].wait()
-    w = w_in[...]
-    sends, at = [], 2 + 2 * CHUNKS
+    small = load([(w_ref, w), (inv_ref, inv)], sem)
     for k in range(CHUNKS):
-        stream.get(k)
-        x = jnp.dot(w, t[k].reshape(RANK, CHUNK), preferred_element_type=F32)
+        if not held:
+            load([(t_ref.at[k], t.at[k])], sem, 2 + k)
+        load([(parts[k], a.at[k])], sem, 2 + CHUNKS + k)
+    t = t_ref if held else t
+    at, per = 2 + 2 * CHUNKS, CHUNK // SUB
+    for copy in small:
+        copy.wait()
+
+    def step(k):
+        if not held:
+            arrived(t.at[k], sem.at[2 + k])
+        arrived(a.at[k], sem.at[2 + CHUNKS + k])
+        x = jnp.dot(w[...], t[k].reshape(RANK, CHUNK), preferred_element_type=F32)
         out[k] = (a[k].astype(F32) - x).astype(BF16)
-        for s in range(CHUNK // SUB):
-            to = pl.ds(pl.multiple_of((k * (CHUNK // SUB) + s) * BLK + core * SUB, SUB), SUB)
-            sends += load([(out.at[k, :, s * SUB : (s + 1) * SUB], err_ref.at[:, to])], sem, at + len(sends))
-    first[1].wait()
-    per = CHUNK // SUB
-    x = t[m // per, :, :, pl.ds(pl.multiple_of(m % per * SUB, SUB), SUB)].reshape(RANK, SUB)
-    f[...] = dot_hi(inv_in[...], x.astype(F32)).T * 0.125
-    sends += load([(f, f_ref.at[pl.ds(pl.multiple_of(core * SUB, SUB), SUB)])], sem, at + len(sends))
-    for send in sends:
-        send.wait()
+        for s in range(per):
+            to = aligned((k * per + s) * BLK + core * SUB, SUB)
+            load([(out.at[k, :, s * SUB : (s + 1) * SUB], err_ref.at[:, to])], sem, at + k * per + s)
+
+    rolled(CHUNKS, step)
+    x = t[m // per, :, :, aligned(m % per * SUB, SUB)].reshape(RANK, SUB)
+    f[...] = dot_hi(inv[...], x.astype(F32)).T * 0.125
+    last = load([(f, f_ref.at[aligned(core * SUB, SUB)])], sem, at + CHUNKS * per)
+
+    def sent(k):
+        for s in range(per):
+            arrived(out.at[k, :, s * SUB : (s + 1) * SUB], sem.at[at + k * per + s])
+
+    rolled(CHUNKS, sent)
+    last[0].wait()
 
 
 def finish(held, where, w, inv, t, parts, before=()):

time: 156 us -> 154 us (0.987)
  transfers between devices with their start and end apart: 20 -> 20, of which waited for: 14 -> 14; matrix products, arithmetic and copies ran while one was open for 0% -> 0% of each run, Pallas kernels for 24% -> 23%
where the time goes in v5:
time: 154 us
  waiting for transfers between devices  59.1 us (38%)
  Pallas kernels  47.1 us (31%)
  starting transfers between devices  42.9 us (28%)
  local copies, waits for them, and re-layouts  3.51 us (2%)
    ppermute x9, waiting for transfers between devices, ring_sum(): lax.ppermute(x, axis, [(i, (i + k) % 4) for i in range(4)])  26.7 us
    all_to_all x1, waiting for transfers between devices, shards(): mine = lax.all_to_all(sums, ('z', 'x', 'y'), 0, 0, tiled=True)  16.4 us
    pallas_call x1, Pallas kernels, solve(): pl.pallas_call(solve_kernel, grid=(1,), in_specs=[VMEM, tall], out_specs=...  12.1 us
    ppermute x9, starting transfers between devices, ring_sum(): lax.ppermute(x, axis, [(i, (i + k) % 4) for i in range(4)])  11.9 us
    ppermute x8, starting transfers between devices, swap(): return lax.ppermute(x, 'c', [(0, 1), (1, 0)])  11.6 us
    pallas_call x2, Pallas kernels, finish(): pl.pallas_call(functools.partial(finish_kernel, held), in_specs=[SMEM, HB...  10.5 us
    pallas_call x1, Pallas kernels, adjust(): pl.pallas_call(adjust_kernel, in_specs=[SMEM, HBM, HBM], out_specs=[HBM]...  9.6 us
    ppermute x8, waiting for transfers between devices, swap(): return lax.ppermute(x, 'c', [(0, 1), (1, 0)])  8.54 us
  transfers between devices with their start and end apart: 20, of which 14 were waited for; matrix products, arithmetic and copies ran while one was open for 0% of the time, Pallas kernels for 23%

profile of v5, /device:TPU:1, one launch (start us, length us, event | category | flops | bytes accessed | tf_op | source)
XLA Modules:
  0.0 153.9 jit_solution(2884301670798772865)
XLA Ops:
  0.6 0.0 copy-start
  0.7 0.9 copy-done
  1.6 1.6 %broadcast_in_dim.4 = bf16[16,256,256]{2,1,0:T(8,128)(2,1)} broadcast(bf16[256,256]{1,0:T(8,128)(2,1)S(1)} %constant_dynamic-slice_fusion), dimensions={1,2} | broadcast | bytes 2228224 | tf_op jit(solution)/shard_map/query_gather/broadcast_in_dim | solution.py:392
  3.2 7.6 %all-to-all-start = ((bf16[16,256,256]{2,1,0:T(8,128)(2,1)}), bf16[16,256,256]{2,1,0:T(8,128)(2,1)S(1)}, u32[]{:S(2)}, u32[]{:S(2)}) async-start(bf16[16,256,256]{2,1,0:T(8,128)(2,1)} %broadcast_in_dim.4), calls=%async_computation | async-start | bytes 4194304 | tf_op jit(solution)/shard_map/query_gather/all_to_all | solution.py:393
  10.8 9.6 %adjust.2 = (bf16[512,4096]{1,0:T(8,128)(2,1)}, bf16[512,1024]{1,0:T(8,128)(2,1)}, bf16[512,1024]{1,0:T(8,128)(2,1)}, bf16[512,1024]{1,0:T(8,128)(2,1)}, bf16[512,1024]{1,0:T(8,128)(2,1)}) custom-call(s32[1]{0:T(128)} %bitcast.2.c_ref, bf16[512,8192]{1,0:T(8,128)(2,1)} %bitcast.12, bf16[512,8192]{1,0:T(8,128)(2,1)} %bitcast.13), custom_call_target="tpu_custom_call" | custom-call | flops 4194304 | bytes 25165824 | tf_op jit(solution)/shard_map/adjust/pallas_call | solution.py:97
  20.4 1.0 collective-permute-start
  21.4 0.1 collective-permute-start.1
  21.5 0.4 collective-permute-start.2
  21.9 0.1 collective-permute-start.3
  22.0 1.9 %collective-permute-done.refs_0_ = bf16[512,1024]{1,0:T(8,128)(2,1)S(1)} collective-permute-done((bf16[512,1024]{1,0:T(8,128)(2,1)}, bf16[512,1024]{1,0:T(8,128)(2,1)S(1)}, u32[]{:S(2)}, u32[]{:S(2)}) %collective-permute-start) | collective-permute-done | bytes 1048608 | tf_op jit(solution)/shard_map/adjust/ppermute | solution.py:372
  23.9 0.0 copy-start.1
  23.9 1.5 collective-permute-done.1.refs_1_
  25.4 0.0 copy-start.2
  25.4 1.5 collective-permute-done.2.refs_2_
  26.9 0.0 copy-start.3
  26.9 1.5 collective-permute-done.3.refs_3_
  28.4 0.0 copy-start.4
  28.4 0.0 copy-done.1
  28.4 0.0 copy-done.2
  28.4 0.0 copy-done.3
  28.4 1.0 copy-done.4
  29.4 5.5 %adjust.3.a_ref = bf16[512,4096]{1,0:T(8,128)(2,1)} custom-call(bf16[512,4096]{1,0:T(8,128)(2,1)} %get-tuple-element.25.own_ref.refs_0_, bf16[512,1024]{1,0:T(8,128)(2,1)} %copy-done.1, bf16[512,1024]{1,0:T(8,128)(2,1)} %copy-done.2, bf16[512,1024]{1,0:T(8,128)(2,1)} %copy-done.3, bf16[512,1024]{1,0:T(8,128)(2,1)} %copy-done.4), custom_call_target="tpu_custom_call" | custom-call | flops 2097152 | bytes 12582912 | tf_op jit(solution)/shard_map/adjust/pallas_call | solution.py:127
  34.9 3.8 %all-to-all-done = bf16[16,256,256]{2,1,0:T(8,128)(2,1)S(1)} async-done(((bf16[16,256,256]{2,1,0:T(8,128)(2,1)}), bf16[16,256,256]{2,1,0:T(8,128)(2,1)S(1)}, u32[]{:S(2)}, u32[]{:S(2)}) %all-to-all-start) | async-done | bytes 2097184 | tf_op jit(solution)/shard_map/query_gather/all_to_all | solution.py:393
  38.7 3.1 %project.1 = (f32[256,256]{1,0:T(8,128)S(1)}, f32[256,256]{1,0:T(8,128)S(1)}) custom-call(s32[1]{0:T(128)} %bitcast.2.c_ref, bf16[4096,256]{1,0:T(8,128)(2,1)S(1)} %bitcast.9, bf16[512,4096]{1,0:T(8,128)(2,1)} %adjust.3.a_ref), custom_call_target="tpu_custom_call" | custom-call | flops 1073741824 | bytes 6291456 | tf_op jit(solution)/shard_map/project/pallas_call | solution.py:155
  41.7 3.5 %collective-permute-start.4 = (f32[256,256]{1,0:T(8,128)S(1)}, f32[256,256]{1,0:T(8,128)S(1)}, u32[]{:S(2)}, u32[]{:S(2)}) collective-permute-start(f32[256,256]{1,0:T(8,128)S(1)} %get-tuple-element.31), channel_id=1, source_target_pairs={{0,16},{16,0},{1,17},{17,1},{2,18},{18,2},{3,19},{19,3},{4,20},{20... | collective-permute-start | bytes 786440 | tf_op jit(solution)/shard_map/project/ppermute | solution.py:372
  45.3 1.2 collective-permute-done.4
  46.5 3.8 %collective-permute-start.7 = (bf16[256,256]{1,0:T(8,128)(2,1)S(1)}, bf16[256,256]{1,0:T(8,128)(2,1)S(1)}, u32[]{:S(2)}, u32[]{:S(2)}) collective-permute-start(bf16[256,256]{1,0:T(8,128)(2,1)S(1)} %add_convert_fusion.1), channel_id=1, source_target_pairs={{0,96},{32,0},{64,32},{96,64},{1,97},{33,1},{65,33},{97,65},{2,98}... | collective-permute-start | bytes 393224 | tf_op jit(solution)/shard_map/project/ppermute | solution.py:376
  50.3 0.0 collective-permute-start.6
  50.3 1.3 collective-permute-start.5
  51.6 1.2 collective-permute-done.7
  52.8 6.3 %collective-permute-done.6 = bf16[256,256]{1,0:T(8,128)(2,1)S(1)} collective-permute-done((bf16[256,256]{1,0:T(8,128)(2,1)S(1)}, bf16[256,256]{1,0:T(8,128)(2,1)S(1)}, u32[]{:S(2)}, u32[]{:S(2)}) %collective-permute-start.6) | collective-permute-done | bytes 131104 | tf_op jit(solution)/shard_map/project/ppermute | solution.py:376
  59.1 0.0 collective-permute-done.5
  59.1 0.1 add_convert_fusion.mine_ref
  59.2 1.2 collective-permute-start.8
  60.4 1.0 collective-permute-done.8.theirs_ref
  61.4 0.8 gram.1
  62.2 0.1 collective-permute-start.11
  62.3 1.3 collective-permute-start.10
  63.7 0.7 collective-permute-start.9
  64.4 3.9 %term.1 = bf16[4,16,16,1024]{3,2,1,0:T(8,128)(2,1)} custom-call(bf16[256,512]{1,0:T(8,128)(2,1)S(1)} %get-tuple-element.32.st_ref, bf16[512,4096]{1,0:T(8,128)(2,1)} %adjust.3.a_ref), custom_call_target="tpu_custom_call" | custom-call | flops 1073741824 | bytes 6291456 | tf_op jit(solution)/shard_map/term/pallas_call | solution.py:214
  68.3 0.0 collective-permute-done.11
  68.3 0.0 collective-permute-done.10
  68.3 0.1 collective-permute-done.9
  68.4 4.7 %all-to-all-start.1 = ((bf16[64,16,1024]{2,1,0:T(8,128)(2,1)}), bf16[64,16,1024]{2,1,0:T(8,128)(2,1)S(1)}, u32[]{:S(2)}, u32[]{:S(2)}) async-start(bf16[64,16,1024]{2,1,0:T(8,128)(2,1)} %bitcast.15), calls=%async_computation.1 | async-start | bytes 4194304 | tf_op jit(solution)/shard_map/term/all_to_all | solution.py:411
  73.1 1.0 collective-permute-start.13
  74.1 2.4 %collective-permute-start.12 = (bf16[128,256]{1,0:T(8,128)(2,1)S(1)}, bf16[128,256]{1,0:T(8,128)(2,1)S(1)}, u32[]{:S(2)}, u32[]{:S(2)}) collective-permute-start(bf16[128,256]{1,0:T(8,128)(2,1)S(1)} %add_add_fusion.1), channel_id=1, source_target_pairs={{0,2},{1,3},{2,0},{3,1},{4,6},{5,7},{6,4},{7,5},{8,10},{9,11},{10,... | collective-permute-start | bytes 196616 | tf_op jit(solution)/shard_map/gather/ppermute | solution.py:376
  76.5 1.2 collective-permute-start.14
  77.7 11.0 %collective-permute-done.13 = bf16[128,256]{1,0:T(8,128)(2,1)S(1)} collective-permute-done((bf16[128,256]{1,0:T(8,128)(2,1)S(1)}, bf16[128,256]{1,0:T(8,128)(2,1)S(1)}, u32[]{:S(2)}, u32[]{:S(2)}) %collective-permute-start.13) | collective-permute-done | bytes 65568 | tf_op jit(solution)/shard_map/gather/ppermute | solution.py:376
  88.7 8.0 %collective-permute-done.12 = bf16[128,256]{1,0:T(8,128)(2,1)S(1)} collective-permute-done((bf16[128,256]{1,0:T(8,128)(2,1)S(1)}, bf16[128,256]{1,0:T(8,128)(2,1)S(1)}, u32[]{:S(2)}, u32[]{:S(2)}) %collective-permute-start.12) | collective-permute-done | bytes 65568 | tf_op jit(solution)/shard_map/gather/ppermute | solution.py:376
  96.7 0.0 collective-permute-done.14
  96.8 3.7 %all-to-all-done.1.x_ref = bf16[64,16,1024]{2,1,0:T(8,128)(2,1)S(1)} async-done(((bf16[64,16,1024]{2,1,0:T(8,128)(2,1)}), bf16[64,16,1024]{2,1,0:T(8,128)(2,1)S(1)}, u32[]{:S(2)}, u32[]{:S(2)}) %all-to-all-start.1) | async-done | bytes 2097184 | tf_op jit(solution)/shard_map/term/all_to_all | solution.py:411
  100.4 1.7 %gather.1 = bf16[64,16,1024]{2,1,0:T(8,128)(2,1)} custom-call(bf16[64,16,1024]{2,1,0:T(8,128)(2,1)S(1)} %all-to-all-done.1.x_ref), custom_call_target="tpu_custom_call" | custom-call | flops 1048576 | bytes 4194304 | tf_op jit(solution)/shard_map/gather/pallas_call | solution.py:239
  102.1 3.5 %collective-permute-start.15 = (f32[128,256]{1,0:T(8,128)S(1)}, f32[128,256]{1,0:T(8,128)S(1)}, u32[]{:S(2)}, u32[]{:S(2)}) collective-permute-start(f32[128,256]{1,0:T(8,128)S(1)} %add_add_fusion), channel_id=1, source_target_pairs={{0,16},{16,0},{1,17},{17,1},{2,18},{18,2},{3,19},{19,3},{4,20},{20... | collective-permute-start | bytes 393224 | tf_op jit(solution)/shard_map/solve/ppermute | solution.py:372
  105.6 7.1 %all-to-all-start.2 = ((bf16[64,16,1024]{2,1,0:T(8,128)(2,1)}), bf16[64,16,1024]{2,1,0:T(8,128)(2,1)S(1)}, u32[]{:S(2)}, u32[]{:S(2)}) async-start(bf16[64,16,1024]{2,1,0:T(8,128)(2,1)} %gather.1), calls=%async_computation.2 | async-start | bytes 4194304 | tf_op jit(solution)/shard_map/gather/all_to_all | solution.py:416
  112.7 0.0 collective-permute-done.15
  112.8 12.1 %solve.1 = (f32[256,256]{1,0:T(8,128)}, bf16[512,256]{1,0:T(8,128)(2,1)}) custom-call(f32[256,256]{1,0:T(8,128)S(1)} %pad_maximum_fusion.g_ref, bf16[512,256]{1,0:T(8,128)(2,1)} %get-tuple-element.38.s_ref), custom_call_target="tpu_custom_call" | custom-call | flops 20000000000 | bytes 1000000 | tf_op jit(solution)/shard_map/solve/pallas_call | solution.py:298
  124.9 16.4 %all-to-all-done.2 = bf16[64,16,1024]{2,1,0:T(8,128)(2,1)S(1)} async-done(((bf16[64,16,1024]{2,1,0:T(8,128)(2,1)}), bf16[64,16,1024]{2,1,0:T(8,128)(2,1)S(1)}, u32[]{:S(2)}, u32[]{:S(2)}) %all-to-all-start.2) | async-done | bytes 2097184 | tf_op jit(solution)/shard_map/gather/all_to_all | solution.py:416
  141.3 1.8 %collective-permute-start.16 = (bf16[4,16,16,1024]{3,2,1,0:T(8,128)(2,1)S(1)}, bf16[4,16,16,1024]{3,2,1,0:T(8,128)(2,1)}, u32[]{:S(2)}, u32[]{:S(2)}) collective-permute-start(bf16[4,16,16,1024]{3,2,1,0:T(8,128)(2,1)S(1)} %bitcast.10), channel_id=1, source_target_pairs={{0,16},{16,0},{1,17},{17,1},{2,18},{18,2},{3,19},{19,3},{4,20},{20... | collective-permute-start | bytes 6291464 | tf_op jit(solution)/shard_map/finish/ppermute | solution.py:372
  143.1 0.1 pad_add_fusion.1.s_ref
  143.2 0.1 pad_add_fusion.s_ref
  143.2 5.1 %finish.2 = (bf16[512,8192]{1,0:T(8,128)(2,1)}, f32[512,256]{1,0:T(8,128)}) custom-call(s32[2]{0:T(128)S(1)} %pad_add_fusion.1.s_ref, bf16[512,256]{1,0:T(8,128)(2,1)} %get-tuple-element.41.w_ref, f32[256,256]{1,0:T(8,128)} %get-tuple-element.42.inv_ref, bf16[4,16,16,1024]{3,2,1,0:T(8,128)(2,1)S(1)} %bitcast.11, ...), custom_call_target="tpu_custom_call" | custom-call | flops 1073741824 | bytes 10485760 | tf_op jit(solution)/shard_map/finish/pallas_call | solution.py:351
  148.4 0.0 collective-permute-done.16.t_ref
  148.4 5.4 %finish.3 = (bf16[512,8192]{1,0:T(8,128)(2,1)}, f32[512,256]{1,0:T(8,128)}) custom-call(s32[2]{0:T(128)S(1)} %pad_add_fusion.s_ref, bf16[512,256]{1,0:T(8,128)(2,1)} %get-tuple-element.41.w_ref, f32[256,256]{1,0:T(8,128)} %get-tuple-element.42.inv_ref, ...), custom_call_target="tpu_custom_call", output_to_operand_aliasing={{0}: (8, {}), {1}: (9, {})} | custom-call | flops 1073741824 | bytes 10485760 | tf_op jit(solution)/shard_map/finish/pallas_call | solution.py:351
  (6 shorter events, 0.2 us)
Async XLA Ops:
  0.6 1.0 copy-start
  3.2 35.5 %all-to-all-start = ((bf16[16,256,256]{2,1,0:T(8,128)(2,1)}), bf16[16,256,256]{2,1,0:T(8,128)(2,1)S(1)}, u32[]{:S(2)}, u32[]{:S(2)}) async-start(bf16[16,256,256]{2,1,0:T(8,128)(2,1)} %broadcast_in_dim.4), calls=%async_computation | async-start | bytes 4194304 | tf_op jit(solution)/shard_map/query_gather/all_to_all | solution.py:393
  20.4 3.5 %collective-permute-start = (bf16[512,1024]{1,0:T(8,128)(2,1)}, bf16[512,1024]{1,0:T(8,128)(2,1)S(1)}, u32[]{:S(2)}, u32[]{:S(2)}) collective-permute-start(bf16[512,1024]{1,0:T(8,128)(2,1)} %get-tuple-element.26.refs_0_), channel_id=1, source_target_pairs={{0,16},{16,0},{1,17},{17,1},{2,18},{18,2},{3,19},{19,3},{4,20},{20... | collective-permute-start | bytes 3145736 | tf_op jit(solution)/shard_map/adjust/ppermute | solution.py:372
  21.4 4.0 %collective-permute-start.1 = (bf16[512,1024]{1,0:T(8,128)(2,1)}, bf16[512,1024]{1,0:T(8,128)(2,1)S(1)}, u32[]{:S(2)}, u32[]{:S(2)}) collective-permute-start(bf16[512,1024]{1,0:T(8,128)(2,1)} %get-tuple-element.27.refs_1_), channel_id=1, source_target_pairs={{0,16},{16,0},{1,17},{17,1},{2,18},{18,2},{3,19},{19,3},{4,20},{20... | collective-permute-start | bytes 3145736 | tf_op jit(solution)/shard_map/adjust/ppermute | solution.py:372
  21.5 5.4 %collective-permute-start.2 = (bf16[512,1024]{1,0:T(8,128)(2,1)}, bf16[512,1024]{1,0:T(8,128)(2,1)S(1)}, u32[]{:S(2)}, u32[]{:S(2)}) collective-permute-start(bf16[512,1024]{1,0:T(8,128)(2,1)} %get-tuple-element.28.refs_2_), channel_id=1, source_target_pairs={{0,16},{16,0},{1,17},{17,1},{2,18},{18,2},{3,19},{19,3},{4,20},{20... | collective-permute-start | bytes 3145736 | tf_op jit(solution)/shard_map/adjust/ppermute | solution.py:372
  21.9 6.5 %collective-permute-start.3 = (bf16[512,1024]{1,0:T(8,128)(2,1)}, bf16[512,1024]{1,0:T(8,128)(2,1)S(1)}, u32[]{:S(2)}, u32[]{:S(2)}) collective-permute-start(bf16[512,1024]{1,0:T(8,128)(2,1)} %get-tuple-element.29.refs_3_), channel_id=1, source_target_pairs={{0,16},{16,0},{1,17},{17,1},{2,18},{18,2},{3,19},{19,3},{4,20},{20... | collective-permute-start | bytes 3145736 | tf_op jit(solution)/shard_map/adjust/ppermute | solution.py:372
  23.9 4.5 %copy-start.1 = (bf16[512,1024]{1,0:T(8,128)(2,1)}, bf16[512,1024]{1,0:T(8,128)(2,1)S(1)}, u32[]{:S(2)}) copy-start(bf16[512,1024]{1,0:T(8,128)(2,1)S(1)} %collective-permute-done.refs_0_) | copy-start | bytes 3145732
  25.4 3.0 %copy-start.2 = (bf16[512,1024]{1,0:T(8,128)(2,1)}, bf16[512,1024]{1,0:T(8,128)(2,1)S(1)}, u32[]{:S(2)}) copy-start(bf16[512,1024]{1,0:T(8,128)(2,1)S(1)} %collective-permute-done.1.refs_1_) | copy-start | bytes 3145732
  26.9 1.5 copy-start.3
  28.4 1.0 copy-start.4
  41.7 4.7 %collective-permute-start.4 = (f32[256,256]{1,0:T(8,128)S(1)}, f32[256,256]{1,0:T(8,128)S(1)}, u32[]{:S(2)}, u32[]{:S(2)}) collective-permute-start(f32[256,256]{1,0:T(8,128)S(1)} %get-tuple-element.31), channel_id=1, source_target_pairs={{0,16},{16,0},{1,17},{17,1},{2,18},{18,2},{3,19},{19,3},{4,20},{20... | collective-permute-start | bytes 786440 | tf_op jit(solution)/shard_map/project/ppermute | solution.py:372
  46.5 6.3 %collective-permute-start.7 = (bf16[256,256]{1,0:T(8,128)(2,1)S(1)}, bf16[256,256]{1,0:T(8,128)(2,1)S(1)}, u32[]{:S(2)}, u32[]{:S(2)}) collective-permute-start(bf16[256,256]{1,0:T(8,128)(2,1)S(1)} %add_convert_fusion.1), channel_id=1, source_target_pairs={{0,96},{32,0},{64,32},{96,64},{1,97},{33,1},{65,33},{97,65},{2,98}... | collective-permute-start | bytes 393224 | tf_op jit(solution)/shard_map/project/ppermute | solution.py:376
  50.3 8.8 %collective-permute-start.6 = (bf16[256,256]{1,0:T(8,128)(2,1)S(1)}, bf16[256,256]{1,0:T(8,128)(2,1)S(1)}, u32[]{:S(2)}, u32[]{:S(2)}) collective-permute-start(bf16[256,256]{1,0:T(8,128)(2,1)S(1)} %add_convert_fusion.1), channel_id=1, source_target_pairs={{0,32},{32,64},{64,96},{96,0},{1,33},{33,65},{65,97},{97,1},{2,34}... | collective-permute-start | bytes 393224 | tf_op jit(solution)/shard_map/project/ppermute | solution.py:376
  50.3 8.8 %collective-permute-start.5 = (bf16[256,256]{1,0:T(8,128)(2,1)S(1)}, bf16[256,256]{1,0:T(8,128)(2,1)S(1)}, u32[]{:S(2)}, u32[]{:S(2)}) collective-permute-start(bf16[256,256]{1,0:T(8,128)(2,1)S(1)} %add_convert_fusion.1), channel_id=1, source_target_pairs={{0,64},{32,96},{64,0},{96,32},{1,65},{33,97},{65,1},{97,33},{2,66}... | collective-permute-start | bytes 393224 | tf_op jit(solution)/shard_map/project/ppermute | solution.py:376
  59.2 2.2 %collective-permute-start.8 = (bf16[256,256]{1,0:T(8,128)(2,1)S(1)}, bf16[256,256]{1,0:T(8,128)(2,1)S(1)}, u32[]{:S(2)}, u32[]{:S(2)}) collective-permute-start(bf16[256,256]{1,0:T(8,128)(2,1)S(1)} %add_convert_fusion.mine_ref), channel_id=1, source_target_pairs={{0,16},{16,0},{1,17},{17,1},{2,18},{18,2},{3,19},{19,3},{4,20},{20... | collective-permute-start | bytes 393224 | tf_op jit(solution)/shard_map/gram/ppermute | solution.py:372
  62.2 6.1 %collective-permute-start.11 = (bf16[128,256]{1,0:T(8,128)(2,1)S(1)}, bf16[128,256]{1,0:T(8,128)(2,1)S(1)}, u32[]{:S(2)}, u32[]{:S(2)}) collective-permute-start(bf16[128,256]{1,0:T(8,128)(2,1)S(1)} %get-tuple-element.33), channel_id=1, source_target_pairs={{0,12},{4,0},{8,4},{12,8},{1,13},{5,1},{9,5},{13,9},{2,14},{6,2},{... | collective-permute-start | bytes 196616 | tf_op jit(solution)/shard_map/gram/ppermute | solution.py:376
  62.3 5.9 %collective-permute-start.10 = (bf16[128,256]{1,0:T(8,128)(2,1)S(1)}, bf16[128,256]{1,0:T(8,128)(2,1)S(1)}, u32[]{:S(2)}, u32[]{:S(2)}) collective-permute-start(bf16[128,256]{1,0:T(8,128)(2,1)S(1)} %get-tuple-element.33), channel_id=1, source_target_pairs={{0,4},{4,8},{8,12},{12,0},{1,5},{5,9},{9,13},{13,1},{2,6},{6,10},{... | collective-permute-start | bytes 196616 | tf_op jit(solution)/shard_map/gram/ppermute | solution.py:376
  63.7 4.7 %collective-permute-start.9 = (bf16[128,256]{1,0:T(8,128)(2,1)S(1)}, bf16[128,256]{1,0:T(8,128)(2,1)S(1)}, u32[]{:S(2)}, u32[]{:S(2)}) collective-permute-start(bf16[128,256]{1,0:T(8,128)(2,1)S(1)} %get-tuple-element.33), channel_id=1, source_target_pairs={{0,8},{4,12},{8,0},{12,4},{1,9},{5,13},{9,1},{13,5},{2,10},{6,14},... | collective-permute-start | bytes 196616 | tf_op jit(solution)/shard_map/gram/ppermute | solution.py:376
  68.4 32.0 %all-to-all-start.1 = ((bf16[64,16,1024]{2,1,0:T(8,128)(2,1)}), bf16[64,16,1024]{2,1,0:T(8,128)(2,1)S(1)}, u32[]{:S(2)}, u32[]{:S(2)}) async-start(bf16[64,16,1024]{2,1,0:T(8,128)(2,1)} %bitcast.15), calls=%async_computation.1 | async-start | bytes 4194304 | tf_op jit(solution)/shard_map/term/all_to_all | solution.py:411
  73.1 15.6 %collective-permute-start.13 = (bf16[128,256]{1,0:T(8,128)(2,1)S(1)}, bf16[128,256]{1,0:T(8,128)(2,1)S(1)}, u32[]{:S(2)}, u32[]{:S(2)}) collective-permute-start(bf16[128,256]{1,0:T(8,128)(2,1)S(1)} %add_add_fusion.1), channel_id=1, source_target_pairs={{0,1},{1,2},{2,3},{3,0},{4,5},{5,6},{6,7},{7,4},{8,9},{9,10},{10,1... | collective-permute-start | bytes 196616 | tf_op jit(solution)/shard_map/gather/ppermute | solution.py:376
  74.1 22.6 %collective-permute-start.12 = (bf16[128,256]{1,0:T(8,128)(2,1)S(1)}, bf16[128,256]{1,0:T(8,128)(2,1)S(1)}, u32[]{:S(2)}, u32[]{:S(2)}) collective-permute-start(bf16[128,256]{1,0:T(8,128)(2,1)S(1)} %add_add_fusion.1), channel_id=1, source_target_pairs={{0,2},{1,3},{2,0},{3,1},{4,6},{5,7},{6,4},{7,5},{8,10},{9,11},{10,... | collective-permute-start | bytes 196616 | tf_op jit(solution)/shard_map/gather/ppermute | solution.py:376
  76.5 20.2 %collective-permute-start.14 = (bf16[128,256]{1,0:T(8,128)(2,1)S(1)}, bf16[128,256]{1,0:T(8,128)(2,1)S(1)}, u32[]{:S(2)}, u32[]{:S(2)}) collective-permute-start(bf16[128,256]{1,0:T(8,128)(2,1)S(1)} %add_add_fusion.1), channel_id=1, source_target_pairs={{0,3},{1,0},{2,1},{3,2},{4,7},{5,4},{6,5},{7,6},{8,11},{9,8},{10,9... | collective-permute-start | bytes 196616 | tf_op jit(solution)/shard_map/gather/ppermute | solution.py:376
  102.1 10.6 %collective-permute-start.15 = (f32[128,256]{1,0:T(8,128)S(1)}, f32[128,256]{1,0:T(8,128)S(1)}, u32[]{:S(2)}, u32[]{:S(2)}) collective-permute-start(f32[128,256]{1,0:T(8,128)S(1)} %add_add_fusion), channel_id=1, source_target_pairs={{0,16},{16,0},{1,17},{17,1},{2,18},{18,2},{3,19},{19,3},{4,20},{20... | collective-permute-start | bytes 393224 | tf_op jit(solution)/shard_map/solve/ppermute | solution.py:372
  105.6 35.7 %all-to-all-start.2 = ((bf16[64,16,1024]{2,1,0:T(8,128)(2,1)}), bf16[64,16,1024]{2,1,0:T(8,128)(2,1)S(1)}, u32[]{:S(2)}, u32[]{:S(2)}) async-start(bf16[64,16,1024]{2,1,0:T(8,128)(2,1)} %gather.1), calls=%async_computation.2 | async-start | bytes 4194304 | tf_op jit(solution)/shard_map/gather/all_to_all | solution.py:416
  141.3 7.1 %collective-permute-start.16 = (bf16[4,16,16,1024]{3,2,1,0:T(8,128)(2,1)S(1)}, bf16[4,16,16,1024]{3,2,1,0:T(8,128)(2,1)}, u32[]{:S(2)}, u32[]{:S(2)}) collective-permute-start(bf16[4,16,16,1024]{3,2,1,0:T(8,128)(2,1)S(1)} %bitcast.10), channel_id=1, source_target_pairs={{0,16},{16,0},{1,17},{17,1},{2,18},{18,2},{3,19},{19,3},{4,20},{20... | collective-permute-start | bytes 6291464 | tf_op jit(solution)/shard_map/finish/ppermute | solution.py:372

commit v6 on v5

--- a/solution.py
+++ b/solution.py
@@ -257,6 +257,7 @@
 NT_DOT = (((1,), (1,)), ((), ()))
 BASE = 64
 PANEL = 16
+TERMS = 3
 
 
 def inverse_factor(a):
@@ -287,20 +288,24 @@
 
 def solve_kernel(g_ref, s_ref, inv_ref, w_ref):
     inv = inverse_factor(g_ref[...])
-    inv_ref[...] = inv
+    rest = inv.T * 0.125
+    for i in range(TERMS):
+        part = rest.astype(BF16)
+        inv_ref[i * RANK : (i + 1) * RANK, :] = part
+        rest = rest - part.astype(F32)
     basis = dot_hi(s_ref[...].astype(F32), inv, NT_DOT)
     w_ref[...] = (dot_hi(basis, inv) * 0.125).astype(BF16)
 
 
 def solve(gram, summed):
-    square = pl.BlockSpec((RANK, RANK), lambda j: (0, 0))
+    terms = pl.BlockSpec((TERMS * RANK, RANK), lambda j: (0, 0))
     tall = pl.BlockSpec((ROWS, RANK), lambda j: (0, 0))
     return pl.pallas_call(
         solve_kernel,
         grid=(1,),
         in_specs=[VMEM, tall],
-        out_specs=[square, tall],
-        out_shape=[pltpu.HBM((RANK, RANK), F32), pltpu.HBM((ROWS, RANK), BF16)],
+        out_specs=[terms, tall],
+        out_shape=[pltpu.HBM((TERMS * RANK, RANK), BF16), pltpu.HBM((ROWS, RANK), BF16)],
         compiler_params=params(),
         cost_estimate=pl.CostEstimate(flops=2 * 10**10, bytes_accessed=10**6, transcendentals=0),
     )(gram, *in_hbm(summed))
@@ -334,8 +339,10 @@
             load([(out.at[k, :, s * SUB : (s + 1) * SUB], err_ref.at[:, to])], sem, at + k * per + s)
 
     rolled(CHUNKS, step)
-    x = t[m // per, :, :, aligned(m % per * SUB, SUB)].reshape(RANK, SUB)
-    f[...] = dot_hi(inv[...], x.astype(F32)).T * 0.125
+    x = t[m // per, :, :, aligned(m % per * SUB, SUB)].reshape(RANK, SUB).T
+    f[...] = jnp.dot(x, inv[:RANK, :], preferred_element_type=F32)
+    for i in range(1, TERMS):
+        f[...] += jnp.dot(x, inv[i * RANK : (i + 1) * RANK, :], preferred_element_type=F32)
     last = load([(f, f_ref.at[aligned(core * SUB, SUB)])], sem, at + CHUNKS * per)
 
     def sent(k):
@@ -360,7 +367,7 @@
             pltpu.VMEM((CHUNKS, ROWS, CHUNK), BF16),
             pltpu.VMEM((SUB, RANK), F32),
             pltpu.VMEM((ROWS, RANK), BF16),
-            pltpu.VMEM((RANK, RANK), F32),
+            pltpu.VMEM((TERMS * RANK, RANK), BF16),
             pltpu.SemaphoreType.DMA((3 + 2 * CHUNKS + NM,)),
         ],
         compiler_params=params(),

time: 154 us -> 154 us (level)
  transfers between devices with their start and end apart: 20 -> 20, of which waited for: 14 -> 14; matrix products, arithmetic and copies ran while one was open for 0% -> 0% of each run, Pallas kernels for 23% -> 24%
where the time goes in v6:
time: 154 us
  waiting for transfers between devices  59 us (38%)
  Pallas kernels  47 us (31%)
  starting transfers between devices  42.9 us (28%)
  local copies, waits for them, and re-layouts  3.51 us (2%)
    ppermute x9, waiting for transfers between devices, ring_sum(): lax.ppermute(x, axis, [(i, (i + k) % 4) for i in range(4)])  26.7 us
    all_to_all x1, waiting for transfers between devices, shards(): mine = lax.all_to_all(sums, ('z', 'x', 'y'), 0, 0, tiled=True)  16.4 us
    pallas_call x1, Pallas kernels, solve(): pl.pallas_call(solve_kernel, grid=(1,), in_specs=[VMEM, tall], out_specs=...  12.2 us
    ppermute x9, starting transfers between devices, ring_sum(): lax.ppermute(x, axis, [(i, (i + k) % 4) for i in range(4)])  11.9 us
    ppermute x8, starting transfers between devices, swap(): return lax.ppermute(x, 'c', [(0, 1), (1, 0)])  11.6 us
    pallas_call x2, Pallas kernels, finish(): pl.pallas_call(functools.partial(finish_kernel, held), in_specs=[SMEM, HB...  10.3 us
    pallas_call x1, Pallas kernels, adjust(): pl.pallas_call(adjust_kernel, in_specs=[SMEM, HBM, HBM], out_specs=[HBM]...  9.6 us
    ppermute x8, waiting for transfers between devices, swap(): return lax.ppermute(x, 'c', [(0, 1), (1, 0)])  8.54 us
  transfers between devices with their start and end apart: 20, of which 14 were waited for; matrix products, arithmetic and copies ran while one was open for 0% of the time, Pallas kernels for 24%

profile of v6, /device:TPU:1, one launch (start us, length us, event | category | flops | bytes accessed | tf_op | source)
XLA Modules:
  0.0 153.8 jit_solution(5304151902710631553)
XLA Ops:
  0.6 0.0 copy-start
  0.7 0.9 copy-done
  1.6 1.6 %broadcast_in_dim.4 = bf16[16,256,256]{2,1,0:T(8,128)(2,1)} broadcast(bf16[256,256]{1,0:T(8,128)(2,1)S(1)} %constant_dynamic-slice_fusion), dimensions={1,2} | broadcast | bytes 2228224 | tf_op jit(solution)/shard_map/query_gather/broadcast_in_dim | solution.py:399
  3.2 7.6 %all-to-all-start = ((bf16[16,256,256]{2,1,0:T(8,128)(2,1)}), bf16[16,256,256]{2,1,0:T(8,128)(2,1)S(1)}, u32[]{:S(2)}, u32[]{:S(2)}) async-start(bf16[16,256,256]{2,1,0:T(8,128)(2,1)} %broadcast_in_dim.4), calls=%async_computation | async-start | bytes 4194304 | tf_op jit(solution)/shard_map/query_gather/all_to_all | solution.py:400
  10.8 9.6 %adjust.2 = (bf16[512,4096]{1,0:T(8,128)(2,1)}, bf16[512,1024]{1,0:T(8,128)(2,1)}, bf16[512,1024]{1,0:T(8,128)(2,1)}, bf16[512,1024]{1,0:T(8,128)(2,1)}, bf16[512,1024]{1,0:T(8,128)(2,1)}) custom-call(s32[1]{0:T(128)} %bitcast.2.c_ref, bf16[512,8192]{1,0:T(8,128)(2,1)} %bitcast.12, bf16[512,8192]{1,0:T(8,128)(2,1)} %bitcast.13), custom_call_target="tpu_custom_call" | custom-call | flops 4194304 | bytes 25165824 | tf_op jit(solution)/shard_map/adjust/pallas_call | solution.py:97
  20.4 1.0 collective-permute-start
  21.4 0.1 collective-permute-start.1
  21.5 0.4 collective-permute-start.2
  21.9 0.1 collective-permute-start.3
  22.0 1.9 %collective-permute-done.refs_0_ = bf16[512,1024]{1,0:T(8,128)(2,1)S(1)} collective-permute-done((bf16[512,1024]{1,0:T(8,128)(2,1)}, bf16[512,1024]{1,0:T(8,128)(2,1)S(1)}, u32[]{:S(2)}, u32[]{:S(2)}) %collective-permute-start) | collective-permute-done | bytes 1048608 | tf_op jit(solution)/shard_map/adjust/ppermute | solution.py:379
  23.9 0.0 copy-start.1
  23.9 1.5 collective-permute-done.1.refs_1_
  25.4 0.0 copy-start.2
  25.4 1.5 collective-permute-done.2.refs_2_
  26.9 0.0 copy-start.3
  26.9 1.5 collective-permute-done.3.refs_3_
  28.4 0.0 copy-start.4
  28.4 0.0 copy-done.1
  28.4 0.0 copy-done.2
  28.4 0.0 copy-done.3
  28.4 1.0 copy-done.4
  29.4 5.5 %adjust.3.a_ref = bf16[512,4096]{1,0:T(8,128)(2,1)} custom-call(bf16[512,4096]{1,0:T(8,128)(2,1)} %get-tuple-element.25.own_ref.refs_0_, bf16[512,1024]{1,0:T(8,128)(2,1)} %copy-done.1, bf16[512,1024]{1,0:T(8,128)(2,1)} %copy-done.2, bf16[512,1024]{1,0:T(8,128)(2,1)} %copy-done.3, bf16[512,1024]{1,0:T(8,128)(2,1)} %copy-done.4), custom_call_target="tpu_custom_call" | custom-call | flops 2097152 | bytes 12582912 | tf_op jit(solution)/shard_map/adjust/pallas_call | solution.py:127
  34.9 3.8 %all-to-all-done = bf16[16,256,256]{2,1,0:T(8,128)(2,1)S(1)} async-done(((bf16[16,256,256]{2,1,0:T(8,128)(2,1)}), bf16[16,256,256]{2,1,0:T(8,128)(2,1)S(1)}, u32[]{:S(2)}, u32[]{:S(2)}) %all-to-all-start) | async-done | bytes 2097184 | tf_op jit(solution)/shard_map/query_gather/all_to_all | solution.py:400
  38.7 3.1 %project.1 = (f32[256,256]{1,0:T(8,128)S(1)}, f32[256,256]{1,0:T(8,128)S(1)}) custom-call(s32[1]{0:T(128)} %bitcast.2.c_ref, bf16[4096,256]{1,0:T(8,128)(2,1)S(1)} %bitcast.9, bf16[512,4096]{1,0:T(8,128)(2,1)} %adjust.3.a_ref), custom_call_target="tpu_custom_call" | custom-call | flops 1073741824 | bytes 6291456 | tf_op jit(solution)/shard_map/project/pallas_call | solution.py:155
  41.7 3.5 %collective-permute-start.4 = (f32[256,256]{1,0:T(8,128)S(1)}, f32[256,256]{1,0:T(8,128)S(1)}, u32[]{:S(2)}, u32[]{:S(2)}) collective-permute-start(f32[256,256]{1,0:T(8,128)S(1)} %get-tuple-element.31), channel_id=1, source_target_pairs={{0,16},{16,0},{1,17},{17,1},{2,18},{18,2},{3,19},{19,3},{4,20},{20... | collective-permute-start | bytes 786440 | tf_op jit(solution)/shard_map/project/ppermute | solution.py:379
  45.3 1.2 collective-permute-done.4
  46.5 3.8 %collective-permute-start.7 = (bf16[256,256]{1,0:T(8,128)(2,1)S(1)}, bf16[256,256]{1,0:T(8,128)(2,1)S(1)}, u32[]{:S(2)}, u32[]{:S(2)}) collective-permute-start(bf16[256,256]{1,0:T(8,128)(2,1)S(1)} %add_convert_fusion.1), channel_id=1, source_target_pairs={{0,96},{32,0},{64,32},{96,64},{1,97},{33,1},{65,33},{97,65},{2,98}... | collective-permute-start | bytes 393224 | tf_op jit(solution)/shard_map/project/ppermute | solution.py:383
  50.3 0.0 collective-permute-start.6
  50.3 1.3 collective-permute-start.5
  51.6 1.2 collective-permute-done.7
  52.8 6.3 %collective-permute-done.6 = bf16[256,256]{1,0:T(8,128)(2,1)S(1)} collective-permute-done((bf16[256,256]{1,0:T(8,128)(2,1)S(1)}, bf16[256,256]{1,0:T(8,128)(2,1)S(1)}, u32[]{:S(2)}, u32[]{:S(2)}) %collective-permute-start.6) | collective-permute-done | bytes 131104 | tf_op jit(solution)/shard_map/project/ppermute | solution.py:383
  59.1 0.0 collective-permute-done.5
  59.1 0.1 add_convert_fusion.mine_ref
  59.2 1.2 collective-permute-start.8
  60.4 1.0 collective-permute-done.8.theirs_ref
  61.4 0.8 gram.1
  62.2 0.1 collective-permute-start.11
  62.3 1.3 collective-permute-start.10
  63.7 0.7 collective-permute-start.9
  64.4 3.9 %term.1 = bf16[4,16,16,1024]{3,2,1,0:T(8,128)(2,1)} custom-call(bf16[256,512]{1,0:T(8,128)(2,1)S(1)} %get-tuple-element.32.st_ref, bf16[512,4096]{1,0:T(8,128)(2,1)} %adjust.3.a_ref), custom_call_target="tpu_custom_call" | custom-call | flops 1073741824 | bytes 6291456 | tf_op jit(solution)/shard_map/term/pallas_call | solution.py:214
  68.3 0.0 collective-permute-done.11
  68.3 0.0 collective-permute-done.10
  68.3 0.1 collective-permute-done.9
  68.4 4.7 %all-to-all-start.1 = ((bf16[64,16,1024]{2,1,0:T(8,128)(2,1)}), bf16[64,16,1024]{2,1,0:T(8,128)(2,1)S(1)}, u32[]{:S(2)}, u32[]{:S(2)}) async-start(bf16[64,16,1024]{2,1,0:T(8,128)(2,1)} %bitcast.15), calls=%async_computation.1 | async-start | bytes 4194304 | tf_op jit(solution)/shard_map/term/all_to_all | solution.py:418
  73.1 1.0 collective-permute-start.13
  74.1 2.4 %collective-permute-start.12 = (bf16[128,256]{1,0:T(8,128)(2,1)S(1)}, bf16[128,256]{1,0:T(8,128)(2,1)S(1)}, u32[]{:S(2)}, u32[]{:S(2)}) collective-permute-start(bf16[128,256]{1,0:T(8,128)(2,1)S(1)} %add_add_fusion.1), channel_id=1, source_target_pairs={{0,2},{1,3},{2,0},{3,1},{4,6},{5,7},{6,4},{7,5},{8,10},{9,11},{10,... | collective-permute-start | bytes 196616 | tf_op jit(solution)/shard_map/gather/ppermute | solution.py:383
  76.5 1.2 collective-permute-start.14
  77.7 11.0 %collective-permute-done.13 = bf16[128,256]{1,0:T(8,128)(2,1)S(1)} collective-permute-done((bf16[128,256]{1,0:T(8,128)(2,1)S(1)}, bf16[128,256]{1,0:T(8,128)(2,1)S(1)}, u32[]{:S(2)}, u32[]{:S(2)}) %collective-permute-start.13) | collective-permute-done | bytes 65568 | tf_op jit(solution)/shard_map/gather/ppermute | solution.py:383
  88.7 8.0 %collective-permute-done.12 = bf16[128,256]{1,0:T(8,128)(2,1)S(1)} collective-permute-done((bf16[128,256]{1,0:T(8,128)(2,1)S(1)}, bf16[128,256]{1,0:T(8,128)(2,1)S(1)}, u32[]{:S(2)}, u32[]{:S(2)}) %collective-permute-start.12) | collective-permute-done | bytes 65568 | tf_op jit(solution)/shard_map/gather/ppermute | solution.py:383
  96.7 0.0 collective-permute-done.14
  96.8 3.7 %all-to-all-done.1.x_ref = bf16[64,16,1024]{2,1,0:T(8,128)(2,1)S(1)} async-done(((bf16[64,16,1024]{2,1,0:T(8,128)(2,1)}), bf16[64,16,1024]{2,1,0:T(8,128)(2,1)S(1)}, u32[]{:S(2)}, u32[]{:S(2)}) %all-to-all-start.1) | async-done | bytes 2097184 | tf_op jit(solution)/shard_map/term/all_to_all | solution.py:418
  100.4 1.7 %gather.1 = bf16[64,16,1024]{2,1,0:T(8,128)(2,1)} custom-call(bf16[64,16,1024]{2,1,0:T(8,128)(2,1)S(1)} %all-to-all-done.1.x_ref), custom_call_target="tpu_custom_call" | custom-call | flops 1048576 | bytes 4194304 | tf_op jit(solution)/shard_map/gather/pallas_call | solution.py:239
  102.1 3.5 %collective-permute-start.15 = (f32[128,256]{1,0:T(8,128)S(1)}, f32[128,256]{1,0:T(8,128)S(1)}, u32[]{:S(2)}, u32[]{:S(2)}) collective-permute-start(f32[128,256]{1,0:T(8,128)S(1)} %add_add_fusion), channel_id=1, source_target_pairs={{0,16},{16,0},{1,17},{17,1},{2,18},{18,2},{3,19},{19,3},{4,20},{20... | collective-permute-start | bytes 393224 | tf_op jit(solution)/shard_map/solve/ppermute | solution.py:379
  105.6 7.1 %all-to-all-start.2 = ((bf16[64,16,1024]{2,1,0:T(8,128)(2,1)}), bf16[64,16,1024]{2,1,0:T(8,128)(2,1)S(1)}, u32[]{:S(2)}, u32[]{:S(2)}) async-start(bf16[64,16,1024]{2,1,0:T(8,128)(2,1)} %gather.1), calls=%async_computation.2 | async-start | bytes 4194304 | tf_op jit(solution)/shard_map/gather/all_to_all | solution.py:423
  112.7 0.0 collective-permute-done.15
  112.8 12.2 %solve.1 = (bf16[768,256]{1,0:T(8,128)(2,1)}, bf16[512,256]{1,0:T(8,128)(2,1)}) custom-call(f32[256,256]{1,0:T(8,128)S(1)} %pad_maximum_fusion.g_ref, bf16[512,256]{1,0:T(8,128)(2,1)} %get-tuple-element.38.s_ref), custom_call_target="tpu_custom_call" | custom-call | flops 20000000000 | bytes 1000000 | tf_op jit(solution)/shard_map/solve/pallas_call | solution.py:303
  125.0 16.4 %all-to-all-done.2 = bf16[64,16,1024]{2,1,0:T(8,128)(2,1)S(1)} async-done(((bf16[64,16,1024]{2,1,0:T(8,128)(2,1)}), bf16[64,16,1024]{2,1,0:T(8,128)(2,1)S(1)}, u32[]{:S(2)}, u32[]{:S(2)}) %all-to-all-start.2) | async-done | bytes 2097184 | tf_op jit(solution)/shard_map/gather/all_to_all | solution.py:423
  141.3 1.8 %collective-permute-start.16 = (bf16[4,16,16,1024]{3,2,1,0:T(8,128)(2,1)S(1)}, bf16[4,16,16,1024]{3,2,1,0:T(8,128)(2,1)}, u32[]{:S(2)}, u32[]{:S(2)}) collective-permute-start(bf16[4,16,16,1024]{3,2,1,0:T(8,128)(2,1)S(1)} %bitcast.10), channel_id=1, source_target_pairs={{0,16},{16,0},{1,17},{17,1},{2,18},{18,2},{3,19},{19,3},{4,20},{20... | collective-permute-start | bytes 6291464 | tf_op jit(solution)/shard_map/finish/ppermute | solution.py:379
  143.1 0.1 pad_add_fusion.1.s_ref
  143.2 0.1 pad_add_fusion.s_ref
  143.2 5.0 %finish.2 = (bf16[512,8192]{1,0:T(8,128)(2,1)}, f32[512,256]{1,0:T(8,128)}) custom-call(s32[2]{0:T(128)S(1)} %pad_add_fusion.1.s_ref, bf16[512,256]{1,0:T(8,128)(2,1)} %get-tuple-element.41.w_ref, bf16[768,256]{1,0:T(8,128)(2,1)} %get-tuple-element.42.inv_ref, bf16[4,16,16,1024]{3,2,1,0:T(8,128)(2,1)S(1)} %bitcast.11, ...), custom_call_target="tpu_custom_call" | custom-call | flops 1073741824 | bytes 10485760 | tf_op jit(solution)/shard_map/finish/pallas_call | solution.py:358
  148.3 0.0 collective-permute-done.16.t_ref
  148.3 5.3 %finish.3 = (bf16[512,8192]{1,0:T(8,128)(2,1)}, f32[512,256]{1,0:T(8,128)}) custom-call(s32[2]{0:T(128)S(1)} %pad_add_fusion.s_ref, bf16[512,256]{1,0:T(8,128)(2,1)} %get-tuple-element.41.w_ref, bf16[768,256]{1,0:T(8,128)(2,1)} %get-tuple-element.42.inv_ref, ...), custom_call_target="tpu_custom_call", output_to_operand_aliasing={{0}: (8, {}), {1}: (9, {})} | custom-call | flops 1073741824 | bytes 10485760 | tf_op jit(solution)/shard_map/finish/pallas_call | solution.py:358
  (6 shorter events, 0.2 us)
Async XLA Ops:
  0.6 1.0 copy-start
  3.2 35.5 %all-to-all-start = ((bf16[16,256,256]{2,1,0:T(8,128)(2,1)}), bf16[16,256,256]{2,1,0:T(8,128)(2,1)S(1)}, u32[]{:S(2)}, u32[]{:S(2)}) async-start(bf16[16,256,256]{2,1,0:T(8,128)(2,1)} %broadcast_in_dim.4), calls=%async_computation | async-start | bytes 4194304 | tf_op jit(solution)/shard_map/query_gather/all_to_all | solution.py:400
  20.4 3.5 %collective-permute-start = (bf16[512,1024]{1,0:T(8,128)(2,1)}, bf16[512,1024]{1,0:T(8,128)(2,1)S(1)}, u32[]{:S(2)}, u32[]{:S(2)}) collective-permute-start(bf16[512,1024]{1,0:T(8,128)(2,1)} %get-tuple-element.26.refs_0_), channel_id=1, source_target_pairs={{0,16},{16,0},{1,17},{17,1},{2,18},{18,2},{3,19},{19,3},{4,20},{20... | collective-permute-start | bytes 3145736 | tf_op jit(solution)/shard_map/adjust/ppermute | solution.py:379
  21.4 4.0 %collective-permute-start.1 = (bf16[512,1024]{1,0:T(8,128)(2,1)}, bf16[512,1024]{1,0:T(8,128)(2,1)S(1)}, u32[]{:S(2)}, u32[]{:S(2)}) collective-permute-start(bf16[512,1024]{1,0:T(8,128)(2,1)} %get-tuple-element.27.refs_1_), channel_id=1, source_target_pairs={{0,16},{16,0},{1,17},{17,1},{2,18},{18,2},{3,19},{19,3},{4,20},{20... | collective-permute-start | bytes 3145736 | tf_op jit(solution)/shard_map/adjust/ppermute | solution.py:379
  21.5 5.4 %collective-permute-start.2 = (bf16[512,1024]{1,0:T(8,128)(2,1)}, bf16[512,1024]{1,0:T(8,128)(2,1)S(1)}, u32[]{:S(2)}, u32[]{:S(2)}) collective-permute-start(bf16[512,1024]{1,0:T(8,128)(2,1)} %get-tuple-element.28.refs_2_), channel_id=1, source_target_pairs={{0,16},{16,0},{1,17},{17,1},{2,18},{18,2},{3,19},{19,3},{4,20},{20... | collective-permute-start | bytes 3145736 | tf_op jit(solution)/shard_map/adjust/ppermute | solution.py:379
  21.9 6.5 %collective-permute-start.3 = (bf16[512,1024]{1,0:T(8,128)(2,1)}, bf16[512,1024]{1,0:T(8,128)(2,1)S(1)}, u32[]{:S(2)}, u32[]{:S(2)}) collective-permute-start(bf16[512,1024]{1,0:T(8,128)(2,1)} %get-tuple-element.29.refs_3_), channel_id=1, source_target_pairs={{0,16},{16,0},{1,17},{17,1},{2,18},{18,2},{3,19},{19,3},{4,20},{20... | collective-permute-start | bytes 3145736 | tf_op jit(solution)/shard_map/adjust/ppermute | solution.py:379
  23.9 4.5 %copy-start.1 = (bf16[512,1024]{1,0:T(8,128)(2,1)}, bf16[512,1024]{1,0:T(8,128)(2,1)S(1)}, u32[]{:S(2)}) copy-start(bf16[512,1024]{1,0:T(8,128)(2,1)S(1)} %collective-permute-done.refs_0_) | copy-start | bytes 3145732
  25.4 3.0 %copy-start.2 = (bf16[512,1024]{1,0:T(8,128)(2,1)}, bf16[512,1024]{1,0:T(8,128)(2,1)S(1)}, u32[]{:S(2)}) copy-start(bf16[512,1024]{1,0:T(8,128)(2,1)S(1)} %collective-permute-done.1.refs_1_) | copy-start | bytes 3145732
  26.9 1.5 copy-start.3
  28.4 1.0 copy-start.4
  41.7 4.7 %collective-permute-start.4 = (f32[256,256]{1,0:T(8,128)S(1)}, f32[256,256]{1,0:T(8,128)S(1)}, u32[]{:S(2)}, u32[]{:S(2)}) collective-permute-start(f32[256,256]{1,0:T(8,128)S(1)} %get-tuple-element.31), channel_id=1, source_target_pairs={{0,16},{16,0},{1,17},{17,1},{2,18},{18,2},{3,19},{19,3},{4,20},{20... | collective-permute-start | bytes 786440 | tf_op jit(solution)/shard_map/project/ppermute | solution.py:379
  46.5 6.3 %collective-permute-start.7 = (bf16[256,256]{1,0:T(8,128)(2,1)S(1)}, bf16[256,256]{1,0:T(8,128)(2,1)S(1)}, u32[]{:S(2)}, u32[]{:S(2)}) collective-permute-start(bf16[256,256]{1,0:T(8,128)(2,1)S(1)} %add_convert_fusion.1), channel_id=1, source_target_pairs={{0,96},{32,0},{64,32},{96,64},{1,97},{33,1},{65,33},{97,65},{2,98}... | collective-permute-start | bytes 393224 | tf_op jit(solution)/shard_map/project/ppermute | solution.py:383
  50.3 8.8 %collective-permute-start.6 = (bf16[256,256]{1,0:T(8,128)(2,1)S(1)}, bf16[256,256]{1,0:T(8,128)(2,1)S(1)}, u32[]{:S(2)}, u32[]{:S(2)}) collective-permute-start(bf16[256,256]{1,0:T(8,128)(2,1)S(1)} %add_convert_fusion.1), channel_id=1, source_target_pairs={{0,32},{32,64},{64,96},{96,0},{1,33},{33,65},{65,97},{97,1},{2,34}... | collective-permute-start | bytes 393224 | tf_op jit(solution)/shard_map/project/ppermute | solution.py:383
  50.3 8.8 %collective-permute-start.5 = (bf16[256,256]{1,0:T(8,128)(2,1)S(1)}, bf16[256,256]{1,0:T(8,128)(2,1)S(1)}, u32[]{:S(2)}, u32[]{:S(2)}) collective-permute-start(bf16[256,256]{1,0:T(8,128)(2,1)S(1)} %add_convert_fusion.1), channel_id=1, source_target_pairs={{0,64},{32,96},{64,0},{96,32},{1,65},{33,97},{65,1},{97,33},{2,66}... | collective-permute-start | bytes 393224 | tf_op jit(solution)/shard_map/project/ppermute | solution.py:383
  59.2 2.2 %collective-permute-start.8 = (bf16[256,256]{1,0:T(8,128)(2,1)S(1)}, bf16[256,256]{1,0:T(8,128)(2,1)S(1)}, u32[]{:S(2)}, u32[]{:S(2)}) collective-permute-start(bf16[256,256]{1,0:T(8,128)(2,1)S(1)} %add_convert_fusion.mine_ref), channel_id=1, source_target_pairs={{0,16},{16,0},{1,17},{17,1},{2,18},{18,2},{3,19},{19,3},{4,20},{20... | collective-permute-start | bytes 393224 | tf_op jit(solution)/shard_map/gram/ppermute | solution.py:379
  62.2 6.1 %collective-permute-start.11 = (bf16[128,256]{1,0:T(8,128)(2,1)S(1)}, bf16[128,256]{1,0:T(8,128)(2,1)S(1)}, u32[]{:S(2)}, u32[]{:S(2)}) collective-permute-start(bf16[128,256]{1,0:T(8,128)(2,1)S(1)} %get-tuple-element.33), channel_id=1, source_target_pairs={{0,12},{4,0},{8,4},{12,8},{1,13},{5,1},{9,5},{13,9},{2,14},{6,2},{... | collective-permute-start | bytes 196616 | tf_op jit(solution)/shard_map/gram/ppermute | solution.py:383
  62.3 5.9 %collective-permute-start.10 = (bf16[128,256]{1,0:T(8,128)(2,1)S(1)}, bf16[128,256]{1,0:T(8,128)(2,1)S(1)}, u32[]{:S(2)}, u32[]{:S(2)}) collective-permute-start(bf16[128,256]{1,0:T(8,128)(2,1)S(1)} %get-tuple-element.33), channel_id=1, source_target_pairs={{0,4},{4,8},{8,12},{12,0},{1,5},{5,9},{9,13},{13,1},{2,6},{6,10},{... | collective-permute-start | bytes 196616 | tf_op jit(solution)/shard_map/gram/ppermute | solution.py:383
  63.7 4.7 %collective-permute-start.9 = (bf16[128,256]{1,0:T(8,128)(2,1)S(1)}, bf16[128,256]{1,0:T(8,128)(2,1)S(1)}, u32[]{:S(2)}, u32[]{:S(2)}) collective-permute-start(bf16[128,256]{1,0:T(8,128)(2,1)S(1)} %get-tuple-element.33), channel_id=1, source_target_pairs={{0,8},{4,12},{8,0},{12,4},{1,9},{5,13},{9,1},{13,5},{2,10},{6,14},... | collective-permute-start | bytes 196616 | tf_op jit(solution)/shard_map/gram/ppermute | solution.py:383
  68.4 32.0 %all-to-all-start.1 = ((bf16[64,16,1024]{2,1,0:T(8,128)(2,1)}), bf16[64,16,1024]{2,1,0:T(8,128)(2,1)S(1)}, u32[]{:S(2)}, u32[]{:S(2)}) async-start(bf16[64,16,1024]{2,1,0:T(8,128)(2,1)} %bitcast.15), calls=%async_computation.1 | async-start | bytes 4194304 | tf_op jit(solution)/shard_map/term/all_to_all | solution.py:418
  73.1 15.6 %collective-permute-start.13 = (bf16[128,256]{1,0:T(8,128)(2,1)S(1)}, bf16[128,256]{1,0:T(8,128)(2,1)S(1)}, u32[]{:S(2)}, u32[]{:S(2)}) collective-permute-start(bf16[128,256]{1,0:T(8,128)(2,1)S(1)} %add_add_fusion.1), channel_id=1, source_target_pairs={{0,1},{1,2},{2,3},{3,0},{4,5},{5,6},{6,7},{7,4},{8,9},{9,10},{10,1... | collective-permute-start | bytes 196616 | tf_op jit(solution)/shard_map/gather/ppermute | solution.py:383
  74.1 22.6 %collective-permute-start.12 = (bf16[128,256]{1,0:T(8,128)(2,1)S(1)}, bf16[128,256]{1,0:T(8,128)(2,1)S(1)}, u32[]{:S(2)}, u32[]{:S(2)}) collective-permute-start(bf16[128,256]{1,0:T(8,128)(2,1)S(1)} %add_add_fusion.1), channel_id=1, source_target_pairs={{0,2},{1,3},{2,0},{3,1},{4,6},{5,7},{6,4},{7,5},{8,10},{9,11},{10,... | collective-permute-start | bytes 196616 | tf_op jit(solution)/shard_map/gather/ppermute | solution.py:383
  76.5 20.2 %collective-permute-start.14 = (bf16[128,256]{1,0:T(8,128)(2,1)S(1)}, bf16[128,256]{1,0:T(8,128)(2,1)S(1)}, u32[]{:S(2)}, u32[]{:S(2)}) collective-permute-start(bf16[128,256]{1,0:T(8,128)(2,1)S(1)} %add_add_fusion.1), channel_id=1, source_target_pairs={{0,3},{1,0},{2,1},{3,2},{4,7},{5,4},{6,5},{7,6},{8,11},{9,8},{10,9... | collective-permute-start | bytes 196616 | tf_op jit(solution)/shard_map/gather/ppermute | solution.py:383
  102.1 10.6 %collective-permute-start.15 = (f32[128,256]{1,0:T(8,128)S(1)}, f32[128,256]{1,0:T(8,128)S(1)}, u32[]{:S(2)}, u32[]{:S(2)}) collective-permute-start(f32[128,256]{1,0:T(8,128)S(1)} %add_add_fusion), channel_id=1, source_target_pairs={{0,16},{16,0},{1,17},{17,1},{2,18},{18,2},{3,19},{19,3},{4,20},{20... | collective-permute-start | bytes 393224 | tf_op jit(solution)/shard_map/solve/ppermute | solution.py:379
  105.6 35.7 %all-to-all-start.2 = ((bf16[64,16,1024]{2,1,0:T(8,128)(2,1)}), bf16[64,16,1024]{2,1,0:T(8,128)(2,1)S(1)}, u32[]{:S(2)}, u32[]{:S(2)}) async-start(bf16[64,16,1024]{2,1,0:T(8,128)(2,1)} %gather.1), calls=%async_computation.2 | async-start | bytes 4194304 | tf_op jit(solution)/shard_map/gather/all_to_all | solution.py:423
  141.3 7.0 %collective-permute-start.16 = (bf16[4,16,16,1024]{3,2,1,0:T(8,128)(2,1)S(1)}, bf16[4,16,16,1024]{3,2,1,0:T(8,128)(2,1)}, u32[]{:S(2)}, u32[]{:S(2)}) collective-permute-start(bf16[4,16,16,1024]{3,2,1,0:T(8,128)(2,1)S(1)} %bitcast.10), channel_id=1, source_target_pairs={{0,16},{16,0},{1,17},{17,1},{2,18},{18,2},{3,19},{19,3},{4,20},{20... | collective-permute-start | bytes 6291464 | tf_op jit(solution)/shard_map/finish/ppermute | solution.py:379

commit v7 on v6

--- a/solution.py
+++ b/solution.py
@@ -147,7 +147,7 @@
     rolled(CHUNKS, step)
     c, h = c_ref[0], ROWS // 2
     keep_ref[...] = acc[aligned(c * h, h), :]
-    give_ref[...] = acc[aligned((1 - c) * h, h), :]
+    give_ref[...] = acc[aligned((1 - c) * h, h), :].astype(BF16)
 
 
 def project(c, query, a):
@@ -156,7 +156,7 @@
         project_kernel,
         in_specs=[SMEM, VMEM, HBM],
         out_specs=[VMEM, VMEM],
-        out_shape=[out, out],
+        out_shape=[out, jax.ShapeDtypeStruct(out.shape, BF16)],
         scratch_shapes=[
             pltpu.VMEM((ROWS, RANK), F32),
             pltpu.VMEM((CHUNKS, ROWS, CHUNK), BF16),

time: 154 us -> 154 us (level)
  no operation moved by 1% of the time
where the time goes in v7:
time: 154 us
  waiting for transfers between devices  58.8 us (38%)
  Pallas kernels  47 us (31%)
  starting transfers between devices  42.9 us (28%)
  local copies, waits for them, and re-layouts  3.51 us (2%)
    ppermute x9, waiting for transfers between devices, ring_sum(): lax.ppermute(x, axis, [(i, (i + k) % 4) for i in range(4)])  26.7 us
    all_to_all x1, waiting for transfers between devices, shards(): mine = lax.all_to_all(sums, ('z', 'x', 'y'), 0, 0, tiled=True)  16.4 us
    pallas_call x1, Pallas kernels, solve(): pl.pallas_call(solve_kernel, grid=(1,), in_specs=[VMEM, tall], out_specs=...  12.2 us
    ppermute x9, starting transfers between devices, ring_sum(): lax.ppermute(x, axis, [(i, (i + k) % 4) for i in range(4)])  11.9 us
    ppermute x8, starting transfers between devices, swap(): return lax.ppermute(x, 'c', [(0, 1), (1, 0)])  11.6 us
    pallas_call x2, Pallas kernels, finish(): pl.pallas_call(functools.partial(finish_kernel, held), in_specs=[SMEM, HB...  10.3 us
    pallas_call x1, Pallas kernels, adjust(): pl.pallas_call(adjust_kernel, in_specs=[SMEM, HBM, HBM], out_specs=[HBM]...  9.6 us
    ppermute x8, waiting for transfers between devices, swap(): return lax.ppermute(x, 'c', [(0, 1), (1, 0)])  8.36 us
  transfers between devices with their start and end apart: 20, of which 14 were waited for; matrix products, arithmetic and copies ran while one was open for 0% of the time, Pallas kernels for 24%

profile of v7, /device:TPU:1, one launch (start us, length us, event | category | flops | bytes accessed | tf_op | source)
XLA Modules:
  0.0 153.6 jit_solution(14626500777925573722)
XLA Ops:
  0.6 0.0 copy-start
  0.7 0.9 copy-done
  1.6 1.6 %broadcast_in_dim.4 = bf16[16,256,256]{2,1,0:T(8,128)(2,1)} broadcast(bf16[256,256]{1,0:T(8,128)(2,1)S(1)} %constant_dynamic-slice_fusion), dimensions={1,2} | broadcast | bytes 2228224 | tf_op jit(solution)/shard_map/query_gather/broadcast_in_dim | solution.py:399
  3.2 7.6 %all-to-all-start = ((bf16[16,256,256]{2,1,0:T(8,128)(2,1)}), bf16[16,256,256]{2,1,0:T(8,128)(2,1)S(1)}, u32[]{:S(2)}, u32[]{:S(2)}) async-start(bf16[16,256,256]{2,1,0:T(8,128)(2,1)} %broadcast_in_dim.4), calls=%async_computation | async-start | bytes 4194304 | tf_op jit(solution)/shard_map/query_gather/all_to_all | solution.py:400
  10.8 9.6 %adjust.2 = (bf16[512,4096]{1,0:T(8,128)(2,1)}, bf16[512,1024]{1,0:T(8,128)(2,1)}, bf16[512,1024]{1,0:T(8,128)(2,1)}, bf16[512,1024]{1,0:T(8,128)(2,1)}, bf16[512,1024]{1,0:T(8,128)(2,1)}) custom-call(s32[1]{0:T(128)} %bitcast.2.c_ref, bf16[512,8192]{1,0:T(8,128)(2,1)} %bitcast.12, bf16[512,8192]{1,0:T(8,128)(2,1)} %bitcast.13), custom_call_target="tpu_custom_call" | custom-call | flops 4194304 | bytes 25165824 | tf_op jit(solution)/shard_map/adjust/pallas_call | solution.py:97
  20.4 1.0 collective-permute-start
  21.4 0.1 collective-permute-start.1
  21.5 0.4 collective-permute-start.2
  21.9 0.1 collective-permute-start.3
  22.0 1.9 %collective-permute-done.refs_0_ = bf16[512,1024]{1,0:T(8,128)(2,1)S(1)} collective-permute-done((bf16[512,1024]{1,0:T(8,128)(2,1)}, bf16[512,1024]{1,0:T(8,128)(2,1)S(1)}, u32[]{:S(2)}, u32[]{:S(2)}) %collective-permute-start) | collective-permute-done | bytes 1048608 | tf_op jit(solution)/shard_map/adjust/ppermute | solution.py:379
  23.9 0.0 copy-start.1
  23.9 1.5 collective-permute-done.1.refs_1_
  25.4 0.0 copy-start.2
  25.4 1.5 collective-permute-done.2.refs_2_
  26.9 0.0 copy-start.3
  26.9 1.5 collective-permute-done.3.refs_3_
  28.4 0.0 copy-start.4
  28.4 0.0 copy-done.1
  28.4 0.0 copy-done.2
  28.4 0.0 copy-done.3
  28.4 1.0 copy-done.4
  29.4 5.5 %adjust.3.a_ref = bf16[512,4096]{1,0:T(8,128)(2,1)} custom-call(bf16[512,4096]{1,0:T(8,128)(2,1)} %get-tuple-element.25.own_ref.refs_0_, bf16[512,1024]{1,0:T(8,128)(2,1)} %copy-done.1, bf16[512,1024]{1,0:T(8,128)(2,1)} %copy-done.2, bf16[512,1024]{1,0:T(8,128)(2,1)} %copy-done.3, bf16[512,1024]{1,0:T(8,128)(2,1)} %copy-done.4), custom_call_target="tpu_custom_call" | custom-call | flops 2097152 | bytes 12582912 | tf_op jit(solution)/shard_map/adjust/pallas_call | solution.py:127
  34.9 3.8 %all-to-all-done = bf16[16,256,256]{2,1,0:T(8,128)(2,1)S(1)} async-done(((bf16[16,256,256]{2,1,0:T(8,128)(2,1)}), bf16[16,256,256]{2,1,0:T(8,128)(2,1)S(1)}, u32[]{:S(2)}, u32[]{:S(2)}) %all-to-all-start) | async-done | bytes 2097184 | tf_op jit(solution)/shard_map/query_gather/all_to_all | solution.py:400
  38.7 3.1 %project.1 = (f32[256,256]{1,0:T(8,128)S(1)}, bf16[256,256]{1,0:T(8,128)(2,1)S(1)}) custom-call(s32[1]{0:T(128)} %bitcast.2.c_ref, bf16[4096,256]{1,0:T(8,128)(2,1)S(1)} %bitcast.9, bf16[512,4096]{1,0:T(8,128)(2,1)} %adjust.3.a_ref), custom_call_target="tpu_custom_call" | custom-call | flops 1073741824 | bytes 6291456 | tf_op jit(solution)/shard_map/project/pallas_call | solution.py:155
  41.7 3.5 %collective-permute-start.4 = (bf16[256,256]{1,0:T(8,128)(2,1)S(1)}, bf16[256,256]{1,0:T(8,128)(2,1)S(1)}, u32[]{:S(2)}, u32[]{:S(2)}) collective-permute-start(bf16[256,256]{1,0:T(8,128)(2,1)S(1)} %get-tuple-element.31), channel_id=1, source_target_pairs={{0,16},{16,0},{1,17},{17,1},{2,18},{18,2},{3,19},{19,3},{4,20},{20... | collective-permute-start | bytes 393224 | tf_op jit(solution)/shard_map/project/ppermute | solution.py:379
  45.2 1.0 collective-permute-done.4
  46.3 3.8 %collective-permute-start.7 = (bf16[256,256]{1,0:T(8,128)(2,1)S(1)}, bf16[256,256]{1,0:T(8,128)(2,1)S(1)}, u32[]{:S(2)}, u32[]{:S(2)}) collective-permute-start(bf16[256,256]{1,0:T(8,128)(2,1)S(1)} %add_convert_fusion.1), channel_id=1, source_target_pairs={{0,96},{32,0},{64,32},{96,64},{1,97},{33,1},{65,33},{97,65},{2,98}... | collective-permute-start | bytes 393224 | tf_op jit(solution)/shard_map/project/ppermute | solution.py:383
  50.1 0.0 collective-permute-start.6
  50.1 1.3 collective-permute-start.5
  51.4 1.2 collective-permute-done.7
  52.6 6.3 %collective-permute-done.6 = bf16[256,256]{1,0:T(8,128)(2,1)S(1)} collective-permute-done((bf16[256,256]{1,0:T(8,128)(2,1)S(1)}, bf16[256,256]{1,0:T(8,128)(2,1)S(1)}, u32[]{:S(2)}, u32[]{:S(2)}) %collective-permute-start.6) | collective-permute-done | bytes 131104 | tf_op jit(solution)/shard_map/project/ppermute | solution.py:383
  58.9 0.0 collective-permute-done.5
  58.9 0.1 add_convert_fusion.mine_ref
  59.0 1.2 collective-permute-start.8
  60.2 1.0 collective-permute-done.8.theirs_ref
  61.2 0.8 gram.1
  62.0 0.1 collective-permute-start.11
  62.2 1.3 collective-permute-start.10
  63.5 0.7 collective-permute-start.9
  64.2 3.9 %term.1 = bf16[4,16,16,1024]{3,2,1,0:T(8,128)(2,1)} custom-call(bf16[256,512]{1,0:T(8,128)(2,1)S(1)} %get-tuple-element.32.st_ref, bf16[512,4096]{1,0:T(8,128)(2,1)} %adjust.3.a_ref), custom_call_target="tpu_custom_call" | custom-call | flops 1073741824 | bytes 6291456 | tf_op jit(solution)/shard_map/term/pallas_call | solution.py:214
  68.1 0.0 collective-permute-done.11
  68.1 0.0 collective-permute-done.10
  68.1 0.1 collective-permute-done.9
  68.2 4.7 %all-to-all-start.1 = ((bf16[64,16,1024]{2,1,0:T(8,128)(2,1)}), bf16[64,16,1024]{2,1,0:T(8,128)(2,1)S(1)}, u32[]{:S(2)}, u32[]{:S(2)}) async-start(bf16[64,16,1024]{2,1,0:T(8,128)(2,1)} %bitcast.15), calls=%async_computation.1 | async-start | bytes 4194304 | tf_op jit(solution)/shard_map/term/all_to_all | solution.py:418
  73.0 1.0 collective-permute-start.13
  73.9 2.4 %collective-permute-start.12 = (bf16[128,256]{1,0:T(8,128)(2,1)S(1)}, bf16[128,256]{1,0:T(8,128)(2,1)S(1)}, u32[]{:S(2)}, u32[]{:S(2)}) collective-permute-start(bf16[128,256]{1,0:T(8,128)(2,1)S(1)} %add_add_fusion.1), channel_id=1, source_target_pairs={{0,2},{1,3},{2,0},{3,1},{4,6},{5,7},{6,4},{7,5},{8,10},{9,11},{10,... | collective-permute-start | bytes 196616 | tf_op jit(solution)/shard_map/gather/ppermute | solution.py:383
  76.3 1.2 collective-permute-start.14
  77.5 11.0 %collective-permute-done.13 = bf16[128,256]{1,0:T(8,128)(2,1)S(1)} collective-permute-done((bf16[128,256]{1,0:T(8,128)(2,1)S(1)}, bf16[128,256]{1,0:T(8,128)(2,1)S(1)}, u32[]{:S(2)}, u32[]{:S(2)}) %collective-permute-start.13) | collective-permute-done | bytes 65568 | tf_op jit(solution)/shard_map/gather/ppermute | solution.py:383
  88.5 8.0 %collective-permute-done.12 = bf16[128,256]{1,0:T(8,128)(2,1)S(1)} collective-permute-done((bf16[128,256]{1,0:T(8,128)(2,1)S(1)}, bf16[128,256]{1,0:T(8,128)(2,1)S(1)}, u32[]{:S(2)}, u32[]{:S(2)}) %collective-permute-start.12) | collective-permute-done | bytes 65568 | tf_op jit(solution)/shard_map/gather/ppermute | solution.py:383
  96.6 0.0 collective-permute-done.14
  96.6 3.7 %all-to-all-done.1.x_ref = bf16[64,16,1024]{2,1,0:T(8,128)(2,1)S(1)} async-done(((bf16[64,16,1024]{2,1,0:T(8,128)(2,1)}), bf16[64,16,1024]{2,1,0:T(8,128)(2,1)S(1)}, u32[]{:S(2)}, u32[]{:S(2)}) %all-to-all-start.1) | async-done | bytes 2097184 | tf_op jit(solution)/shard_map/term/all_to_all | solution.py:418
  100.3 1.7 %gather.1 = bf16[64,16,1024]{2,1,0:T(8,128)(2,1)} custom-call(bf16[64,16,1024]{2,1,0:T(8,128)(2,1)S(1)} %all-to-all-done.1.x_ref), custom_call_target="tpu_custom_call" | custom-call | flops 1048576 | bytes 4194304 | tf_op jit(solution)/shard_map/gather/pallas_call | solution.py:239
  101.9 3.5 %collective-permute-start.15 = (f32[128,256]{1,0:T(8,128)S(1)}, f32[128,256]{1,0:T(8,128)S(1)}, u32[]{:S(2)}, u32[]{:S(2)}) collective-permute-start(f32[128,256]{1,0:T(8,128)S(1)} %add_add_fusion), channel_id=1, source_target_pairs={{0,16},{16,0},{1,17},{17,1},{2,18},{18,2},{3,19},{19,3},{4,20},{20... | collective-permute-start | bytes 393224 | tf_op jit(solution)/shard_map/solve/ppermute | solution.py:379
  105.4 7.1 %all-to-all-start.2 = ((bf16[64,16,1024]{2,1,0:T(8,128)(2,1)}), bf16[64,16,1024]{2,1,0:T(8,128)(2,1)S(1)}, u32[]{:S(2)}, u32[]{:S(2)}) async-start(bf16[64,16,1024]{2,1,0:T(8,128)(2,1)} %gather.1), calls=%async_computation.2 | async-start | bytes 4194304 | tf_op jit(solution)/shard_map/gather/all_to_all | solution.py:423
  112.5 0.0 collective-permute-done.15
  112.6 12.2 %solve.1 = (bf16[768,256]{1,0:T(8,128)(2,1)}, bf16[512,256]{1,0:T(8,128)(2,1)}) custom-call(f32[256,256]{1,0:T(8,128)S(1)} %pad_maximum_fusion.g_ref, bf16[512,256]{1,0:T(8,128)(2,1)} %get-tuple-element.38.s_ref), custom_call_target="tpu_custom_call" | custom-call | flops 20000000000 | bytes 1000000 | tf_op jit(solution)/shard_map/solve/pallas_call | solution.py:303
  124.8 16.4 %all-to-all-done.2 = bf16[64,16,1024]{2,1,0:T(8,128)(2,1)S(1)} async-done(((bf16[64,16,1024]{2,1,0:T(8,128)(2,1)}), bf16[64,16,1024]{2,1,0:T(8,128)(2,1)S(1)}, u32[]{:S(2)}, u32[]{:S(2)}) %all-to-all-start.2) | async-done | bytes 2097184 | tf_op jit(solution)/shard_map/gather/all_to_all | solution.py:423
  141.1 1.8 %collective-permute-start.16 = (bf16[4,16,16,1024]{3,2,1,0:T(8,128)(2,1)S(1)}, bf16[4,16,16,1024]{3,2,1,0:T(8,128)(2,1)}, u32[]{:S(2)}, u32[]{:S(2)}) collective-permute-start(bf16[4,16,16,1024]{3,2,1,0:T(8,128)(2,1)S(1)} %bitcast.10), channel_id=1, source_target_pairs={{0,16},{16,0},{1,17},{17,1},{2,18},{18,2},{3,19},{19,3},{4,20},{20... | collective-permute-start | bytes 6291464 | tf_op jit(solution)/shard_map/finish/ppermute | solution.py:379
  142.9 0.1 pad_add_fusion.1.s_ref
  143.0 0.1 pad_add_fusion.s_ref
  143.1 5.0 %finish.2 = (bf16[512,8192]{1,0:T(8,128)(2,1)}, f32[512,256]{1,0:T(8,128)}) custom-call(s32[2]{0:T(128)S(1)} %pad_add_fusion.1.s_ref, bf16[512,256]{1,0:T(8,128)(2,1)} %get-tuple-element.41.w_ref, bf16[768,256]{1,0:T(8,128)(2,1)} %get-tuple-element.42.inv_ref, bf16[4,16,16,1024]{3,2,1,0:T(8,128)(2,1)S(1)} %bitcast.11, ...), custom_call_target="tpu_custom_call" | custom-call | flops 1073741824 | bytes 10485760 | tf_op jit(solution)/shard_map/finish/pallas_call | solution.py:358
  148.1 0.0 collective-permute-done.16.t_ref
  148.1 5.3 %finish.3 = (bf16[512,8192]{1,0:T(8,128)(2,1)}, f32[512,256]{1,0:T(8,128)}) custom-call(s32[2]{0:T(128)S(1)} %pad_add_fusion.s_ref, bf16[512,256]{1,0:T(8,128)(2,1)} %get-tuple-element.41.w_ref, bf16[768,256]{1,0:T(8,128)(2,1)} %get-tuple-element.42.inv_ref, ...), custom_call_target="tpu_custom_call", output_to_operand_aliasing={{0}: (8, {}), {1}: (9, {})} | custom-call | flops 1073741824 | bytes 10485760 | tf_op jit(solution)/shard_map/finish/pallas_call | solution.py:358
  (6 shorter events, 0.2 us)
Async XLA Ops:
  0.6 1.0 copy-start
  3.2 35.5 %all-to-all-start = ((bf16[16,256,256]{2,1,0:T(8,128)(2,1)}), bf16[16,256,256]{2,1,0:T(8,128)(2,1)S(1)}, u32[]{:S(2)}, u32[]{:S(2)}) async-start(bf16[16,256,256]{2,1,0:T(8,128)(2,1)} %broadcast_in_dim.4), calls=%async_computation | async-start | bytes 4194304 | tf_op jit(solution)/shard_map/query_gather/all_to_all | solution.py:400
  20.4 3.5 %collective-permute-start = (bf16[512,1024]{1,0:T(8,128)(2,1)}, bf16[512,1024]{1,0:T(8,128)(2,1)S(1)}, u32[]{:S(2)}, u32[]{:S(2)}) collective-permute-start(bf16[512,1024]{1,0:T(8,128)(2,1)} %get-tuple-element.26.refs_0_), channel_id=1, source_target_pairs={{0,16},{16,0},{1,17},{17,1},{2,18},{18,2},{3,19},{19,3},{4,20},{20... | collective-permute-start | bytes 3145736 | tf_op jit(solution)/shard_map/adjust/ppermute | solution.py:379
  21.4 4.0 %collective-permute-start.1 = (bf16[512,1024]{1,0:T(8,128)(2,1)}, bf16[512,1024]{1,0:T(8,128)(2,1)S(1)}, u32[]{:S(2)}, u32[]{:S(2)}) collective-permute-start(bf16[512,1024]{1,0:T(8,128)(2,1)} %get-tuple-element.27.refs_1_), channel_id=1, source_target_pairs={{0,16},{16,0},{1,17},{17,1},{2,18},{18,2},{3,19},{19,3},{4,20},{20... | collective-permute-start | bytes 3145736 | tf_op jit(solution)/shard_map/adjust/ppermute | solution.py:379
  21.5 5.4 %collective-permute-start.2 = (bf16[512,1024]{1,0:T(8,128)(2,1)}, bf16[512,1024]{1,0:T(8,128)(2,1)S(1)}, u32[]{:S(2)}, u32[]{:S(2)}) collective-permute-start(bf16[512,1024]{1,0:T(8,128)(2,1)} %get-tuple-element.28.refs_2_), channel_id=1, source_target_pairs={{0,16},{16,0},{1,17},{17,1},{2,18},{18,2},{3,19},{19,3},{4,20},{20... | collective-permute-start | bytes 3145736 | tf_op jit(solution)/shard_map/adjust/ppermute | solution.py:379
  21.9 6.5 %collective-permute-start.3 = (bf16[512,1024]{1,0:T(8,128)(2,1)}, bf16[512,1024]{1,0:T(8,128)(2,1)S(1)}, u32[]{:S(2)}, u32[]{:S(2)}) collective-permute-start(bf16[512,1024]{1,0:T(8,128)(2,1)} %get-tuple-element.29.refs_3_), channel_id=1, source_target_pairs={{0,16},{16,0},{1,17},{17,1},{2,18},{18,2},{3,19},{19,3},{4,20},{20... | collective-permute-start | bytes 3145736 | tf_op jit(solution)/shard_map/adjust/ppermute | solution.py:379
  23.9 4.5 %copy-start.1 = (bf16[512,1024]{1,0:T(8,128)(2,1)}, bf16[512,1024]{1,0:T(8,128)(2,1)S(1)}, u32[]{:S(2)}) copy-start(bf16[512,1024]{1,0:T(8,128)(2,1)S(1)} %collective-permute-done.refs_0_) | copy-start | bytes 3145732
  25.4 3.0 %copy-start.2 = (bf16[512,1024]{1,0:T(8,128)(2,1)}, bf16[512,1024]{1,0:T(8,128)(2,1)S(1)}, u32[]{:S(2)}) copy-start(bf16[512,1024]{1,0:T(8,128)(2,1)S(1)} %collective-permute-done.1.refs_1_) | copy-start | bytes 3145732
  26.9 1.5 copy-start.3
  28.4 1.0 copy-start.4
  41.7 4.5 %collective-permute-start.4 = (bf16[256,256]{1,0:T(8,128)(2,1)S(1)}, bf16[256,256]{1,0:T(8,128)(2,1)S(1)}, u32[]{:S(2)}, u32[]{:S(2)}) collective-permute-start(bf16[256,256]{1,0:T(8,128)(2,1)S(1)} %get-tuple-element.31), channel_id=1, source_target_pairs={{0,16},{16,0},{1,17},{17,1},{2,18},{18,2},{3,19},{19,3},{4,20},{20... | collective-permute-start | bytes 393224 | tf_op jit(solution)/shard_map/project/ppermute | solution.py:379
  46.3 6.3 %collective-permute-start.7 = (bf16[256,256]{1,0:T(8,128)(2,1)S(1)}, bf16[256,256]{1,0:T(8,128)(2,1)S(1)}, u32[]{:S(2)}, u32[]{:S(2)}) collective-permute-start(bf16[256,256]{1,0:T(8,128)(2,1)S(1)} %add_convert_fusion.1), channel_id=1, source_target_pairs={{0,96},{32,0},{64,32},{96,64},{1,97},{33,1},{65,33},{97,65},{2,98}... | collective-permute-start | bytes 393224 | tf_op jit(solution)/shard_map/project/ppermute | solution.py:383
  50.1 8.8 %collective-permute-start.6 = (bf16[256,256]{1,0:T(8,128)(2,1)S(1)}, bf16[256,256]{1,0:T(8,128)(2,1)S(1)}, u32[]{:S(2)}, u32[]{:S(2)}) collective-permute-start(bf16[256,256]{1,0:T(8,128)(2,1)S(1)} %add_convert_fusion.1), channel_id=1, source_target_pairs={{0,32},{32,64},{64,96},{96,0},{1,33},{33,65},{65,97},{97,1},{2,34}... | collective-permute-start | bytes 393224 | tf_op jit(solution)/shard_map/project/ppermute | solution.py:383
  50.1 8.8 %collective-permute-start.5 = (bf16[256,256]{1,0:T(8,128)(2,1)S(1)}, bf16[256,256]{1,0:T(8,128)(2,1)S(1)}, u32[]{:S(2)}, u32[]{:S(2)}) collective-permute-start(bf16[256,256]{1,0:T(8,128)(2,1)S(1)} %add_convert_fusion.1), channel_id=1, source_target_pairs={{0,64},{32,96},{64,0},{96,32},{1,65},{33,97},{65,1},{97,33},{2,66}... | collective-permute-start | bytes 393224 | tf_op jit(solution)/shard_map/project/ppermute | solution.py:383
  59.0 2.2 %collective-permute-start.8 = (bf16[256,256]{1,0:T(8,128)(2,1)S(1)}, bf16[256,256]{1,0:T(8,128)(2,1)S(1)}, u32[]{:S(2)}, u32[]{:S(2)}) collective-permute-start(bf16[256,256]{1,0:T(8,128)(2,1)S(1)} %add_convert_fusion.mine_ref), channel_id=1, source_target_pairs={{0,16},{16,0},{1,17},{17,1},{2,18},{18,2},{3,19},{19,3},{4,20},{20... | collective-permute-start | bytes 393224 | tf_op jit(solution)/shard_map/gram/ppermute | solution.py:379
  62.0 6.1 %collective-permute-start.11 = (bf16[128,256]{1,0:T(8,128)(2,1)S(1)}, bf16[128,256]{1,0:T(8,128)(2,1)S(1)}, u32[]{:S(2)}, u32[]{:S(2)}) collective-permute-start(bf16[128,256]{1,0:T(8,128)(2,1)S(1)} %get-tuple-element.33), channel_id=1, source_target_pairs={{0,12},{4,0},{8,4},{12,8},{1,13},{5,1},{9,5},{13,9},{2,14},{6,2},{... | collective-permute-start | bytes 196616 | tf_op jit(solution)/shard_map/gram/ppermute | solution.py:383
  62.2 5.9 %collective-permute-start.10 = (bf16[128,256]{1,0:T(8,128)(2,1)S(1)}, bf16[128,256]{1,0:T(8,128)(2,1)S(1)}, u32[]{:S(2)}, u32[]{:S(2)}) collective-permute-start(bf16[128,256]{1,0:T(8,128)(2,1)S(1)} %get-tuple-element.33), channel_id=1, source_target_pairs={{0,4},{4,8},{8,12},{12,0},{1,5},{5,9},{9,13},{13,1},{2,6},{6,10},{... | collective-permute-start | bytes 196616 | tf_op jit(solution)/shard_map/gram/ppermute | solution.py:383
  63.5 4.7 %collective-permute-start.9 = (bf16[128,256]{1,0:T(8,128)(2,1)S(1)}, bf16[128,256]{1,0:T(8,128)(2,1)S(1)}, u32[]{:S(2)}, u32[]{:S(2)}) collective-permute-start(bf16[128,256]{1,0:T(8,128)(2,1)S(1)} %get-tuple-element.33), channel_id=1, source_target_pairs={{0,8},{4,12},{8,0},{12,4},{1,9},{5,13},{9,1},{13,5},{2,10},{6,14},... | collective-permute-start | bytes 196616 | tf_op jit(solution)/shard_map/gram/ppermute | solution.py:383
  68.2 32.0 %all-to-all-start.1 = ((bf16[64,16,1024]{2,1,0:T(8,128)(2,1)}), bf16[64,16,1024]{2,1,0:T(8,128)(2,1)S(1)}, u32[]{:S(2)}, u32[]{:S(2)}) async-start(bf16[64,16,1024]{2,1,0:T(8,128)(2,1)} %bitcast.15), calls=%async_computation.1 | async-start | bytes 4194304 | tf_op jit(solution)/shard_map/term/all_to_all | solution.py:418
  73.0 15.6 %collective-permute-start.13 = (bf16[128,256]{1,0:T(8,128)(2,1)S(1)}, bf16[128,256]{1,0:T(8,128)(2,1)S(1)}, u32[]{:S(2)}, u32[]{:S(2)}) collective-permute-start(bf16[128,256]{1,0:T(8,128)(2,1)S(1)} %add_add_fusion.1), channel_id=1, source_target_pairs={{0,1},{1,2},{2,3},{3,0},{4,5},{5,6},{6,7},{7,4},{8,9},{9,10},{10,1... | collective-permute-start | bytes 196616 | tf_op jit(solution)/shard_map/gather/ppermute | solution.py:383
  73.9 22.6 %collective-permute-start.12 = (bf16[128,256]{1,0:T(8,128)(2,1)S(1)}, bf16[128,256]{1,0:T(8,128)(2,1)S(1)}, u32[]{:S(2)}, u32[]{:S(2)}) collective-permute-start(bf16[128,256]{1,0:T(8,128)(2,1)S(1)} %add_add_fusion.1), channel_id=1, source_target_pairs={{0,2},{1,3},{2,0},{3,1},{4,6},{5,7},{6,4},{7,5},{8,10},{9,11},{10,... | collective-permute-start | bytes 196616 | tf_op jit(solution)/shard_map/gather/ppermute | solution.py:383
  76.3 20.2 %collective-permute-start.14 = (bf16[128,256]{1,0:T(8,128)(2,1)S(1)}, bf16[128,256]{1,0:T(8,128)(2,1)S(1)}, u32[]{:S(2)}, u32[]{:S(2)}) collective-permute-start(bf16[128,256]{1,0:T(8,128)(2,1)S(1)} %add_add_fusion.1), channel_id=1, source_target_pairs={{0,3},{1,0},{2,1},{3,2},{4,7},{5,4},{6,5},{7,6},{8,11},{9,8},{10,9... | collective-permute-start | bytes 196616 | tf_op jit(solution)/shard_map/gather/ppermute | solution.py:383
  101.9 10.6 %collective-permute-start.15 = (f32[128,256]{1,0:T(8,128)S(1)}, f32[128,256]{1,0:T(8,128)S(1)}, u32[]{:S(2)}, u32[]{:S(2)}) collective-permute-start(f32[128,256]{1,0:T(8,128)S(1)} %add_add_fusion), channel_id=1, source_target_pairs={{0,16},{16,0},{1,17},{17,1},{2,18},{18,2},{3,19},{19,3},{4,20},{20... | collective-permute-start | bytes 393224 | tf_op jit(solution)/shard_map/solve/ppermute | solution.py:379
  105.4 35.7 %all-to-all-start.2 = ((bf16[64,16,1024]{2,1,0:T(8,128)(2,1)}), bf16[64,16,1024]{2,1,0:T(8,128)(2,1)S(1)}, u32[]{:S(2)}, u32[]{:S(2)}) async-start(bf16[64,16,1024]{2,1,0:T(8,128)(2,1)} %gather.1), calls=%async_computation.2 | async-start | bytes 4194304 | tf_op jit(solution)/shard_map/gather/all_to_all | solution.py:423
  141.1 7.0 %collective-permute-start.16 = (bf16[4,16,16,1024]{3,2,1,0:T(8,128)(2,1)S(1)}, bf16[4,16,16,1024]{3,2,1,0:T(8,128)(2,1)}, u32[]{:S(2)}, u32[]{:S(2)}) collective-permute-start(bf16[4,16,16,1024]{3,2,1,0:T(8,128)(2,1)S(1)} %bitcast.10), channel_id=1, source_target_pairs={{0,16},{16,0},{1,17},{17,1},{2,18},{18,2},{3,19},{19,3},{4,20},{20... | collective-permute-start | bytes 6291464 | tf_op jit(solution)/shard_map/finish/ppermute | solution.py:379
